TPU v7x, 512 devices: a whole 4x8x8 slice. The times are simulated.
512 devices in a mesh: seq: 64 (over x, z, core), head: 8 (over y).
Axes of the slice: x: 4, y: 8, z: 8, core: 2. Of those that a mesh axis runs over, the one named last changes fastest.
Arguments:
- queries: bfloat16 [49152, 1024], P('seq', 'head'), may hold values from -5 to 5
- key_rows: bfloat16 [49152, 1024], P('seq', 'head'), may hold values from -5 to 5
- values: bfloat16 [49152, 1024], P('seq', 'head'), may hold values from -6 to 6
- offsets: int32 [4, 8], replicated, may hold values from 0 to 7, as said below
Outputs:
- attended: bfloat16 [49152, 1024], P(('seq', 'head'))
Inputs may be any that keep to these rules, and one draw needn't show every extreme that they name: offsets[b, h] lies in 0 to 2**b - 1, and in every branch b some head has offset 2**b - 1.
All inputs are finite; a program needn't handle non-finite values.
Results may differ from a plain program's by a relative error of at most 0.0045.
Values may be sent and summed in bfloat16 or wider, within the bound.
No kernel may reach another device: no remote copies, remote signals or barrier semaphores. Data moves between devices by JAX's collectives and lax.ppermute only.
A program may use at most 128 MiB of HBM per device.

v0:
```python
import math

import jax
import jax.numpy as jnp
from jax import lax
from jax.sharding import PartitionSpec as P


def from_behind(value, axis, steps):
    count = lax.axis_size(axis)
    first, last = (max(0, -steps), min(count, count - steps))
    return lax.ppermute(value, axis, [(source, source + steps) for source in range(first, last)])


def select_rows(source, onehot, dilation):
    row_count, feature_width = source.shape
    head_count = onehot.shape[1]
    if dilation == 1:
        return source
    grouped = source.reshape(
        row_count // dilation, dilation, head_count, feature_width // head_count
    )
    chosen = jnp.einsum(
        "qrhd,rh->qhd", grouped, onehot.astype(jnp.bfloat16), preferred_element_type=jnp.float32
    )
    return chosen.astype(jnp.bfloat16).reshape(row_count // dilation, feature_width)


def attend_piece(state_now, key_piece, first_row, query_block, query_index, segment_low):
    head_count = query_block.shape[1]
    head_size = query_block.shape[2]
    piece_rows = key_piece.shape[1]
    block_rows = 512 if piece_rows % 512 == 0 else piece_rows
    block_count = piece_rows // block_rows
    blocked = key_piece.reshape(2, block_count, block_rows, head_count, head_size)
    score_scale = 1.0 / math.sqrt(head_size)

    def advance(state, block_item):
        key_block, value_block, block_index = block_item
        key_index = first_row + block_index * block_rows + jnp.arange(block_rows, dtype=jnp.int32)
        allowed = (key_index[None, :] >= segment_low) & (key_index[None, :] <= query_index[:, None])

        def update(inner):
            running_max, running_sum, accumulated = inner
            scores = (
                jnp.einsum(
                    "qhd,khd->hqk", query_block, key_block, preferred_element_type=jnp.float32
                )
                * score_scale
            )
            scores = jnp.where(allowed[None], scores, -jnp.inf)
            new_max = jnp.maximum(running_max, jnp.max(scores, axis=2))
            factor = jnp.exp(running_max - new_max)
            weights = jnp.exp(scores - new_max[:, :, None])
            new_sum = running_sum * factor + jnp.sum(weights, axis=2)
            product = jnp.einsum(
                "hqk,khd->hqd",
                weights.astype(jnp.bfloat16),
                value_block,
                preferred_element_type=jnp.float32,
            )
            return (new_max, new_sum, accumulated * factor[:, :, None] + product)

        def unchanged(inner):
            return inner

        return (lax.cond(jnp.any(allowed), update, unchanged, state), None)

    block_items = (blocked[0], blocked[1], jnp.arange(block_count, dtype=jnp.int32))
    state_now, _ = lax.scan(advance, state_now, block_items)
    return state_now


def make_folder(query_block, query_index, segment_low):

    def folder(state_now, key_piece, first_row):
        return attend_piece(state_now, key_piece, first_row, query_block, query_index, segment_low)

    return folder


def segment_attend(stacked, state_now, folder, group_size, own_first):
    state_now = folder(state_now, stacked, own_first)
    buffer = stacked
    first_row = own_first
    for bit_index in range(group_size.bit_length() - 1):
        distance = 1 << bit_index
        arrived = from_behind(buffer, "seq", distance)
        first_row = first_row - distance * stacked.shape[1]
        state_now = folder(state_now, arrived, first_row)
        if distance * 2 < group_size:
            buffer = jnp.concatenate([arrived, buffer], axis=1)
    return state_now


def on_device(queries, key_rows, values, offsets):
    seq_count = lax.axis_size("seq")
    seq_place = lax.axis_index("seq")
    row_count, feature_width = queries.shape
    branches = offsets.shape[0]
    head_count = offsets.shape[1] // lax.axis_size("head")
    head_size = feature_width // head_count
    head_first = lax.axis_index("head") * head_count
    contexts = []
    for branch in range(branches):
        dilation = 2**branch
        group_size = seq_count // 2 ** (branches - 1 - branch)
        chosen_rows = row_count // dilation
        head_offset = lax.dynamic_slice_in_dim(offsets[branch], head_first, head_count)
        onehot = jnp.arange(dilation, dtype=jnp.int32)[:, None] == head_offset[None, :]
        query_block = select_rows(queries, onehot, dilation).reshape(
            chosen_rows, head_count, head_size
        )
        stacked = jnp.stack(
            [select_rows(key_rows, onehot, dilation), select_rows(values, onehot, dilation)]
        )
        own_first = seq_place * chosen_rows
        query_index = own_first + jnp.arange(chosen_rows, dtype=jnp.int32)
        segment_low = seq_place // group_size * group_size * chosen_rows
        initial = (
            jnp.full((head_count, chosen_rows), -1e30, jnp.float32),
            jnp.zeros((head_count, chosen_rows), jnp.float32),
            jnp.zeros((head_count, chosen_rows, head_size), jnp.float32),
        )
        folder = make_folder(query_block, query_index, segment_low)
        contexts.append(
            (branch, stacked, initial, folder, group_size, own_first, onehot, chosen_rows, dilation)
        )
    results = {}
    members = [item[:6] for item in contexts]
    for branch, stacked, initial, folder, group_size, own_first in members:
        results[branch] = segment_attend(stacked, initial, folder, group_size, own_first)
    outs_list, logs_list, picks_list = ([], [], [])
    for item in contexts:
        branch, onehot, chosen_rows, dilation = (item[0], item[6], item[7], item[8])
        running_max, running_sum, accumulated = results[branch]
        branch_out = jnp.transpose(accumulated / running_sum[:, :, None], (1, 0, 2))
        log_total = jnp.transpose(running_max + jnp.log(running_sum), (1, 0))
        placed = branch_out[:, None, :, :] * onehot[None, :, :, None].astype(jnp.float32)
        outs_list.append(placed.reshape(row_count, head_count, head_size))
        logs_list.append(
            jnp.broadcast_to(log_total[:, None, :], (chosen_rows, dilation, head_count)).reshape(
                row_count, head_count
            )
        )
        picks_list.append(
            jnp.broadcast_to(onehot[None, :, :], (chosen_rows, dilation, head_count)).reshape(
                row_count, head_count
            )
        )
    branch_outs = jnp.stack(outs_list)
    branch_logs = jnp.stack(logs_list)
    branch_picks = jnp.stack(picks_list)
    best_log = jnp.max(jnp.where(branch_picks, branch_logs, -jnp.inf), axis=0)
    merge_weight = jnp.where(branch_picks, jnp.exp(branch_logs - best_log[None]), 0.0)
    merged = (
        jnp.sum(merge_weight[:, :, :, None] * branch_outs, axis=0)
        / jnp.sum(merge_weight, axis=0)[:, :, None]
    )
    merged = merged.astype(jnp.bfloat16).reshape(row_count, feature_width)
    return lax.all_to_all(merged, "head", split_axis=0, concat_axis=1, tiled=True)


def solution(mesh):
    placed = (P("seq", "head"), P("seq", "head"), P("seq", "head"), P())
    return jax.shard_map(
        on_device, mesh=mesh, in_specs=placed, out_specs=P(("seq", "head"), None), check_vma=False
    )
```

profile of v0, /device:TPU:450, one launch (start us, length us, event | category | flops | bytes accessed | tf_op | source)
XLA Modules:
  0.0 475.9 jit_solution(9732312305740462293)
XLA Ops:
  42.1 2.8 fusion.321
  69.3 2.1 collective-permute-start.13
  72.6 4.3 collective-permute-start.8
  79.5 6.4 %collective-permute-start.14 = (bf16[2,384,128]{2,1,0:T(8,128)(2,1)}, bf16[2,384,128]{2,1,0:T(8,128)(2,1)}, u32[]{:S(2)}, u32[]{:S(2)}) collective-permute-start(bf16[2,384,128]{2,1,0:T(8,128)(2,1)} %maximum_maximum_fusion.9), channel_id=1, source_target_pairs={{0,32},{8,40},{16,48},{24,56},{32,64},{40,72},{48,80},{56,88},{64,... | collective-permute-start | bytes 589832 | tf_op jit(solution)/shard_map/ppermute | solution.py:12
  88.1 3.4 collective-permute-start.4
  94.6 2.8 collective-permute-start.9
  98.2 3.9 conditional.29
  103.9 5.7 %collective-permute-start.15 = (bf16[2,768,128]{2,1,0:T(8,128)(2,1)}, bf16[2,768,128]{2,1,0:T(8,128)(2,1)S(1)}, u32[]{:S(2)}, u32[]{:S(2)}) collective-permute-start(bf16[2,768,128]{2,1,0:T(8,128)(2,1)} %maximum_maximum_fusion.7), channel_id=1, source_target_pairs={{0,64},{8,72},{16,80},{24,88},{32,96},{40,104},{48,112},{56,120},{... | collective-permute-start | bytes 1179656 | tf_op jit(solution)/shard_map/ppermute | solution.py:12
  111.2 4.9 %conditional.34 = ((f32[1,96]{1,0:T(1,128)}, f32[1,96]{1,0:T(1,128)}, f32[1,96,128]{2,1,0:T(8,128)S(1)})) conditional(s32[]{:T(128)} %convert_element_type.286, (f32[1,96]{1,0:T(1,128)}, f32[1,96]{1,0:T(1,128)}, f32[1,96,128]{2,1,0:T(8,128)S(1)}) %tuple.731, (bf16[96,1,128]{2,0,1:T(8,128)(2,1)S(1)}, bf16[384,1,128]{2,0,1:T(8,128)(2,1)}, ...), branch_computations={%region_104.105_spmd, %region_105.108_spmd} | conditional | flops 19157280 | bytes 804896 | solution.py:67
  117.0 3.6 collective-permute-start.1
  120.6 2.7 conditional.23
  125.2 2.8 collective-permute-start.5
  128.1 2.4 conditional.26
  130.5 6.0 %collective-permute-done.9 = bf16[2,768,128]{2,1,0:T(8,128)(2,1)S(1)} collective-permute-done((bf16[2,768,128]{2,1,0:T(8,128)(2,1)}, bf16[2,768,128]{2,1,0:T(8,128)(2,1)S(1)}, u32[]{:S(2)}, u32[]{:S(2)}) %collective-permute-start.9) | collective-permute-done | bytes 393248 | tf_op jit(solution)/shard_map/ppermute | solution.py:12
  139.5 3.2 conditional.30
  147.1 3.2 collective-permute-start.16
  151.2 2.6 collective-permute-done.1
  153.8 2.0 fusion.350
  156.4 20.5 %while.24 = (s32[]{:T(128)}, f32[1,768]{1,0:T(1,128)S(1)}, f32[1,768]{1,0:T(1,128)S(1)}, f32[1,768,128]{2,1,0:T(8,128)S(1)}, s32[3]{0:T(128)}, /*index=5*/s32[]{...) while((s32[]{:T(128)}, f32[1,768]{1,0:T(1,128)S(1)}, ...), condition=%wide.region_16.17_spmd.clone, body=%wide.region_10.16_spmd.clone.sunk | while | flops 205459968 | bytes 6815023 | solution.py:70
  160.1 3.1 conditional.52
  167.0 3.1 conditional.52
  173.8 3.1 conditional.52
  176.9 2.4 maximum_maximum_fusion
  179.3 2.2 collective-permute-start.2
  181.5 55.6 %collective-permute-done.5 = bf16[2,1536,128]{2,1,0:T(8,128)(2,1)} collective-permute-done((bf16[2,1536,128]{2,1,0:T(8,128)(2,1)}, bf16[2,1536,128]{2,1,0:T(8,128)(2,1)}, u32[]{:S(2)}, u32[]{:S(2)}) %collective-permute-start.5) | collective-permute-done | bytes 786464 | tf_op jit(solution)/shard_map/ppermute | solution.py:12
  238.9 14.2 %while.26 = (s32[]{:T(128)}, f32[1,384]{1,0:T(1,128)S(1)}, f32[1,384]{1,0:T(1,128)}, f32[1,384,128]{2,1,0:T(8,128)S(1)}, s32[3]{0:T(128)}, /*index=5*/s32[]{:T(1...) while((s32[]{:T(128)}, f32[1,384]{1,0:T(1,128)S(1)}, ...), condition=%wide.region_45.46_spmd.clone, body=%wide.region_39.45_spmd.clone.sunk | while | flops 102730752 | bytes 3554159 | solution.py:70
  253.1 2.5 maximum_maximum_fusion.1
  255.6 4.6 collective-permute-start.6
  261.4 15.1 %while.28 = (s32[]{:T(128)}, f32[1,192]{1,0:T(1,128)S(1)}, f32[1,192]{1,0:T(1,128)}, f32[1,192,128]{2,1,0:T(8,128)S(1)}, s32[3]{0:T(128)S(1)}, /*index=5*/s32[]{...) while((s32[]{:T(128)}, f32[1,192]{1,0:T(1,128)S(1)}, ...), condition=%wide.region_79.80_spmd.clone, body=%wide.region_73.79_spmd.clone.sunk | while | flops 51365956 | bytes 1903927 | solution.py:70
  264.2 2.2 conditional.56
  269.3 2.2 conditional.56
  274.3 2.2 conditional.56
  276.5 2.2 constant_dynamic-update-slice_fusion.4
  283.5 2.2 constant_dynamic-update-slice_fusion.15
  290.0 2.4 collective-permute-start.17
  293.6 10.5 %while.30 = (s32[]{:T(128)}, f32[1,96]{1,0:T(1,128)S(1)}, f32[1,96]{1,0:T(1,128)S(1)}, f32[1,96,128]{2,1,0:T(8,128)S(1)}, s32[3]{0:T(128)S(1)}, /*index=5*/s32[]...) while((s32[]{:T(128)}, f32[1,96]{1,0:T(1,128)S(1)}, ...), condition=%wide.region_118.119_spmd.clone, body=%wide.region_112.118_spmd.clone.sunk | while | flops 25683844 | bytes 1085751 | solution.py:70
  304.1 51.0 %collective-permute-done.2 = bf16[2,3072,128]{2,1,0:T(8,128)(2,1)} collective-permute-done((bf16[2,3072,128]{2,1,0:T(8,128)(2,1)}, bf16[2,3072,128]{2,1,0:T(8,128)(2,1)}, u32[]{:S(2)}, u32[]{:S(2)}) %collective-permute-start.2) | collective-permute-done | bytes 1572896 | tf_op jit(solution)/shard_map/ppermute | solution.py:12
  356.6 24.6 %while.25 = (s32[]{:T(128)}, f32[1,768]{1,0:T(1,128)S(1)}, f32[1,768]{1,0:T(1,128)S(1)}, f32[1,768,128]{2,1,0:T(8,128)S(1)}, s32[6]{0:T(128)S(1)}, /*index=5*/s3...) while((s32[]{:T(128)}, f32[1,768]{1,0:T(1,128)S(1)}, ...), condition=%wide.region_23.24_spmd.clone, body=%wide.region_17.23_spmd.clone.sunk | while | flops 205459968 | bytes 6816055 | solution.py:70
  383.0 22.2 %while.27 = (s32[]{:T(128)}, f32[1,384]{1,0:T(1,128)S(1)}, f32[1,384]{1,0:T(1,128)S(1)}, f32[1,384,128]{2,1,0:T(8,128)S(1)}, s32[6]{0:T(128)S(1)}, /*index=5*/s3...) while((s32[]{:T(128)}, f32[1,384]{1,0:T(1,128)S(1)}, ...), condition=%wide.region_52.53_spmd.clone, body=%wide.region_46.52_spmd.clone.sunk | while | flops 102730752 | bytes 3541815 | solution.py:70
  407.6 29.4 %while.29 = (s32[]{:T(128)}, f32[1,192]{1,0:T(1,128)S(1)}, f32[1,192]{1,0:T(1,128)}, f32[1,192,128]{2,1,0:T(8,128)S(1)}, s32[6]{0:T(128)S(1)}, /*index=5*/s32[]{...) while((s32[]{:T(128)}, f32[1,192]{1,0:T(1,128)S(1)}, ...), condition=%wide.region_86.87_spmd.clone, body=%wide.region_80.86_spmd.clone.sunk | while | flops 51365956 | bytes 1903927 | solution.py:70
  410.4 2.2 conditional.57
  415.3 2.2 conditional.57
  420.2 2.2 conditional.57
  425.0 2.2 conditional.57
  429.9 2.2 conditional.57
  434.8 2.2 conditional.57
  440.7 16.3 %while.31 = (s32[]{:T(128)}, f32[1,96]{1,0:T(1,128)S(1)}, f32[1,96]{1,0:T(1,128)S(1)}, f32[1,96,128]{2,1,0:T(8,128)S(1)}, s32[6]{0:T(128)S(1)}, /*index=5*/s32[]...) while((s32[]{:T(128)}, f32[1,96]{1,0:T(1,128)S(1)}, ...), condition=%wide.region_125.126_spmd.clone, body=%wide.region_119.125_spmd.clone.sunk | while | flops 25683844 | bytes 1085751 | solution.py:70
  458.5 16.7 %all_to_all.16 = bf16[8,96,128]{2,1,0:T(8,128)(2,1)S(1)} all-to-all(bf16[8,96,128]{2,1,0:T(8,128)(2,1)S(1)} %divide_convert_fusion), channel_id=1, replica_groups=mesh['seq'=64,'head'=8] {'head'}, dimensions={0} | all-to-all | bytes 393216 | tf_op jit(solution)/shard_map/all_to_all | solution.py:161
  (779 shorter events, 253.6 us)
Async XLA Ops:
  0.0 12.1 %copy-start.1 = (bf16[768,128]{1,0:T(8,128)(2,1)S(1)}, bf16[768,128]{1,0:T(8,128)(2,1)}, u32[]{:S(2)}) copy-start(bf16[768,128]{1,0:T(8,128)(2,1)} %param.65) | copy-start | bytes 589828
  0.0 13.1 %copy-start.2 = (bf16[768,128]{1,0:T(8,128)(2,1)S(1)}, bf16[768,128]{1,0:T(8,128)(2,1)}, u32[]{:S(2)}) copy-start(bf16[768,128]{1,0:T(8,128)(2,1)} %param.66) | copy-start | bytes 589828
  5.1 88.2 %copy-start.15 = (bf16[1,192,128]{2,1,0:T(8,128)(2,1)}, bf16[1,192,128]{2,1,0:T(8,128)(2,1)S(1)}, u32[]{:S(2)}) copy-start(bf16[1,192,128]{2,1,0:T(8,128)(2,1)S(1)} %get-tuple-element.2970) | copy-start | bytes 147460
  5.8 66.1 %collective-permute-start.7 = (bf16[2,192,128]{2,1,0:T(8,128)(2,1)}, bf16[2,192,128]{2,1,0:T(8,128)(2,1)S(1)}, u32[]{:S(2)}, u32[]{:S(2)}) collective-permute-start(bf16[2,192,128]{2,1,0:T(8,128)(2,1)} %pad_maximum_fusion.2), channel_id=1, source_target_pairs={{0,8},{8,16},{16,24},{24,32},{32,40},{40,48},{48,56},{56,64},{64,7... | collective-permute-start | bytes 294920 | tf_op jit(solution)/shard_map/ppermute | solution.py:12
  9.5 106.6 %collective-permute-start = (bf16[2,768,128]{2,1,0:T(8,128)(2,1)}, bf16[2,768,128]{2,1,0:T(8,128)(2,1)S(1)}, u32[]{:S(2)}, u32[]{:S(2)}) collective-permute-start(bf16[2,768,128]{2,1,0:T(8,128)(2,1)} %pad_maximum_fusion), channel_id=1, source_target_pairs={{0,8},{8,16},{16,24},{24,32},{32,40},{40,48},{48,56},{56,64},{64,7... | collective-permute-start | bytes 1179656 | tf_op jit(solution)/shard_map/ppermute | solution.py:12
  13.1 12.7 %copy-start = (bf16[768,128]{1,0:T(8,128)(2,1)S(1)}, bf16[768,128]{1,0:T(8,128)(2,1)}, u32[]{:S(2)}) copy-start(bf16[768,128]{1,0:T(8,128)(2,1)} %param.64) | copy-start | bytes 589828
  14.9 71.8 %copy-start.7 = (bf16[1,384,128]{2,1,0:T(8,128)(2,1)}, bf16[1,384,128]{2,1,0:T(8,128)(2,1)S(1)}, u32[]{:S(2)}) copy-start(bf16[1,384,128]{2,1,0:T(8,128)(2,1)S(1)} %get-tuple-element.2960) | copy-start | bytes 294916
  14.9 71.8 %copy-start.8 = (bf16[1,384,128]{2,1,0:T(8,128)(2,1)}, bf16[1,384,128]{2,1,0:T(8,128)(2,1)S(1)}, u32[]{:S(2)}) copy-start(bf16[1,384,128]{2,1,0:T(8,128)(2,1)S(1)} %get-tuple-element.3015) | copy-start | bytes 294916
  15.7 71.0 %collective-permute-start.3 = (bf16[2,384,128]{2,1,0:T(8,128)(2,1)}, bf16[2,384,128]{2,1,0:T(8,128)(2,1)S(1)}, u32[]{:S(2)}, u32[]{:S(2)}) collective-permute-start(bf16[2,384,128]{2,1,0:T(8,128)(2,1)} %pad_maximum_fusion.1), channel_id=1, source_target_pairs={{0,8},{8,16},{16,24},{24,32},{32,40},{40,48},{48,56},{56,64},{64,7... | collective-permute-start | bytes 589832 | tf_op jit(solution)/shard_map/ppermute | solution.py:12
  20.4 48.8 %copy-start.21 = (bf16[1,96,128]{2,1,0:T(8,128)(2,1)}, bf16[1,96,128]{2,1,0:T(8,128)(2,1)S(1)}, u32[]{:S(2)}) copy-start(bf16[1,96,128]{2,1,0:T(8,128)(2,1)S(1)} %get-tuple-element.2978) | copy-start | bytes 73732
  21.0 48.2 %collective-permute-start.12 = (bf16[2,96,128]{2,1,0:T(8,128)(2,1)}, bf16[2,96,128]{2,1,0:T(8,128)(2,1)S(1)}, u32[]{:S(2)}, u32[]{:S(2)}) collective-permute-start(bf16[2,96,128]{2,1,0:T(8,128)(2,1)} %pad_maximum_fusion.3), channel_id=1, source_target_pairs={{0,8},{8,16},{16,24},{24,32},{32,40},{40,48},{48,56},{56,64},{64,7... | collective-permute-start | bytes 147464 | tf_op jit(solution)/shard_map/ppermute | solution.py:12
  67.8 9.1 %copy-start.40 = (pred[192,192]{0,1:T(32,128)(4,1)S(1)}, pred[192,192]{0,1:T(32,128)(4,1)}, u32[]{:S(2)}) copy-start(pred[192,192]{0,1:T(32,128)(4,1)} %get-tuple-element.2996) | copy-start | bytes 110596
  68.7 17.2 %copy-start.46 = (pred[96,192]{1,0:T(32,128)(4,1)S(1)}, pred[96,192]{1,0:T(32,128)(4,1)}, u32[]{:S(2)}) copy-start(pred[96,192]{1,0:T(32,128)(4,1)} %get-tuple-element.3001) | copy-start | bytes 55300
  69.2 16.7 %copy-start.18 = (bf16[2,96,128]{2,1,0:T(8,128)(2,1)}, bf16[2,96,128]{2,1,0:T(8,128)(2,1)S(1)}, u32[]{:S(2)}) copy-start(bf16[2,96,128]{2,1,0:T(8,128)(2,1)S(1)} %collective-permute-done.12) | copy-start | bytes 147460
  69.3 9.5 %copy-start.22 = (bf16[1,96,128]{2,1,0:T(8,128)(2,1)S(1)}, bf16[1,96,128]{2,1,0:T(8,128)(2,1)}, u32[]{:S(2)}) copy-start(bf16[1,96,128]{2,1,0:T(8,128)(2,1)} %copy-done.21) | copy-start | bytes 73732
  69.3 9.5 %collective-permute-start.13 = (bf16[2,192,128]{2,1,0:T(8,128)(2,1)S(1)}, bf16[2,192,128]{2,1,0:T(8,128)(2,1)S(1)}, u32[]{:S(2)}, u32[]{:S(2)}) collective-permute-start(bf16[2,192,128]{2,1,0:T(8,128)(2,1)S(1)} %maximum_maximum_fusion.10), channel_id=1, source_target_pairs={{0,16},{8,24},{16,32},{24,40},{32,48},{40,56},{48,64},{56,72},{64,... | collective-permute-start | bytes 294920 | tf_op jit(solution)/shard_map/ppermute | solution.py:12
  71.9 21.4 %copy-start.9 = (bf16[2,192,128]{2,1,0:T(8,128)(2,1)}, bf16[2,192,128]{2,1,0:T(8,128)(2,1)S(1)}, u32[]{:S(2)}) copy-start(bf16[2,192,128]{2,1,0:T(8,128)(2,1)S(1)} %collective-permute-done.7) | copy-start | bytes 294916
  72.6 20.7 %collective-permute-start.8 = (bf16[2,384,128]{2,1,0:T(8,128)(2,1)}, bf16[2,384,128]{2,1,0:T(8,128)(2,1)S(1)}, u32[]{:S(2)}, u32[]{:S(2)}) collective-permute-start(bf16[2,384,128]{2,1,0:T(8,128)(2,1)} %maximum_maximum_fusion.8), channel_id=1, source_target_pairs={{0,16},{8,24},{16,32},{24,40},{32,48},{40,56},{48,64},{56,72},{64,... | collective-permute-start | bytes 589832 | tf_op jit(solution)/shard_map/ppermute | solution.py:12
  78.8 12.7 %copy-start.32 = (f32[1,384]{1,0:T(1,128)S(1)}, f32[1,384]{1,0:T(1,128)}, u32[]{:S(2)}) copy-start(f32[1,384]{1,0:T(1,128)} %copy-done.31) | copy-start | bytes 4612
  78.8 23.3 %copy-start.12 = (bf16[2,192,128]{2,1,0:T(8,128)(2,1)}, bf16[2,192,128]{2,1,0:T(8,128)(2,1)S(1)}, u32[]{:S(2)}) copy-start(bf16[2,192,128]{2,1,0:T(8,128)(2,1)S(1)} %collective-permute-done.13) | copy-start | bytes 294916
  79.5 22.6 %collective-permute-start.14 = (bf16[2,384,128]{2,1,0:T(8,128)(2,1)}, bf16[2,384,128]{2,1,0:T(8,128)(2,1)}, u32[]{:S(2)}, u32[]{:S(2)}) collective-permute-start(bf16[2,384,128]{2,1,0:T(8,128)(2,1)} %maximum_maximum_fusion.9), channel_id=1, source_target_pairs={{0,32},{8,40},{16,48},{24,56},{32,64},{40,72},{48,80},{56,88},{64,... | collective-permute-start | bytes 589832 | tf_op jit(solution)/shard_map/ppermute | solution.py:12
  87.3 36.0 %copy-start.3 = (bf16[2,384,128]{2,1,0:T(8,128)(2,1)}, bf16[2,384,128]{2,1,0:T(8,128)(2,1)S(1)}, u32[]{:S(2)}) copy-start(bf16[2,384,128]{2,1,0:T(8,128)(2,1)S(1)} %collective-permute-done.3) | copy-start | bytes 589828
  88.1 35.2 %collective-permute-start.4 = (bf16[2,768,128]{2,1,0:T(8,128)(2,1)}, bf16[2,768,128]{2,1,0:T(8,128)(2,1)S(1)}, u32[]{:S(2)}, u32[]{:S(2)}) collective-permute-start(bf16[2,768,128]{2,1,0:T(8,128)(2,1)} %maximum_maximum_fusion.5), channel_id=1, source_target_pairs={{0,16},{8,24},{16,32},{24,40},{32,48},{40,56},{48,64},{56,72},{64,... | collective-permute-start | bytes 1179656 | tf_op jit(solution)/shard_map/ppermute | solution.py:12
  93.8 42.7 %copy-start.5 = (bf16[2,384,128]{2,1,0:T(8,128)(2,1)}, bf16[2,384,128]{2,1,0:T(8,128)(2,1)S(1)}, u32[]{:S(2)}) copy-start(bf16[2,384,128]{2,1,0:T(8,128)(2,1)S(1)} %collective-permute-done.8) | copy-start | bytes 589828
  94.6 41.9 %collective-permute-start.9 = (bf16[2,768,128]{2,1,0:T(8,128)(2,1)}, bf16[2,768,128]{2,1,0:T(8,128)(2,1)S(1)}, u32[]{:S(2)}, u32[]{:S(2)}) collective-permute-start(bf16[2,768,128]{2,1,0:T(8,128)(2,1)} %maximum_maximum_fusion.6), channel_id=1, source_target_pairs={{0,32},{8,40},{16,48},{24,56},{32,64},{40,72},{48,80},{56,88},{64,... | collective-permute-start | bytes 1179656 | tf_op jit(solution)/shard_map/ppermute | solution.py:12
  103.9 38.9 %collective-permute-start.15 = (bf16[2,768,128]{2,1,0:T(8,128)(2,1)}, bf16[2,768,128]{2,1,0:T(8,128)(2,1)S(1)}, u32[]{:S(2)}, u32[]{:S(2)}) collective-permute-start(bf16[2,768,128]{2,1,0:T(8,128)(2,1)} %maximum_maximum_fusion.7), channel_id=1, source_target_pairs={{0,64},{8,72},{16,80},{24,88},{32,96},{40,104},{48,112},{56,120},{... | collective-permute-start | bytes 1179656 | tf_op jit(solution)/shard_map/ppermute | solution.py:12
  117.0 36.8 %collective-permute-start.1 = (bf16[2,1536,128]{2,1,0:T(8,128)(2,1)}, bf16[2,1536,128]{2,1,0:T(8,128)(2,1)}, u32[]{:S(2)}, u32[]{:S(2)}) collective-permute-start(bf16[2,1536,128]{2,1,0:T(8,128)(2,1)} %maximum_maximum_fusion.2), channel_id=1, source_target_pairs={{0,16},{8,24},{16,32},{24,40},{32,48},{40,56},{48,64},{56,72},{64,... | collective-permute-start | bytes 2359304 | tf_op jit(solution)/shard_map/ppermute | solution.py:12
  125.2 112.0 %collective-permute-start.5 = (bf16[2,1536,128]{2,1,0:T(8,128)(2,1)}, bf16[2,1536,128]{2,1,0:T(8,128)(2,1)}, u32[]{:S(2)}, u32[]{:S(2)}) collective-permute-start(bf16[2,1536,128]{2,1,0:T(8,128)(2,1)} %maximum_maximum_fusion.3), channel_id=1, source_target_pairs={{0,32},{8,40},{16,48},{24,56},{32,64},{40,72},{48,80},{56,88},{64,... | collective-permute-start | bytes 2359304 | tf_op jit(solution)/shard_map/ppermute | solution.py:12
  128.0 8.5 %copy-start.10 = (bf16[2,192,128]{2,1,0:T(8,128)(2,1)S(1)}, bf16[2,192,128]{2,1,0:T(8,128)(2,1)}, u32[]{:S(2)}) copy-start(bf16[2,192,128]{2,1,0:T(8,128)(2,1)} %copy-done.9) | copy-start | bytes 294916
  137.5 122.7 %collective-permute-start.10 = (bf16[2,1536,128]{2,1,0:T(8,128)(2,1)}, bf16[2,1536,128]{2,1,0:T(8,128)(2,1)}, u32[]{:S(2)}, u32[]{:S(2)}) collective-permute-start(bf16[2,1536,128]{2,1,0:T(8,128)(2,1)} %maximum_maximum_fusion.4), channel_id=1, source_target_pairs={{0,64},{8,72},{16,80},{24,88},{32,96},{40,104},{48,112},{56,120},{... | collective-permute-start | bytes 2359304 | tf_op jit(solution)/shard_map/ppermute | solution.py:12
  139.5 10.8 %copy-start.26 = (f32[1,96]{1,0:T(1,128)S(1)}, f32[1,96]{1,0:T(1,128)}, u32[]{:S(2)}) copy-start(f32[1,96]{1,0:T(1,128)} %get-tuple-element.1984) | copy-start | bytes 1156
  139.5 10.8 %copy-start.39 = (pred[96,768]{1,0:T(32,128)(4,1)S(1)}, pred[96,768]{1,0:T(32,128)(4,1)}, u32[]{:S(2)}) copy-start(pred[96,768]{1,0:T(32,128)(4,1)} %get-tuple-element.2985) | copy-start | bytes 221188
  139.5 10.8 %copy-start.42 = (f32[1,96]{1,0:T(1,128)S(1)}, f32[1,96]{1,0:T(1,128)}, u32[]{:S(2)}) copy-start(f32[1,96]{1,0:T(1,128)} %get-tuple-element.1985) | copy-start | bytes 1156
  147.1 136.4 %collective-permute-start.16 = (bf16[2,1536,128]{2,1,0:T(8,128)(2,1)}, bf16[2,1536,128]{2,1,0:T(8,128)(2,1)}, u32[]{:S(2)}, u32[]{:S(2)}) collective-permute-start(bf16[2,1536,128]{2,1,0:T(8,128)(2,1)} %constant_dynamic-update-slice_fusion.5), channel_id=1, source_target_pairs={{0,128},{8,136},{16,144},{24,152},{32,160},{40,168},{48,176},{56,1... | collective-permute-start | bytes 2359304 | tf_op jit(solution)/shard_map/ppermute | solution.py:12
  179.3 175.8 %collective-permute-start.2 = (bf16[2,3072,128]{2,1,0:T(8,128)(2,1)}, bf16[2,3072,128]{2,1,0:T(8,128)(2,1)}, u32[]{:S(2)}, u32[]{:S(2)}) collective-permute-start(bf16[2,3072,128]{2,1,0:T(8,128)(2,1)} %maximum_maximum_fusion), channel_id=1, source_target_pairs={{0,32},{8,40},{16,48},{24,56},{32,64},{40,72},{48,80},{56,88},{64,... | collective-permute-start | bytes 4718600 | tf_op jit(solution)/shard_map/ppermute | solution.py:12
  238.9 14.2 %copy-start.4 = (bf16[2,384,128]{2,1,0:T(8,128)(2,1)S(1)}, bf16[2,384,128]{2,1,0:T(8,128)(2,1)}, u32[]{:S(2)}) copy-start(bf16[2,384,128]{2,1,0:T(8,128)(2,1)} %copy-done.3) | copy-start | bytes 589828
  255.6 125.9 %collective-permute-start.6 = (bf16[2,3072,128]{2,1,0:T(8,128)(2,1)}, bf16[2,3072,128]{2,1,0:T(8,128)(2,1)}, u32[]{:S(2)}, u32[]{:S(2)}) collective-permute-start(bf16[2,3072,128]{2,1,0:T(8,128)(2,1)} %maximum_maximum_fusion.1), channel_id=1, source_target_pairs={{0,64},{8,72},{16,80},{24,88},{32,96},{40,104},{48,112},{56,120},{... | collective-permute-start | bytes 4718600 | tf_op jit(solution)/shard_map/ppermute | solution.py:12
  281.5 124.7 %collective-permute-start.11 = (bf16[2,3072,128]{2,1,0:T(8,128)(2,1)}, bf16[2,3072,128]{2,1,0:T(8,128)(2,1)}, u32[]{:S(2)}, u32[]{:S(2)}) collective-permute-start(bf16[2,3072,128]{2,1,0:T(8,128)(2,1)} %constant_dynamic-update-slice_fusion), channel_id=1, source_target_pairs={{0,128},{8,136},{16,144},{24,152},{32,160},{40,168},{48,176},{56,1... | collective-permute-start | bytes 4718600 | tf_op jit(solution)/shard_map/ppermute | solution.py:12
  290.0 149.1 %collective-permute-start.17 = (bf16[2,3072,128]{2,1,0:T(8,128)(2,1)}, bf16[2,3072,128]{2,1,0:T(8,128)(2,1)}, u32[]{:S(2)}, u32[]{:S(2)}) collective-permute-start(bf16[2,3072,128]{2,1,0:T(8,128)(2,1)} %constant_dynamic-update-slice_fusion.10), channel_id=1, source_target_pairs={{0,256},{8,264},{16,272},{24,280},{32,288},{40,296},{48,304},{56,3... | collective-permute-start | bytes 4718600 | tf_op jit(solution)/shard_map/ppermute | solution.py:12
  407.6 31.3 %copy-start.50 = (f32[768]{0:T(1024)S(1)}, f32[768]{0:T(1024)}, u32[]{:S(2)}) copy-start(f32[768]{0:T(1024)} %mul.730) | copy-start | bytes 9220
  440.6 16.7 %copy-start.55 = (pred[1,768,1]{1,2,0:T(4,128)(4,1)S(1)}, pred[1,768,1]{1,2,0:T(4,128)(4,1)}, u32[]{:S(2)}) copy-start(pred[1,768,1]{1,2,0:T(4,128)(4,1)} %stack.80) | copy-start | bytes 2308
  440.6 16.7 %copy-start.56 = (pred[1,768,1]{1,2,0:T(4,128)(4,1)S(1)}, pred[1,768,1]{1,2,0:T(4,128)(4,1)}, u32[]{:S(2)}) copy-start(pred[1,768,1]{1,2,0:T(4,128)(4,1)} %stack.79) | copy-start | bytes 2308
  440.6 16.7 %copy-start.58 = (pred[1,768,1]{1,2,0:T(4,128)(4,1)S(1)}, pred[1,768,1]{1,2,0:T(4,128)(4,1)}, u32[]{:S(2)}) copy-start(pred[1,768,1]{1,2,0:T(4,128)(4,1)} %stack.81) | copy-start | bytes 2308
  440.6 16.7 %copy-start.59 = (pred[4]{0:T(512)(128)(4,1)S(1)}, pred[4]{0:T(512)(128)(4,1)}, u32[]{:S(2)}) copy-start(pred[4]{0:T(512)(128)(4,1)} %pad.73.clone) | copy-start | bytes 16
  440.6 17.0 %copy-start.52 = (f32[768]{0:T(1024)S(1)}, f32[768]{0:T(1024)}, u32[]{:S(2)}) copy-start(f32[768]{0:T(1024)} %mul.737) | copy-start | bytes 9220
  440.6 17.1 %copy-start.53 = (pred[1,768]{1,0:T(4,128)(4,1)S(1)}, pred[1,768]{1,0:T(4,128)(4,1)}, u32[]{:S(2)}) copy-start(pred[1,768]{1,0:T(4,128)(4,1)} %stack.66) | copy-start | bytes 2308
  440.6 17.1 %copy-start.54 = (pred[1,768]{1,0:T(4,128)(4,1)S(1)}, pred[1,768]{1,0:T(4,128)(4,1)}, u32[]{:S(2)}) copy-start(pred[1,768]{1,0:T(4,128)(4,1)} %stack.65) | copy-start | bytes 2308
  440.6 17.1 %copy-start.57 = (pred[1,768]{1,0:T(4,128)(4,1)S(1)}, pred[1,768]{1,0:T(4,128)(4,1)}, u32[]{:S(2)}) copy-start(pred[1,768]{1,0:T(4,128)(4,1)} %stack.67) | copy-start | bytes 2308
  (34 other events, 117.3 us)
where the time goes:
time: 479 us; the launch traced here: 476 us
  waiting for transfers between devices  115 us (24%)
  other arithmetic  105 us (22%)
  local copies, waits for them, and re-layouts  70.2 us (15%)
  starting transfers between devices  55 us (11%)
  matrix products  52.4 us (11%)
  loops' own time  49.9 us (10%)
  blocking collectives  16.7 us (3%)
  between operations  11.5 us (2%)
    ppermute x18, waiting for transfers between devices, from_behind(): lax.ppermute(value, axis, [(source, source + steps) for source in range(f...  115 us
    ppermute x18, starting transfers between devices, from_behind(): lax.ppermute(value, axis, [(source, source + steps) for source in range(f...  55 us
    another operation x8, loops' own time, attend_piece(): state_now, _ = lax.scan(advance, state_now, block_items)  48.2 us
    and x42, other arithmetic, advance(): (key_index[None, :] >= segment_low) & (key_index[None, :] <= query_index[...  40 us
    dynamic_slice x36, local copies, waits for them, and re-layouts, attend_piece(): state_now, _ = lax.scan(advance, state_now, block_items)  25.7 us
    dot_general x43, matrix products, update(): jnp.einsum('qhd,khd->hqk', query_block, key_block, preferred_element_type...  22.6 us
    dot_general x43, matrix products, update(): jnp.einsum('hqk,khd->hqd', weights.astype(jnp.bfloat16), value_block, pre...  19.8 us
    add x43, other arithmetic, update(): new_sum = running_sum * factor + jnp.sum(weights, axis=2)  18.6 us
  transfers between devices with their start and end apart: 18, of which 4 were waited for; matrix products, arithmetic and copies ran while one was open for 44% of the time, Pallas kernels for 0%

commit v1 on v0

v1 whole, which is shorter than its diff:
```python
import math

import jax
import jax.numpy as jnp
from jax import lax
from jax.experimental import pallas as pl
from jax.experimental.pallas import tpu as pltpu
from jax.sharding import PartitionSpec as P

ROWS = 768
HD = 128
CHUNK = 256
LANES = 8
GROUPS = 8
BRANCHES = 4
PICKED = (0, 384, 192, 96)
START = (0, 0, 384, 576)
TOTAL = 672
CUT = (0, 0, 384, 384, 576, 576, 576, 576)
SCALE = math.log2(math.e) / math.sqrt(HD)
NEG = -1e30
LOW, HIGH = 2.0**-60, 2.0**120
F32, BF16 = jnp.float32, jnp.bfloat16


def message_rows(d):
    rows = TOTAL - CUT[d]
    sums = -(-rows // 128)
    return rows, sums, rows + -(-3 * sums // 16) * 16


def iota(shape, axis):
    return lax.broadcasted_iota(jnp.int32, shape, axis)


def dot_t(a, b):
    return lax.dot_general(a, b, (((1,), (1,)), ((), ())), preferred_element_type=F32)


def pick_matrix(sm):
    parts = []
    for b in range(1, BRANCHES):
        count, dilation = CHUNK >> b, 1 << b
        hit = iota((count, CHUNK), 1) == iota((count, CHUNK), 0) * dilation + sm[1 + b]
        parts.append(jnp.where(hit, 1.0, 0.0).astype(BF16))
    return jnp.concatenate(parts, axis=0)


def with_ones(values):
    return jnp.concatenate([values, jnp.ones_like(values)], axis=1)


def prep_kernel(sm, q, k, v, kv, near, middle, far):
    kv[:, :HD] = k[...]
    kv[:, HD:] = v[...]
    pick = pick_matrix(sm)
    for c in range(ROWS // CHUNK):
        got = jnp.dot(pick, q[c * CHUNK : (c + 1) * CHUNK, :], preferred_element_type=F32).astype(BF16)
        for b in range(1, BRANCHES):
            count = CHUNK >> b
            at = CHUNK - (CHUNK >> (b - 1))
            piece = got[at : at + count, :]
            row = START[b] + c * count
            near[row : row + count, :] = piece
            if b >= 2:
                middle[row - 384 : row - 384 + count, :] = piece
            if b >= 3:
                far[row - 576 : row - 576 + count, :] = piece


def fast_tile(q, kv, allowed=None):
    p = jnp.exp2(dot_t(q, kv[:, :HD]) * SCALE)
    if allowed is not None:
        p = jnp.where(allowed, p, 0.0)
    return jnp.dot(p.astype(BF16), with_ones(kv[:, HD:]), preferred_element_type=F32)


def slow_tile(q, kv, allowed, acc, top, rows):
    s = jnp.where(allowed, dot_t(q, kv[:, :HD]) * SCALE, NEG)
    old = top[rows, :]
    new = jnp.maximum(old, jnp.broadcast_to(jnp.max(s, axis=1, keepdims=True), old.shape))
    factor = jnp.exp2(old - new)
    p = jnp.where(allowed, jnp.exp2(s - new[:, :1]), 0.0).astype(BF16)
    added = jnp.dot(p, with_ones(kv[:, HD:]), preferred_element_type=F32)
    acc[rows, :] = acc[rows, :] * jnp.concatenate([factor, factor], axis=1) + added
    top[rows, :] = new


def in_range(total):
    return (jnp.min(total) >= LOW) & (jnp.max(total) <= HIGH)


def branch_pass(q, kv, acc, top, own, lane):
    keys = kv.shape[0]
    step = 768
    acc[...] = jnp.zeros_like(acc)
    top[...] = jnp.zeros_like(top)

    def fast(i, carry):
        block = kv[pl.ds(pl.multiple_of(i * step, step), step), :]
        for c in range(ROWS // CHUNK):
            rows = pl.ds(c * CHUNK, CHUNK)
            allowed = None
            if c * CHUNK < own:
                row = iota((CHUNK, step), 0) + c * CHUNK
                col = iota((CHUNK, step), 1) + i * step
                allowed = (row >= own) | (col <= row + lane * own)
            acc[rows, :] += fast_tile(q[rows, :], block, allowed)
        return carry

    lax.fori_loop(0, keys // step, fast, 0)

    @pl.when(jnp.logical_not(in_range(acc[:, HD:])))
    def _():
        acc[...] = jnp.zeros_like(acc)
        top[...] = jnp.full_like(top, NEG)

        def slow(i, carry):
            block = kv[pl.ds(pl.multiple_of(i * CHUNK, CHUNK), CHUNK), :]

            def rows_step(c, inner):
                rows = pl.ds(pl.multiple_of(c * CHUNK, CHUNK), CHUNK)
                row = iota((CHUNK, CHUNK), 0) + c * CHUNK
                col = iota((CHUNK, CHUNK), 1) + i * CHUNK
                allowed = (row >= own) | (col <= row + lane * own)
                slow_tile(q[rows, :], block, allowed, acc, top, rows)
                return inner

            return lax.fori_loop(0, ROWS // CHUNK, rows_step, carry)

        lax.fori_loop(0, keys // CHUNK, slow, 0)


def split3(x):
    high = x.astype(BF16)
    rest = x - high.astype(F32)
    mid = rest.astype(BF16)
    return high, mid, (rest - mid.astype(F32)).astype(BF16)


def block_index(r, sibling, lane):
    z, core = lane // 2, lane % 2
    return lax.rem(z - r + 4, 4) * 2 + (1 - core if sibling else core)


def cross_kernel(sm, *refs):
    kvs, refs = refs[:8], refs[8:]
    own_q, refs = refs[0], refs[1:]
    qs, refs = (None,) + refs[:7], refs[7:]
    outs, refs = (None,) + refs[:7], refs[7:]
    own_out, own_sum, refs = refs[0], refs[1], refs[2:]
    keys, refs = (None,) + refs[:3], refs[3:]
    q_all, acc, top, sums = refs[0], refs[1], refs[2], (None,) + refs[3:10]
    lane = sm[1]
    pick = pick_matrix(sm)
    for n, kv in enumerate(kvs):
        block = block_index(n // 2, n % 2, lane)
        for c in range(ROWS // CHUNK):
            got = jnp.dot(pick, kv[c * CHUNK : (c + 1) * CHUNK, :], preferred_element_type=F32).astype(BF16)
            for b in range(1, BRANCHES):
                count = CHUNK >> b
                at = CHUNK - (CHUNK >> (b - 1))
                row = pl.multiple_of(block * PICKED[b] + c * count, count)
                keys[b][pl.ds(row, count), :] = got[at : at + count, :]
    for d in range(1, GROUPS):
        sums[d][...] = jnp.zeros_like(sums[d])
    for b in range(1, BRANCHES):
        own, first = PICKED[b], START[b]
        q_all[0:own, :] = own_q[first : first + own, :]
        for d in range(1, 1 << b):
            q_all[d * own : (d + 1) * own, :] = qs[d][first - CUT[d] : first - CUT[d] + own, :]
        branch_pass(q_all, keys[b], acc, top, own, lane)
        for d in range(1 << b):
            rows = slice(d * own, (d + 1) * own)
            total = acc[rows, HD:]
            out = acc[rows, :HD] / total
            log_sum = top[rows, :] + jnp.log2(total)
            if d == 0:
                own_out[first : first + own, :] = out
                own_sum[first : first + own, :] = log_sum
            else:
                at = first - CUT[d]
                outs[d][at : at + own, :] = out.astype(BF16)
                sums[d][at : at + own, :] = log_sum
    diagonal = iota((128, 128), 0) == iota((128, 128), 1)
    for d in range(1, GROUPS):
        rows, count, padded = message_rows(d)
        tail = jnp.zeros((padded - rows, 128), F32)
        place = iota(tail.shape, 0)
        for c in range(count):
            line = jnp.sum(jnp.where(diagonal, sums[d][c * 128 : (c + 1) * 128, :], 0.0), axis=0, keepdims=True)
            for n, piece in enumerate(split3(line)):
                tail = jnp.where(place == 3 * c + n, jnp.broadcast_to(piece.astype(F32), tail.shape), tail)
        outs[d][rows:padded, :] = tail.astype(BF16)


def dense_kernel(sm, *refs):
    kvs = refs[:8]
    q, out, log_sum, acc, top = refs[8:]
    lane = sm[1]
    top[...] = jnp.zeros_like(top)
    lower = iota((CHUNK, CHUNK), 1) <= iota((CHUNK, CHUNK), 0)
    for c in range(ROWS // CHUNK):
        rows = pl.ds(c * CHUNK, CHUNK)
        total = fast_tile(q[rows, :], kvs[0][c * CHUNK : (c + 1) * CHUNK, :], lower)
        if c:
            total = total + fast_tile(q[rows, :], kvs[0][: c * CHUNK, :])
        acc[rows, :] = total
    for n in range(1, 8):

        @pl.when(block_index(n // 2, n % 2, lane) < lane)
        def _(n=n):
            for c in range(ROWS // CHUNK):
                rows = pl.ds(c * CHUNK, CHUNK)
                acc[rows, :] += fast_tile(q[rows, :], kvs[n][...])

    @pl.when(jnp.logical_not(in_range(acc[:, HD:])))
    def _():
        acc[...] = jnp.zeros_like(acc)
        top[...] = jnp.full_like(top, NEG)
        for n in range(8):
            block = block_index(n // 2, n % 2, lane)

            @pl.when(block <= lane)
            def _(n=n, block=block):
                def step(i, carry):
                    c, k = i // 3, lax.rem(i, 3)
                    rows = pl.ds(pl.multiple_of(c * CHUNK, CHUNK), CHUNK)
                    part = kvs[n][pl.ds(pl.multiple_of(k * CHUNK, CHUNK), CHUNK), :]
                    row = iota((CHUNK, CHUNK), 0) + c * CHUNK + lane * ROWS
                    col = iota((CHUNK, CHUNK), 1) + k * CHUNK + block * ROWS
                    slow_tile(q[rows, :], part, col <= row, acc, top, rows)
                    return carry

                lax.fori_loop(0, 9, step, 0)

    total = acc[:, HD:]
    out[...] = acc[:, :HD] / total
    log_sum[...] = top[...] + jnp.log2(total)


def merge_kernel(sm, *refs):
    got, refs = (None,) + refs[:7], refs[7:]
    own_out, own_sum, out0, sum0, merged, got_sums = refs[0], refs[1], refs[2], refs[3], refs[4], (None,) + refs[5:12]
    compact, compact_sum = refs[12], refs[13]
    group = sm[0]
    diagonal = iota((128, 128), 0) == iota((128, 128), 1)
    ones = jnp.ones((128, 128), BF16)
    for d in range(1, GROUPS):
        rows, count, _ = message_rows(d)
        for c in range(count):
            total = jnp.zeros((128, 128), F32)
            for n in range(3):
                line = got[d][rows + 3 * c + n : rows + 3 * c + n + 1, :]
                spread = jnp.where(diagonal, jnp.broadcast_to(line.astype(F32), (128, 128)), 0.0).astype(BF16)
                total = total + jnp.dot(spread, ones, preferred_element_type=F32)
            got_sums[d][c * 128 : (c + 1) * 128, :] = total
    for b in range(1, BRANCHES):
        own, first = PICKED[b], START[b]
        outs = [own_out[first : first + own, :]]
        logs = [own_sum[first : first + own, :]]
        for d in range(1, 1 << b):
            at = first - CUT[d]
            valid = lax.rem(group, 1 << b) >= d
            outs.append(got[d][at : at + own, :].astype(F32))
            logs.append(jnp.where(valid, got_sums[d][at : at + own, :], NEG))
        best = logs[0]
        for log in logs[1:]:
            best = jnp.maximum(best, log)
        top = jnp.zeros_like(best)
        bottom = jnp.zeros_like(best)
        for out, log in zip(outs, logs):
            weight = jnp.exp2(log - best)
            top = top + weight * out
            bottom = bottom + weight
        compact[first : first + own, :] = top / bottom
        compact_sum[first : first + own, :] = best + jnp.log2(bottom)
    for c in range(ROWS // CHUNK):
        rows = slice(c * CHUNK, (c + 1) * CHUNK)
        outs = [out0[rows, :]]
        logs = [sum0[rows, :]]
        for b in range(1, BRANCHES):
            count, dilation = CHUNK >> b, 1 << b
            at = START[b] + c * count
            offset = sm[1 + b]
            place = jnp.where(
                iota((CHUNK, count), 0) == iota((CHUNK, count), 1) * dilation + offset, 1.0, 0.0
            ).astype(BF16)
            out_parts = split3(compact[at : at + count, :])
            log_parts = split3(compact_sum[at : at + count, :])
            first = jnp.concatenate([out_parts[0], log_parts[0]], axis=1)
            second = jnp.concatenate([out_parts[1], log_parts[1]], axis=1)
            spread = jnp.dot(place, first, preferred_element_type=F32)
            spread = spread + jnp.dot(place, second, preferred_element_type=F32)
            log = spread[:, HD:] + jnp.dot(place, log_parts[2], preferred_element_type=F32)
            chosen = lax.rem(iota((CHUNK, HD), 0), dilation) == offset
            outs.append(spread[:, :HD])
            logs.append(jnp.where(chosen, log, NEG))
        best = logs[0]
        for log in logs[1:]:
            best = jnp.maximum(best, log)
        top = jnp.zeros_like(best)
        bottom = jnp.zeros_like(best)
        for out, log in zip(outs, logs):
            weight = jnp.exp2(log - best)
            top = top + weight * out
            bottom = bottom + weight
        merged[rows, :] = (top / bottom).astype(BF16)


def call(kernel, name, sm, operands, outputs, scratch, flops):
    shapes = [jax.ShapeDtypeStruct(shape, dtype) for shape, dtype in outputs]
    moved = sum(math.prod(x.shape) * x.dtype.itemsize for x in list(operands) + shapes)
    return pl.pallas_call(
        kernel,
        name=name,
        out_shape=shapes,
        in_specs=[pl.BlockSpec(memory_space=pltpu.SMEM)]
        + [pl.BlockSpec(memory_space=pltpu.VMEM)] * len(operands),
        out_specs=[pl.BlockSpec(memory_space=pltpu.VMEM)] * len(shapes),
        scratch_shapes=[pltpu.VMEM(shape, dtype) for shape, dtype in scratch],
        compiler_params=pltpu.CompilerParams(vmem_limit_bytes=48 * 1024 * 1024),
        cost_estimate=pl.CostEstimate(flops=flops, bytes_accessed=moved, transcendentals=0),
    )(sm, *operands)


def place_of(index):
    x, z, core = index // 16, index // 2 % 8, index % 2
    return 2 * x + z // 4, z % 4, core


def index_of(group, z, core):
    return (group // 2 * 8 + group % 2 * 4 + z) * 2 + core


def to_earlier(d):
    pairs = []
    for index in range(64):
        group, z, core = place_of(index)
        if group >= d:
            pairs.append((index, index_of(group - d, z ^ 2 if d % 2 else z, core)))
    return pairs


def rotation(r):
    pairs = []
    for index in range(64):
        group, z, core = place_of(index)
        pairs.append((index, index_of(group, (z + r) % 4, core)))
    return pairs


def on_device(queries, key_rows, values, offsets):
    seq, head = lax.axis_index("seq"), lax.axis_index("head")
    mine = lax.dynamic_slice_in_dim(offsets, head, 1, axis=1)[:, 0]
    sm = jnp.concatenate([jnp.stack([seq // 8, seq % 8]).astype(jnp.int32), mine[1:], jnp.zeros((3,), jnp.int32)])
    kv, near, middle, far = call(
        prep_kernel,
        "pick_queries",
        sm,
        [queries, key_rows, values],
        [((ROWS, 2 * HD), BF16), ((TOTAL, HD), BF16), ((288, HD), BF16), ((96, HD), BF16)],
        [],
        2 * 672 * 256 * 128,
    )
    pair = [(i, i ^ 1) for i in range(64)]
    gathered = [kv] + [lax.ppermute(kv, "seq", rotation(r)) for r in (1, 2, 3)]
    kvs = []
    for block in gathered:
        kvs += [block, lax.ppermute(block, "seq", pair)]
    sent = [None, near, middle, middle, far, far, far, far]
    visiting = [lax.ppermute(sent[d], "seq", to_earlier(d)) for d in range(1, GROUPS)]
    crossed = call(
        cross_kernel,
        "branches_1_to_3",
        sm,
        kvs + [near] + visiting,
        [((message_rows(d)[2], HD), BF16) for d in range(1, GROUPS)] + [((TOTAL, HD), F32)] * 2,
        [((3072, 2 * HD), BF16), ((1536, 2 * HD), BF16), ((768, 2 * HD), BF16)]
        + [((ROWS, HD), BF16), ((ROWS, 2 * HD), F32), ((ROWS, HD), F32)]
        + [((message_rows(d)[1] * 128, 128), F32) for d in range(1, GROUPS)],
        4 * 768 * 5376 * 128,
    )
    back = [
        lax.ppermute(crossed[d - 1], "seq", [(b, a) for a, b in to_earlier(d)]) for d in range(1, GROUPS)
    ]
    out0, sum0 = call(
        dense_kernel,
        "branch_0",
        sm,
        kvs + [queries],
        [((ROWS, HD), F32)] * 2,
        [((ROWS, 2 * HD), F32), ((ROWS, HD), F32)],
        4 * 768 * 6144 * 128,
    )
    (merged,) = call(
        merge_kernel,
        "merge",
        sm,
        back + list(crossed[7:]) + [out0, sum0],
        [((ROWS, HD), BF16)],
        [((message_rows(d)[1] * 128, 128), F32) for d in range(1, GROUPS)] + [((TOTAL, HD), F32)] * 2,
        1000000,
    )
    return lax.all_to_all(merged, "head", split_axis=0, concat_axis=1, tiled=True)


def solution(mesh):
    placed = (P("seq", "head"), P("seq", "head"), P("seq", "head"), P())
    return jax.shard_map(
        on_device, mesh=mesh, in_specs=placed, out_specs=P(("seq", "head"), None), check_vma=False
    )
```

time: 479 us -> 211 us (0.44)
  the two profiles are of different devices: /device:TPU:450 before, /device:TPU:192 now
where the time goes in v1:
time: 211 us; the launch traced here: 210 us
  Pallas kernels  91.3 us (43%)
  waiting for transfers between devices  56.2 us (27%)
  starting transfers between devices  41.3 us (20%)
  blocking collectives  16.7 us (8%)
  local copies, waits for them, and re-layouts  4.35 us (2%)
    pallas_call x4, Pallas kernels, call(): pl.pallas_call(kernel, name=name, out_shape=shapes, in_specs=[pl.BlockSpe...  91.3 us
    ppermute x7, waiting for transfers between devices, on_device(): lax.ppermute(sent[d], 'seq', to_earlier(d))  40.1 us
    all_to_all x1, blocking collectives, on_device(): lax.all_to_all(merged, 'head', split_axis=0, concat_axis=1, tiled=True)  16.7 us
    ppermute x3, waiting for transfers between devices, on_device(): gathered = [kv] + [lax.ppermute(kv, 'seq', rotation(r)) for r in (1, 2, 3)]  16 us
    ppermute x7, starting transfers between devices, on_device(): lax.ppermute(crossed[d - 1], 'seq', [(b, a) for a, b in to_earlier(d)])  14 us
    ppermute x3, starting transfers between devices, on_device(): gathered = [kv] + [lax.ppermute(kv, 'seq', rotation(r)) for r in (1, 2, 3)]  9.51 us
    ppermute x7, starting transfers between devices, on_device(): lax.ppermute(sent[d], 'seq', to_earlier(d))  9.13 us
    ppermute x4, starting transfers between devices, on_device(): kvs += [block, lax.ppermute(block, 'seq', pair)]  8.63 us
  transfers between devices with their start and end apart: 21, of which 7 were waited for; matrix products, arithmetic and copies ran while one was open for 0% of the time, Pallas kernels for 21%

profile of v1, /device:TPU:192, one launch (start us, length us, event | category | flops | bytes accessed | tf_op | source)
XLA Modules:
  0.0 210.2 jit_solution(18093328056433378022)
XLA Ops:
  0.0 0.7 copy-done
  0.7 0.1 constant_dynamic-slice_fusion
  0.8 0.1 slice_reduce_fusion
  0.9 0.1 pad_add_fusion.sm
  1.0 0.9 copy-done.1
  1.9 0.9 copy-done.2
  2.8 0.9 copy-done.3
  3.8 0.8 pick_queries.1
  4.6 5.1 %collective-permute-start.1 = (bf16[768,256]{1,0:T(8,128)(2,1)S(1)}, bf16[768,256]{1,0:T(8,128)(2,1)S(1)}, u32[]{:S(2)}, u32[]{:S(2)}) collective-permute-start(bf16[768,256]{1,0:T(8,128)(2,1)S(1)} %get-tuple-element.20.refs_0_), channel_id=1, source_target_pairs={{0,16},{8,24},{16,32},{24,40},{32,48},{40,56},{48,0},{56,8},{64,80... | collective-permute-start | bytes 1179656 | tf_op jit(solution)/shard_map/ppermute | solution.py:367
  9.7 1.9 collective-permute-start.3
  11.7 2.5 %collective-permute-start.5 = (bf16[768,256]{1,0:T(8,128)(2,1)S(1)}, bf16[768,256]{1,0:T(8,128)(2,1)S(1)}, u32[]{:S(2)}, u32[]{:S(2)}) collective-permute-start(bf16[768,256]{1,0:T(8,128)(2,1)S(1)} %get-tuple-element.20.refs_0_), channel_id=1, source_target_pairs={{0,48},{8,56},{16,0},{24,8},{32,16},{40,24},{48,32},{56,40},{64,11... | collective-permute-start | bytes 1179656 | tf_op jit(solution)/shard_map/ppermute | solution.py:367
  14.1 1.3 collective-permute-start.10
  15.4 1.3 collective-permute-start.11
  16.7 4.6 %collective-permute-done.10.refs_12_ = bf16[96,128]{1,0:T(8,128)(2,1)S(1)} collective-permute-done((bf16[96,128]{1,0:T(8,128)(2,1)S(1)}, bf16[96,128]{1,0:T(8,128)(2,1)S(1)}, u32[]{:S(2)}, u32[]{:S(2)}) %collective-permute-start.10) | collective-permute-done | bytes 24608 | tf_op jit(solution)/shard_map/ppermute | solution.py:372
  21.4 1.9 collective-permute-start
  23.3 2.4 %collective-permute-start.2 = (bf16[768,256]{1,0:T(8,128)(2,1)S(1)}, bf16[768,256]{1,0:T(8,128)(2,1)S(1)}, u32[]{:S(2)}, u32[]{:S(2)}) collective-permute-start(bf16[768,256]{1,0:T(8,128)(2,1)S(1)} %collective-permute-done.1.refs_2_), channel_id=1, source_target_pairs={{0,8},{8,0},{16,24},{24,16},{32,40},{40,32},{48,56},{56,48},{64,72... | collective-permute-start | bytes 1179656 | tf_op jit(solution)/shard_map/ppermute | solution.py:370
  25.7 16.0 %collective-permute-done.3.refs_4_ = bf16[768,256]{1,0:T(8,128)(2,1)S(1)} collective-permute-done((bf16[768,256]{1,0:T(8,128)(2,1)S(1)}, bf16[768,256]{1,0:T(8,128)(2,1)S(1)}, u32[]{:S(2)}, u32[]{:S(2)}) %collective-permute-start.3) | collective-permute-done | bytes 393248 | tf_op jit(solution)/shard_map/ppermute | solution.py:367
  41.7 1.9 collective-permute-start.4
  43.6 0.0 collective-permute-done.5.refs_6_
  43.6 2.4 %collective-permute-start.6 = (bf16[768,256]{1,0:T(8,128)(2,1)S(1)}, bf16[768,256]{1,0:T(8,128)(2,1)S(1)}, u32[]{:S(2)}, u32[]{:S(2)}) collective-permute-start(bf16[768,256]{1,0:T(8,128)(2,1)S(1)} %collective-permute-done.5.refs_6_), channel_id=1, source_target_pairs={{0,8},{8,0},{16,24},{24,16},{32,40},{40,32},{48,56},{56,48},{64,72... | collective-permute-start | bytes 1179656 | tf_op jit(solution)/shard_map/ppermute | solution.py:370
  46.1 0.0 collective-permute-done.11.refs_13_
  46.1 1.3 collective-permute-start.12
  47.4 5.6 %collective-permute-done.12.refs_14_ = bf16[96,128]{1,0:T(8,128)(2,1)S(1)} collective-permute-done((bf16[96,128]{1,0:T(8,128)(2,1)S(1)}, bf16[96,128]{1,0:T(8,128)(2,1)S(1)}, u32[]{:S(2)}, u32[]{:S(2)}) %collective-permute-start.12) | collective-permute-done | bytes 24608 | tf_op jit(solution)/shard_map/ppermute | solution.py:372
  53.0 1.3 collective-permute-start.13
  54.3 8.7 %collective-permute-done.13.refs_15_ = bf16[96,128]{1,0:T(8,128)(2,1)S(1)} collective-permute-done((bf16[96,128]{1,0:T(8,128)(2,1)S(1)}, bf16[96,128]{1,0:T(8,128)(2,1)S(1)}, u32[]{:S(2)}, u32[]{:S(2)}) %collective-permute-start.13) | collective-permute-done | bytes 24608 | tf_op jit(solution)/shard_map/ppermute | solution.py:372
  63.0 1.3 collective-permute-start.8
  64.3 4.9 %collective-permute-done.8.refs_10_ = bf16[288,128]{1,0:T(8,128)(2,1)S(1)} collective-permute-done((bf16[288,128]{1,0:T(8,128)(2,1)S(1)}, bf16[288,128]{1,0:T(8,128)(2,1)S(1)}, u32[]{:S(2)}, u32[]{:S(2)}) %collective-permute-start.8) | collective-permute-done | bytes 73760 | tf_op jit(solution)/shard_map/ppermute | solution.py:372
  69.3 1.3 collective-permute-start.9
  70.6 8.1 %collective-permute-done.9.refs_11_ = bf16[288,128]{1,0:T(8,128)(2,1)S(1)} collective-permute-done((bf16[288,128]{1,0:T(8,128)(2,1)S(1)}, bf16[288,128]{1,0:T(8,128)(2,1)S(1)}, u32[]{:S(2)}, u32[]{:S(2)}) %collective-permute-start.9) | collective-permute-done | bytes 73760 | tf_op jit(solution)/shard_map/ppermute | solution.py:372
  78.6 1.4 collective-permute-start.7
  80.0 8.1 %collective-permute-done.7.refs_9_ = bf16[672,128]{1,0:T(8,128)(2,1)S(1)} collective-permute-done((bf16[672,128]{1,0:T(8,128)(2,1)S(1)}, bf16[672,128]{1,0:T(8,128)(2,1)S(1)}, u32[]{:S(2)}, u32[]{:S(2)}) %collective-permute-start.7) | collective-permute-done | bytes 172064 | tf_op jit(solution)/shard_map/ppermute | solution.py:372
  88.2 0.0 collective-permute-done.refs_1_
  88.2 0.0 collective-permute-done.2.refs_3_
  88.2 0.0 collective-permute-done.4.refs_5_
  88.2 0.0 collective-permute-done.6.refs_7_
  88.2 44.6 %branches_1_to_3.1 = (bf16[704,128]{1,0:T(8,128)(2,1)S(1)}, bf16[304,128]{1,0:T(8,128)(2,1)S(1)}, bf16[304,128]{1,0:T(8,128)(2,1)S(1)}, bf16[112,128]{1,0:T(8,12...) custom-call(s32[8]{0:T(128)S(1)} %pad_add_fusion.sm, ...), custom_call_target="tpu_custom_call" | custom-call | flops 2113929216 | bytes 4874240 | tf_op jit(solution)/shard_map/branches_1_to_3/pallas_call | solution.py:314
  132.7 1.3 collective-permute-start.17
  134.0 2.7 %collective-permute-start.18 = (bf16[112,128]{1,0:T(8,128)(2,1)S(1)}, bf16[112,128]{1,0:T(8,128)(2,1)S(1)}, u32[]{:S(2)}, u32[]{:S(2)}) collective-permute-start(bf16[112,128]{1,0:T(8,128)(2,1)S(1)} %get-tuple-element.28), channel_id=1, source_target_pairs={{32,320},{40,328},{48,336},{56,344},{0,352},{8,360},{16,368},{24,3... | collective-permute-start | bytes 86024 | tf_op jit(solution)/shard_map/ppermute | solution.py:385
  136.7 2.5 %collective-permute-start.14 = (bf16[704,128]{1,0:T(8,128)(2,1)S(1)}, bf16[704,128]{1,0:T(8,128)(2,1)S(1)}, u32[]{:S(2)}, u32[]{:S(2)}) collective-permute-start(bf16[704,128]{1,0:T(8,128)(2,1)S(1)} %get-tuple-element.24), channel_id=1, source_target_pairs={{32,64},{40,72},{48,80},{56,88},{0,96},{8,104},{16,112},{24,120},{... | collective-permute-start | bytes 540680 | tf_op jit(solution)/shard_map/ppermute | solution.py:385
  139.2 1.3 collective-permute-start.15
  140.5 1.3 collective-permute-start.16
  141.9 1.3 collective-permute-start.19
  143.2 3.7 %collective-permute-start.20 = (bf16[112,128]{1,0:T(8,128)(2,1)S(1)}, bf16[112,128]{1,0:T(8,128)(2,1)S(1)}, u32[]{:S(2)}, u32[]{:S(2)}) collective-permute-start(bf16[112,128]{1,0:T(8,128)(2,1)S(1)} %get-tuple-element.30), channel_id=1, source_target_pairs={{32,448},{40,456},{48,464},{56,472},{0,480},{8,488},{16,496},{24,5... | collective-permute-start | bytes 86024 | tf_op jit(solution)/shard_map/ppermute | solution.py:385
  146.8 43.8 %branch_0.1 = (f32[768,128]{1,0:T(8,128)S(1)}, f32[768,128]{1,0:T(8,128)S(1)}) custom-call(s32[8]{0:T(128)S(1)} %pad_add_fusion.sm, bf16[768,256]{1,0:T(8,128)(2,1)S(1)} %get-tuple-element.20.refs_0_, bf16[768,256]{1,0:T(8,128)(2,1)S(1)} %collective-permute-done.refs_1_, bf16[768,256]{1,0:T(8,128)(2,1)S(1)} %collective-permute-done.1.refs_2_, ...), custom_call_target="tpu_custom_call" | custom-call | flops 2415919104 | bytes 4128768 | tf_op jit(solution)/shard_map/branch_0/pallas_call | solution.py:314
  190.6 0.0 collective-permute-done.20.refs_6_
  190.7 2.2 %merge.1 = bf16[768,128]{1,0:T(8,128)(2,1)S(1)} custom-call(s32[8]{0:T(128)S(1)} %pad_add_fusion.sm, bf16[704,128]{1,0:T(8,128)(2,1)S(1)} %collective-permute-done.14.refs_0_, bf16[304,128]{1,0:T(8,128)(2,1)S(1)} %collective-permute-done.15.refs_1_, bf16[304,128]{1,0:T(8,128)(2,1)S(1)} %collective-permute-done.16.refs_2_, ...), custom_call_target="tpu_custom_call" | custom-call | flops 1000000 | bytes 2121728 | tf_op jit(solution)/shard_map/merge/pallas_call | solution.py:314
  192.8 16.7 %all_to_all.19 = bf16[8,96,128]{2,1,0:T(8,128)(2,1)S(1)} all-to-all(bf16[8,96,128]{2,1,0:T(8,128)(2,1)S(1)} %bitcast.9), channel_id=1, replica_groups=mesh['seq'=64,'head'=8] {'head'}, dimensions={0} | all-to-all | bytes 393216 | tf_op jit(solution)/shard_map/all_to_all | solution.py:405
  209.5 0.7 copy_bitcast_fusion
  (14 shorter events, 0.0 us)
Async XLA Ops:
  0.0 0.7 copy-start
  1.0 0.9 copy-start.1
  1.9 0.9 copy-start.2
  2.8 0.9 copy-start.3
  4.6 18.7 %collective-permute-start.1 = (bf16[768,256]{1,0:T(8,128)(2,1)S(1)}, bf16[768,256]{1,0:T(8,128)(2,1)S(1)}, u32[]{:S(2)}, u32[]{:S(2)}) collective-permute-start(bf16[768,256]{1,0:T(8,128)(2,1)S(1)} %get-tuple-element.20.refs_0_), channel_id=1, source_target_pairs={{0,16},{8,24},{16,32},{24,40},{32,48},{40,56},{48,0},{56,8},{64,80... | collective-permute-start | bytes 1179656 | tf_op jit(solution)/shard_map/ppermute | solution.py:367
  9.7 32.0 %collective-permute-start.3 = (bf16[768,256]{1,0:T(8,128)(2,1)S(1)}, bf16[768,256]{1,0:T(8,128)(2,1)S(1)}, u32[]{:S(2)}, u32[]{:S(2)}) collective-permute-start(bf16[768,256]{1,0:T(8,128)(2,1)S(1)} %get-tuple-element.20.refs_0_), channel_id=1, source_target_pairs={{0,32},{8,40},{16,48},{24,56},{32,0},{40,8},{48,16},{56,24},{64,96... | collective-permute-start | bytes 1179656 | tf_op jit(solution)/shard_map/ppermute | solution.py:367
  11.7 32.0 %collective-permute-start.5 = (bf16[768,256]{1,0:T(8,128)(2,1)S(1)}, bf16[768,256]{1,0:T(8,128)(2,1)S(1)}, u32[]{:S(2)}, u32[]{:S(2)}) collective-permute-start(bf16[768,256]{1,0:T(8,128)(2,1)S(1)} %get-tuple-element.20.refs_0_), channel_id=1, source_target_pairs={{0,48},{8,56},{16,0},{24,8},{32,16},{40,24},{48,32},{56,40},{64,11... | collective-permute-start | bytes 1179656 | tf_op jit(solution)/shard_map/ppermute | solution.py:367
  14.1 7.2 %collective-permute-start.10 = (bf16[96,128]{1,0:T(8,128)(2,1)S(1)}, bf16[96,128]{1,0:T(8,128)(2,1)S(1)}, u32[]{:S(2)}, u32[]{:S(2)}) collective-permute-start(bf16[96,128]{1,0:T(8,128)(2,1)S(1)} %get-tuple-element.23), channel_id=1, source_target_pairs={{256,0},{264,8},{272,16},{280,24},{288,32},{296,40},{304,48},{312,... | collective-permute-start | bytes 73736 | tf_op jit(solution)/shard_map/ppermute | solution.py:372
  15.4 30.6 %collective-permute-start.11 = (bf16[96,128]{1,0:T(8,128)(2,1)S(1)}, bf16[96,128]{1,0:T(8,128)(2,1)S(1)}, u32[]{:S(2)}, u32[]{:S(2)}) collective-permute-start(bf16[96,128]{1,0:T(8,128)(2,1)S(1)} %get-tuple-element.23), channel_id=1, source_target_pairs={{320,32},{328,40},{336,48},{344,56},{352,0},{360,8},{368,16},{376,... | collective-permute-start | bytes 73736 | tf_op jit(solution)/shard_map/ppermute | solution.py:372
  21.4 66.8 %collective-permute-start = (bf16[768,256]{1,0:T(8,128)(2,1)S(1)}, bf16[768,256]{1,0:T(8,128)(2,1)S(1)}, u32[]{:S(2)}, u32[]{:S(2)}) collective-permute-start(bf16[768,256]{1,0:T(8,128)(2,1)S(1)} %get-tuple-element.20.refs_0_), channel_id=1, source_target_pairs={{0,8},{8,0},{16,24},{24,16},{32,40},{40,32},{48,56},{56,48},{64,72... | collective-permute-start | bytes 1179656 | tf_op jit(solution)/shard_map/ppermute | solution.py:370
  23.3 64.9 %collective-permute-start.2 = (bf16[768,256]{1,0:T(8,128)(2,1)S(1)}, bf16[768,256]{1,0:T(8,128)(2,1)S(1)}, u32[]{:S(2)}, u32[]{:S(2)}) collective-permute-start(bf16[768,256]{1,0:T(8,128)(2,1)S(1)} %collective-permute-done.1.refs_2_), channel_id=1, source_target_pairs={{0,8},{8,0},{16,24},{24,16},{32,40},{40,32},{48,56},{56,48},{64,72... | collective-permute-start | bytes 1179656 | tf_op jit(solution)/shard_map/ppermute | solution.py:370
  41.7 46.4 %collective-permute-start.4 = (bf16[768,256]{1,0:T(8,128)(2,1)S(1)}, bf16[768,256]{1,0:T(8,128)(2,1)S(1)}, u32[]{:S(2)}, u32[]{:S(2)}) collective-permute-start(bf16[768,256]{1,0:T(8,128)(2,1)S(1)} %collective-permute-done.3.refs_4_), channel_id=1, source_target_pairs={{0,8},{8,0},{16,24},{24,16},{32,40},{40,32},{48,56},{56,48},{64,72... | collective-permute-start | bytes 1179656 | tf_op jit(solution)/shard_map/ppermute | solution.py:370
  43.6 44.5 %collective-permute-start.6 = (bf16[768,256]{1,0:T(8,128)(2,1)S(1)}, bf16[768,256]{1,0:T(8,128)(2,1)S(1)}, u32[]{:S(2)}, u32[]{:S(2)}) collective-permute-start(bf16[768,256]{1,0:T(8,128)(2,1)S(1)} %collective-permute-done.5.refs_6_), channel_id=1, source_target_pairs={{0,8},{8,0},{16,24},{24,16},{32,40},{40,32},{48,56},{56,48},{64,72... | collective-permute-start | bytes 1179656 | tf_op jit(solution)/shard_map/ppermute | solution.py:370
  46.1 6.9 %collective-permute-start.12 = (bf16[96,128]{1,0:T(8,128)(2,1)S(1)}, bf16[96,128]{1,0:T(8,128)(2,1)S(1)}, u32[]{:S(2)}, u32[]{:S(2)}) collective-permute-start(bf16[96,128]{1,0:T(8,128)(2,1)S(1)} %get-tuple-element.23), channel_id=1, source_target_pairs={{384,0},{392,8},{400,16},{408,24},{416,32},{424,40},{432,48},{440,... | collective-permute-start | bytes 73736 | tf_op jit(solution)/shard_map/ppermute | solution.py:372
  53.0 10.0 %collective-permute-start.13 = (bf16[96,128]{1,0:T(8,128)(2,1)S(1)}, bf16[96,128]{1,0:T(8,128)(2,1)S(1)}, u32[]{:S(2)}, u32[]{:S(2)}) collective-permute-start(bf16[96,128]{1,0:T(8,128)(2,1)S(1)} %get-tuple-element.23), channel_id=1, source_target_pairs={{448,32},{456,40},{464,48},{472,56},{480,0},{488,8},{496,16},{504,... | collective-permute-start | bytes 73736 | tf_op jit(solution)/shard_map/ppermute | solution.py:372
  63.0 6.2 %collective-permute-start.8 = (bf16[288,128]{1,0:T(8,128)(2,1)S(1)}, bf16[288,128]{1,0:T(8,128)(2,1)S(1)}, u32[]{:S(2)}, u32[]{:S(2)}) collective-permute-start(bf16[288,128]{1,0:T(8,128)(2,1)S(1)} %get-tuple-element.22), channel_id=1, source_target_pairs={{128,0},{136,8},{144,16},{152,24},{160,32},{168,40},{176,48},{184,... | collective-permute-start | bytes 221192 | tf_op jit(solution)/shard_map/ppermute | solution.py:372
  69.3 9.3 %collective-permute-start.9 = (bf16[288,128]{1,0:T(8,128)(2,1)S(1)}, bf16[288,128]{1,0:T(8,128)(2,1)S(1)}, u32[]{:S(2)}, u32[]{:S(2)}) collective-permute-start(bf16[288,128]{1,0:T(8,128)(2,1)S(1)} %get-tuple-element.22), channel_id=1, source_target_pairs={{192,32},{200,40},{208,48},{216,56},{224,0},{232,8},{240,16},{248,... | collective-permute-start | bytes 221192 | tf_op jit(solution)/shard_map/ppermute | solution.py:372
  78.6 68.2 %copy-start.4 = (bf16[768,128]{1,0:T(8,128)(2,1)S(1)}, bf16[768,128]{1,0:T(8,128)(2,1)}, u32[]{:S(2)}) copy-start(bf16[768,128]{1,0:T(8,128)(2,1)} %refs_8_.1) | copy-start | bytes 589828
  78.6 9.5 %collective-permute-start.7 = (bf16[672,128]{1,0:T(8,128)(2,1)S(1)}, bf16[672,128]{1,0:T(8,128)(2,1)S(1)}, u32[]{:S(2)}, u32[]{:S(2)}) collective-permute-start(bf16[672,128]{1,0:T(8,128)(2,1)S(1)} %get-tuple-element.21.refs_8_), channel_id=1, source_target_pairs={{64,32},{72,40},{80,48},{88,56},{96,0},{104,8},{112,16},{120,24},{... | collective-permute-start | bytes 516104 | tf_op jit(solution)/shard_map/ppermute | solution.py:372
  132.7 9.1 %collective-permute-start.17 = (bf16[112,128]{1,0:T(8,128)(2,1)S(1)}, bf16[112,128]{1,0:T(8,128)(2,1)S(1)}, u32[]{:S(2)}, u32[]{:S(2)}) collective-permute-start(bf16[112,128]{1,0:T(8,128)(2,1)S(1)} %get-tuple-element.27), channel_id=1, source_target_pairs={{0,256},{8,264},{16,272},{24,280},{32,288},{40,296},{48,304},{56,3... | collective-permute-start | bytes 86024 | tf_op jit(solution)/shard_map/ppermute | solution.py:385
  134.0 9.1 %collective-permute-start.18 = (bf16[112,128]{1,0:T(8,128)(2,1)S(1)}, bf16[112,128]{1,0:T(8,128)(2,1)S(1)}, u32[]{:S(2)}, u32[]{:S(2)}) collective-permute-start(bf16[112,128]{1,0:T(8,128)(2,1)S(1)} %get-tuple-element.28), channel_id=1, source_target_pairs={{32,320},{40,328},{48,336},{56,344},{0,352},{8,360},{16,368},{24,3... | collective-permute-start | bytes 86024 | tf_op jit(solution)/shard_map/ppermute | solution.py:385
  136.7 53.9 %collective-permute-start.14 = (bf16[704,128]{1,0:T(8,128)(2,1)S(1)}, bf16[704,128]{1,0:T(8,128)(2,1)S(1)}, u32[]{:S(2)}, u32[]{:S(2)}) collective-permute-start(bf16[704,128]{1,0:T(8,128)(2,1)S(1)} %get-tuple-element.24), channel_id=1, source_target_pairs={{32,64},{40,72},{48,80},{56,88},{0,96},{8,104},{16,112},{24,120},{... | collective-permute-start | bytes 540680 | tf_op jit(solution)/shard_map/ppermute | solution.py:385
  139.2 51.4 %collective-permute-start.15 = (bf16[304,128]{1,0:T(8,128)(2,1)S(1)}, bf16[304,128]{1,0:T(8,128)(2,1)S(1)}, u32[]{:S(2)}, u32[]{:S(2)}) collective-permute-start(bf16[304,128]{1,0:T(8,128)(2,1)S(1)} %get-tuple-element.25), channel_id=1, source_target_pairs={{0,128},{8,136},{16,144},{24,152},{32,160},{40,168},{48,176},{56,1... | collective-permute-start | bytes 233480 | tf_op jit(solution)/shard_map/ppermute | solution.py:385
  140.5 50.1 %collective-permute-start.16 = (bf16[304,128]{1,0:T(8,128)(2,1)S(1)}, bf16[304,128]{1,0:T(8,128)(2,1)S(1)}, u32[]{:S(2)}, u32[]{:S(2)}) collective-permute-start(bf16[304,128]{1,0:T(8,128)(2,1)S(1)} %get-tuple-element.26), channel_id=1, source_target_pairs={{32,192},{40,200},{48,208},{56,216},{0,224},{8,232},{16,240},{24,2... | collective-permute-start | bytes 233480 | tf_op jit(solution)/shard_map/ppermute | solution.py:385
  141.9 48.8 %collective-permute-start.19 = (bf16[112,128]{1,0:T(8,128)(2,1)S(1)}, bf16[112,128]{1,0:T(8,128)(2,1)S(1)}, u32[]{:S(2)}, u32[]{:S(2)}) collective-permute-start(bf16[112,128]{1,0:T(8,128)(2,1)S(1)} %get-tuple-element.29), channel_id=1, source_target_pairs={{0,384},{8,392},{16,400},{24,408},{32,416},{40,424},{48,432},{56,4... | collective-permute-start | bytes 86024 | tf_op jit(solution)/shard_map/ppermute | solution.py:385
  143.2 47.5 %collective-permute-start.20 = (bf16[112,128]{1,0:T(8,128)(2,1)S(1)}, bf16[112,128]{1,0:T(8,128)(2,1)S(1)}, u32[]{:S(2)}, u32[]{:S(2)}) collective-permute-start(bf16[112,128]{1,0:T(8,128)(2,1)S(1)} %get-tuple-element.30), channel_id=1, source_target_pairs={{32,448},{40,456},{48,464},{56,472},{0,480},{8,488},{16,496},{24,5... | collective-permute-start | bytes 86024 | tf_op jit(solution)/shard_map/ppermute | solution.py:385

commit v2 on v1

v2 whole, which is shorter than its diff:
```python
import functools
import math

import jax
import jax.numpy as jnp
from jax import lax
from jax.experimental import pallas as pl
from jax.experimental.pallas import tpu as pltpu
from jax.sharding import PartitionSpec as P

ROWS = 768
HD = 128
CHUNK = 256
LANES = 8
GROUPS = 8
BRANCHES = 4
PICKED = (0, 384, 192, 96)
START = (0, 0, 384, 576)
TOTAL = 672
CROSS = (0, 384, 576, 672)
CROSS_START = (0, 0, 384, 960)
VISITING = 1632
CUT = (0, 0, 384, 384, 576, 576, 576, 576)
SCALE = math.log2(math.e) / math.sqrt(HD)
NEG = -1e30
LOW, HIGH = 2.0**-60, 2.0**120
F32, BF16 = jnp.float32, jnp.bfloat16


def message_rows(d):
    rows = TOTAL - CUT[d]
    sums = -(-rows // 128)
    return rows, sums, rows + -(-3 * sums // 16) * 16


def iota(shape, axis):
    return lax.broadcasted_iota(jnp.int32, shape, axis)


def dot_t(a, b):
    return lax.dot_general(a, b, (((1,), (1,)), ((), ())), preferred_element_type=F32)


def pick_matrix(sm):
    parts = []
    for b in range(1, BRANCHES):
        count, dilation = CHUNK >> b, 1 << b
        hit = iota((count, CHUNK), 1) == iota((count, CHUNK), 0) * dilation + sm[1 + b]
        parts.append(jnp.where(hit, 1.0, 0.0).astype(BF16))
    return jnp.concatenate(parts, axis=0)


def with_ones(values):
    return jnp.concatenate([values, jnp.ones_like(values)], axis=1)


def split3(x):
    high = x.astype(BF16)
    rest = x - high.astype(F32)
    mid = rest.astype(BF16)
    return high, mid, (rest - mid.astype(F32)).astype(BF16)


def pack_kernel(k, v, kv, sems):
    copies = [
        pltpu.make_async_copy(k, kv.at[:, pl.ds(0, HD)], sems.at[0]),
        pltpu.make_async_copy(v, kv.at[:, pl.ds(HD, HD)], sems.at[1]),
    ]
    for copy in copies:
        copy.start()
    for copy in copies:
        copy.wait()


def pick_kernel(sm, q, near):
    pick = pick_matrix(sm)
    for c in range(ROWS // CHUNK):
        got = jnp.dot(pick, q[c * CHUNK : (c + 1) * CHUNK, :], preferred_element_type=F32).astype(BF16)
        for b in range(1, BRANCHES):
            count = CHUNK >> b
            at = CHUNK - (CHUNK >> (b - 1))
            piece = got[at : at + count, :]
            row = START[b] + c * count
            near[row : row + count, :] = piece


def fast_tile(q, kv, allowed=None):
    p = jnp.exp2(dot_t(q, kv[:, :HD]) * SCALE)
    if allowed is not None:
        p = jnp.where(allowed, p, 0.0)
    return jnp.dot(p.astype(BF16), with_ones(kv[:, HD:]), preferred_element_type=F32)


def slow_tile(q, kv, allowed, acc, top, rows):
    s = dot_t(q, kv[:, :HD]) * SCALE
    if allowed is not None:
        s = jnp.where(allowed, s, NEG)
    old = top[rows, :]
    new = jnp.maximum(old, jnp.broadcast_to(jnp.max(s, axis=1, keepdims=True), old.shape))
    factor = jnp.exp2(old - new)
    p = jnp.exp2(s - new[:, :1])
    if allowed is not None:
        p = jnp.where(allowed, p, 0.0)
    added = jnp.dot(p.astype(BF16), with_ones(kv[:, HD:]), preferred_element_type=F32)
    acc[rows, :] = acc[rows, :] * jnp.concatenate([factor, factor], axis=1) + added
    top[rows, :] = new


def in_range(total):
    return (jnp.min(total) >= LOW) & (jnp.max(total) <= HIGH)


def select_keys(sm, kv, keys, part):
    pick = pick_matrix(sm)
    for c in range(ROWS // CHUNK):
        got = jnp.dot(pick, kv[c * CHUNK : (c + 1) * CHUNK, :], preferred_element_type=F32).astype(BF16)
        for b in range(1, BRANCHES):
            count = CHUNK >> b
            at = CHUNK - (CHUNK >> (b - 1))
            row = part * PICKED[b] + c * count
            keys[b][row : row + count, :] = got[at : at + count, :]


def add_cross(q, keys, acc, first):
    for b in range(1, BRANCHES):
        size = CROSS[b]
        step = 192
        for at in range(0, size, step):
            rows = pl.ds(CROSS_START[b] + at, min(step, size - at))
            total = fast_tile(q[rows, :], keys[b][...])
            acc[rows, :] = total if first else acc[rows, :] + total


def add_own(q, own_q, blocks, keys, acc):
    for c in range(ROWS // CHUNK):
        rows = pl.ds(c * CHUNK, CHUNK)
        total = acc[rows, :]
        for kv in blocks:
            total = total + fast_tile(q[rows, :], kv[...])
        acc[rows, :] = total
    for b in range(1, BRANCHES):
        step = min(192, PICKED[b])
        for at in range(0, PICKED[b], step):
            start = START[b] + at
            rows = pl.ds(ROWS + start, step)
            acc[rows, :] += fast_tile(own_q[start : start + step, :], keys[b][...])


def first_kernel(sm, mine, other, q, near, own, *keys):
    keys = (None,) + keys
    select_keys(sm, mine, keys, 0)
    select_keys(sm, other, keys, 1)
    lower = iota((CHUNK, CHUNK), 1) <= iota((CHUNK, CHUNK), 0)
    for c in range(ROWS // CHUNK):
        rows = pl.ds(c * CHUNK, CHUNK)
        total = fast_tile(q[rows, :], mine[c * CHUNK : (c + 1) * CHUNK, :], lower)
        if c:
            total = total + fast_tile(q[rows, :], mine[: c * CHUNK, :])
        own[rows, :] = total
    for b in range(1, BRANCHES):
        size = PICKED[b]
        lower = iota((size, size), 1) <= iota((size, size), 0)
        own[ROWS + START[b] : ROWS + START[b] + size, :] = fast_tile(
            near[START[b] : START[b] + size, :], keys[b][0:size, :], lower
        )

    @pl.when(lax.rem(sm[1], 2) == 1)
    def _():
        for c in range(ROWS // CHUNK):
            rows = pl.ds(c * CHUNK, CHUNK)
            own[rows, :] += fast_tile(q[rows, :], other[...])
        for b in range(1, BRANCHES):
            size = PICKED[b]
            rows = pl.ds(ROWS + START[b], size)
            own[rows, :] += fast_tile(near[START[b] : START[b] + size, :], keys[b][size : 2 * size, :])


def second_kernel(sm, mine0, other0, mine, other, q, near, r1, r2, r4, r6, own_in, visiting, cross, own, *keys):
    del own_in
    keys = (None,) + keys
    visiting[0:384, :] = r1[0:384, :]
    visiting[384:576, :] = r1[384:576, :]
    visiting[576:768, :] = r2[0:192, :]
    visiting[768:960, :] = r2[288:480, :]
    visiting[960:1056, :] = r1[576:672, :]
    visiting[1056:1152, :] = r2[192:288, :]
    visiting[1152:1248, :] = r2[480:576, :]
    visiting[1248:1440, :] = r4[...]
    visiting[1440:1632, :] = r6[...]
    select_keys(sm, mine0, keys, 0)
    select_keys(sm, other0, keys, 1)
    add_cross(visiting, keys, cross, True)
    select_keys(sm, mine, keys, 0)
    select_keys(sm, other, keys, 1)
    add_cross(visiting, keys, cross, False)

    @pl.when(before(sm, 1))
    def _():
        add_own(q, near, (mine, other), keys, own)


def before(sm, stage):
    z = sm[1] // 2
    return jnp.bitwise_xor(z, stage) < z


def stage_kernel(stage, sm, mine, other, q, near, visiting, cross_in, own_in, cross, own, *keys):
    del cross_in, own_in
    keys = (None,) + keys
    select_keys(sm, mine, keys, 0)
    select_keys(sm, other, keys, 1)
    add_cross(visiting, keys, cross, False)

    @pl.when(before(sm, stage))
    def _():
        add_own(q, near, (mine, other), keys, own)


def last_cross_kernel(sm, *refs):
    kvs, refs = refs[:8], refs[8:]
    visiting, cross, refs = refs[0], refs[2], refs[3:]
    outs, refs = (None,) + refs[:7], refs[7:]
    keys, top, sums = (None,) + refs[:3], refs[3], (None,) + refs[4:11]
    select_keys(sm, kvs[6], keys, 0)
    select_keys(sm, kvs[7], keys, 1)
    add_cross(visiting, keys, cross, False)
    top[...] = jnp.zeros_like(top)

    @pl.when(jnp.logical_not(in_range(cross[:, HD:])))
    def _():
        cross[...] = jnp.zeros_like(cross)
        top[...] = jnp.full_like(top, NEG)
        for n in range(0, 8, 2):
            select_keys(sm, kvs[n], keys, 0)
            select_keys(sm, kvs[n + 1], keys, 1)
            for b in range(1, BRANCHES):

                def step(i, carry, b=b):
                    rows = pl.ds(pl.multiple_of(CROSS_START[b] + i * 96, 96), 96)
                    slow_tile(visiting[rows, :], keys[b], None, cross, top, rows)
                    return carry

                lax.fori_loop(0, CROSS[b] // 96, step, 0)

    for d in range(1, GROUPS):
        sums[d][...] = jnp.zeros_like(sums[d])
    for b in range(1, BRANCHES):
        for d in range(1, 1 << b):
            row = CROSS_START[b] + (d - 1) * PICKED[b]
            rows = slice(row, row + PICKED[b])
            total = cross[rows, HD:]
            at = START[b] - CUT[d]
            outs[d][at : at + PICKED[b], :] = (cross[rows, :HD] / total).astype(BF16)
            sums[d][at : at + PICKED[b], :] = top[rows, :] + jnp.log2(total)
    diagonal = iota((128, 128), 0) == iota((128, 128), 1)
    for d in range(1, GROUPS):
        rows, count, padded = message_rows(d)
        tail = jnp.zeros((padded - rows, 128), F32)
        place = iota(tail.shape, 0)
        for c in range(count):
            line = jnp.sum(jnp.where(diagonal, sums[d][c * 128 : (c + 1) * 128, :], 0.0), axis=0, keepdims=True)
            for n, piece in enumerate(split3(line)):
                tail = jnp.where(place == 3 * c + n, jnp.broadcast_to(piece.astype(F32), tail.shape), tail)
        outs[d][rows:padded, :] = tail.astype(BF16)


def last_own_kernel(sm, *refs):
    kvs, refs = refs[:8], refs[8:]
    q, near, own, out, log_sum, refs = refs[0], refs[1], refs[3], refs[4], refs[5], refs[6:]
    keys, top = (None,) + refs[:3], refs[3]
    lane = sm[1]

    @pl.when(before(sm, 3))
    def _():
        select_keys(sm, kvs[6], keys, 0)
        select_keys(sm, kvs[7], keys, 1)
        add_own(q, near, kvs[6:8], keys, own)

    top[...] = jnp.zeros_like(top)

    @pl.when(jnp.logical_not(in_range(own[:, HD:])))
    def _():
        own[...] = jnp.zeros_like(own)
        top[...] = jnp.full_like(top, NEG)
        for n in range(8):
            z = jnp.bitwise_xor(lane // 2, n // 2)
            block = 2 * z + (lax.rem(lane, 2) if n % 2 == 0 else 1 - lax.rem(lane, 2))

            @pl.when(block <= lane)
            def _(n=n, block=block):
                select_keys(sm, kvs[n], keys, 0)
                for b in range(BRANCHES):
                    size = ROWS >> b
                    source, key = (q, kvs[n]) if b == 0 else (near, keys[b])

                    def step(i, carry, b=b, size=size, source=source, key=key):
                        at = pl.multiple_of(START[b] + i * 96, 96)
                        rows = pl.ds(pl.multiple_of((ROWS if b else 0) + at, 96), 96)
                        row = iota((96, size), 0) + i * 96 + lane * size
                        col = iota((96, size), 1) + block * size
                        slow_tile(source[pl.ds(at, 96), :], key[0:size, :], col <= row, own, top, rows)
                        return carry

                    lax.fori_loop(0, size // 96, step, 0)

    total = own[:, HD:]
    out[...] = own[:, :HD] / total
    log_sum[...] = top[...] + jnp.log2(total)


def merge_kernel(sm, *refs):
    got, refs = (None,) + refs[:7], refs[7:]
    own_out, own_sum, merged, got_sums = refs[0], refs[1], refs[2], (None,) + refs[3:10]
    compact, compact_sum = refs[10], refs[11]
    group = sm[0]
    diagonal = iota((128, 128), 0) == iota((128, 128), 1)
    ones = jnp.ones((128, 128), BF16)
    for d in range(1, GROUPS):
        rows, count, _ = message_rows(d)
        for c in range(count):
            total = jnp.zeros((128, 128), F32)
            for n in range(3):
                line = got[d][rows + 3 * c + n : rows + 3 * c + n + 1, :]
                spread = jnp.where(diagonal, jnp.broadcast_to(line.astype(F32), (128, 128)), 0.0).astype(BF16)
                total = total + jnp.dot(spread, ones, preferred_element_type=F32)
            got_sums[d][c * 128 : (c + 1) * 128, :] = total
    for b in range(1, BRANCHES):
        own, first = PICKED[b], START[b]
        outs = [own_out[ROWS + first : ROWS + first + own, :]]
        logs = [own_sum[ROWS + first : ROWS + first + own, :]]
        for d in range(1, 1 << b):
            at = first - CUT[d]
            valid = jnp.bitwise_xor(group, d) < group
            outs.append(got[d][at : at + own, :].astype(F32))
            logs.append(jnp.where(valid, got_sums[d][at : at + own, :], NEG))
        best = logs[0]
        for log in logs[1:]:
            best = jnp.maximum(best, log)
        top = jnp.zeros_like(best)
        bottom = jnp.zeros_like(best)
        for out, log in zip(outs, logs):
            weight = jnp.exp2(log - best)
            top = top + weight * out
            bottom = bottom + weight
        compact[first : first + own, :] = top / bottom
        compact_sum[first : first + own, :] = best + jnp.log2(bottom)
    for c in range(ROWS // CHUNK):
        rows = slice(c * CHUNK, (c + 1) * CHUNK)
        outs = [own_out[rows, :]]
        logs = [own_sum[rows, :]]
        for b in range(1, BRANCHES):
            count, dilation = CHUNK >> b, 1 << b
            at = START[b] + c * count
            offset = sm[1 + b]
            place = jnp.where(
                iota((CHUNK, count), 0) == iota((CHUNK, count), 1) * dilation + offset, 1.0, 0.0
            ).astype(BF16)
            out_parts = split3(compact[at : at + count, :])
            log_parts = split3(compact_sum[at : at + count, :])
            first = jnp.concatenate([out_parts[0], log_parts[0]], axis=1)
            second = jnp.concatenate([out_parts[1], log_parts[1]], axis=1)
            spread = jnp.dot(place, first, preferred_element_type=F32)
            spread = spread + jnp.dot(place, second, preferred_element_type=F32)
            log = spread[:, HD:] + jnp.dot(place, log_parts[2], preferred_element_type=F32)
            chosen = lax.rem(iota((CHUNK, HD), 0), dilation) == offset
            outs.append(spread[:, :HD])
            logs.append(jnp.where(chosen, log, NEG))
        best = logs[0]
        for log in logs[1:]:
            best = jnp.maximum(best, log)
        top = jnp.zeros_like(best)
        bottom = jnp.zeros_like(best)
        for out, log in zip(outs, logs):
            weight = jnp.exp2(log - best)
            top = top + weight * out
            bottom = bottom + weight
        merged[rows, :] = (top / bottom).astype(BF16)


def call(kernel, name, sm, operands, outputs, scratch, flops, aliases=None):
    shapes = [jax.ShapeDtypeStruct(shape, dtype) for shape, dtype in outputs]
    moved = sum(math.prod(x.shape) * x.dtype.itemsize for x in list(operands) + shapes)
    return pl.pallas_call(
        kernel,
        name=name,
        out_shape=shapes,
        in_specs=[pl.BlockSpec(memory_space=pltpu.SMEM)]
        + [pl.BlockSpec(memory_space=pltpu.VMEM)] * len(operands),
        out_specs=[pl.BlockSpec(memory_space=pltpu.VMEM)] * len(shapes),
        scratch_shapes=[pltpu.VMEM(shape, dtype) for shape, dtype in scratch],
        input_output_aliases=aliases or {},
        compiler_params=pltpu.CompilerParams(vmem_limit_bytes=32 * 1024 * 1024),
        cost_estimate=pl.CostEstimate(flops=1, bytes_accessed=1, transcendentals=0),
    )(sm, *operands)


def pack(k, v):
    return pl.pallas_call(
        pack_kernel,
        name="pack",
        out_shape=jax.ShapeDtypeStruct((ROWS, 2 * HD), BF16),
        in_specs=[pl.BlockSpec(memory_space=pl.ANY)] * 2,
        out_specs=pl.BlockSpec(memory_space=pltpu.VMEM),
        scratch_shapes=[pltpu.SemaphoreType.DMA((2,))],
    )(k, v)


def place_of(index):
    x, z, core = index // 16, index // 2 % 8, index % 2
    return 2 * x + z // 4, z % 4, core


def index_of(group, z, core):
    return (group // 2 * 8 + group % 2 * 4 + z) * 2 + core


def partner(index, j):
    group, z, core = place_of(index)
    return index_of(group ^ j, z ^ 2 if j % 2 else z, core)


def meet(j):
    return [(index, partner(index, j)) for index in range(64)]


def to_later(j):
    return [(index, other) for index, other in meet(j) if place_of(other)[0] > place_of(index)[0]]


def exchange(step):
    pairs = []
    for index in range(64):
        group, z, core = place_of(index)
        pairs.append((index, index_of(group, z ^ step, core)))
    return pairs


def on_device(queries, key_rows, values, offsets):
    seq, head = lax.axis_index("seq"), lax.axis_index("head")
    mine = lax.dynamic_slice_in_dim(offsets, head, 1, axis=1)[:, 0]
    sm = jnp.concatenate([jnp.stack([seq // 8, seq % 8]).astype(jnp.int32), mine[1:], jnp.zeros((3,), jnp.int32)])
    kv = pack(key_rows, values)
    queries, kv = lax.optimization_barrier((queries, kv))
    (near,) = call(
        pick_kernel, "pick_queries", sm, [queries], [((TOTAL, HD), BF16)], [], 2 * 672 * 256 * 128
    )
    pair = [(i, i ^ 1) for i in range(64)]
    keys = [((ROWS, 2 * HD), BF16), ((384, 2 * HD), BF16), ((192, 2 * HD), BF16)]
    state = [((VISITING, 2 * HD), F32), ((ROWS + TOTAL, 2 * HD), F32)]
    work = 4 * HD * 2 * ROWS * 2 * ROWS
    r1 = lax.ppermute(near, "seq", meet(1))
    block2 = lax.ppermute(kv, "seq", exchange(2))
    block1 = lax.ppermute(kv, "seq", exchange(1))
    kvs = [kv, lax.ppermute(kv, "seq", pair)]
    r2 = lax.ppermute(jnp.concatenate([near[384:], r1[384:]]), "seq", meet(2))
    (own,) = call(first_kernel, "own_chip", sm, kvs + [queries, near], state[1:], keys, work // 2)
    pair3 = jnp.concatenate([near[576:], r1[576:]])
    r4 = lax.ppermute(pair3, "seq", meet(4))
    r6 = lax.ppermute(pair3, "seq", meet(6))
    block2, r2, r4, r6, own = lax.optimization_barrier((block2, r2, r4, r6, own))
    block3 = lax.ppermute(block2, "seq", exchange(1))
    block1, own = lax.optimization_barrier((block1, own))
    kvs += [block1, lax.ppermute(block1, "seq", pair)]
    kvs += [block2, lax.ppermute(block2, "seq", pair)]
    kvs[5], own = lax.optimization_barrier((kvs[5], own))
    visiting, cross, own = call(
        second_kernel,
        "chip_1",
        sm,
        kvs[:4] + [queries, near, r1, r2, r4, r6, own],
        [((VISITING, HD), BF16)] + state,
        keys,
        work,
        {11: 2},
    )
    cross, own = call(
        functools.partial(stage_kernel, 2),
        "chip_2",
        sm,
        kvs[4:] + [queries, near, visiting, cross, own],
        state,
        keys,
        work,
        {6: 0, 7: 1},
    )
    block3, own = lax.optimization_barrier((block3, own))
    kvs += [block3, lax.ppermute(block3, "seq", pair)]
    crossed = call(
        last_cross_kernel,
        "cross_end",
        sm,
        kvs + [visiting, cross],
        state[:1] + [((message_rows(d)[2], HD), BF16) for d in range(1, GROUPS)],
        keys + [((VISITING, HD), F32)] + [((message_rows(d)[1] * 128, 128), F32) for d in range(1, GROUPS)],
        work // 2,
        {10: 0},
    )
    back = [
        lax.ppermute(crossed[d], "seq", to_later(d)) for d in range(1, GROUPS)
    ]
    _, out, log_sum = call(
        last_own_kernel,
        "own_end",
        sm,
        kvs + [queries, near, own],
        state[1:] + [((ROWS + TOTAL, HD), F32)] * 2,
        keys + [((ROWS + TOTAL, HD), F32)],
        work // 2,
        {11: 0},
    )
    (merged,) = call(
        merge_kernel,
        "merge",
        sm,
        back + [out, log_sum],
        [((ROWS, HD), BF16)],
        [((message_rows(d)[1] * 128, 128), F32) for d in range(1, GROUPS)] + [((TOTAL, HD), F32)] * 2,
        1000000,
    )
    return lax.all_to_all(merged, "head", split_axis=0, concat_axis=1, tiled=True)


def solution(mesh):
    placed = (P("seq", "head"), P("seq", "head"), P("seq", "head"), P())
    return jax.shard_map(
        on_device, mesh=mesh, in_specs=placed, out_specs=P(("seq", "head"), None), check_vma=False
    )
```

time: 211 us -> 205 us (0.972)
  the two profiles are of different devices: /device:TPU:192 before, /device:TPU:193 now
where the time goes in v2:
time: 205 us; the launch traced here: 204 us
  Pallas kernels  92.7 us (45%)
  starting transfers between devices  55.2 us (27%)
  blocking collectives  48 us (23%)
  waiting for transfers between devices  4.25 us (2%)
  local copies, waits for them, and re-layouts  3.51 us (2%)
    pallas_call x7, Pallas kernels, call(): pl.pallas_call(kernel, name=name, out_shape=shapes, in_specs=[pl.BlockSpe...  90.9 us
    all_to_all x1, blocking collectives, on_device(): lax.all_to_all(merged, 'head', split_axis=0, concat_axis=1, tiled=True)  48 us
    ppermute x7, starting transfers between devices, on_device(): lax.ppermute(crossed[d], 'seq', to_later(d))  20.7 us
    ppermute x1, starting transfers between devices, on_device(): r1 = lax.ppermute(near, 'seq', meet(1))  6.12 us
  transfers between devices with their start and end apart: 18, of which 3 were waited for; matrix products, arithmetic and copies ran while one was open for 0% of the time, Pallas kernels for 42%

profile of v2, /device:TPU:193, one launch (start us, length us, event | category | flops | bytes accessed | tf_op | source)
XLA Modules:
  0.0 204.2 jit_solution(11027144387089230573)
XLA Ops:
  0.0 0.7 copy-done
  0.7 0.1 constant_dynamic-slice_fusion
  0.8 0.1 slice_reduce_fusion
  0.9 1.8 pack.1.mine.mine0.refs_0_
  2.7 0.1 pad_add_fusion.sm
  2.8 0.9 copy-done.3
  3.7 0.8 pick_queries.1.near.refs_9_
  4.5 6.1 %collective-permute-start.3 = (bf16[672,128]{1,0:T(8,128)(2,1)S(1)}, bf16[672,128]{1,0:T(8,128)(2,1)S(1)}, u32[]{:S(2)}, u32[]{:S(2)}) collective-permute-start(bf16[672,128]{1,0:T(8,128)(2,1)S(1)} %pick_queries.1.near.refs_9_), channel_id=1, source_target_pairs={{0,96},{8,104},{16,112},{24,120},{32,64},{40,72},{48,80},{56,88},{... | collective-permute-start | bytes 516104 | tf_op jit(solution)/shard_map/ppermute | solution.py:451
  10.6 2.9 %collective-permute-start = (bf16[768,256]{1,0:T(8,128)(2,1)}, bf16[768,256]{1,0:T(8,128)(2,1)S(1)}, u32[]{:S(2)}, u32[]{:S(2)}) collective-permute-start(bf16[768,256]{1,0:T(8,128)(2,1)} %pack.1.mine.mine0.refs_0_), channel_id=1, source_target_pairs={{0,8},{8,0},{16,24},{24,16},{32,40},{40,32},{48,56},{56,48},{64,72... | collective-permute-start | bytes 1179656 | tf_op jit(solution)/shard_map/ppermute | solution.py:454
  13.5 4.0 %collective-permute-start.2 = (bf16[768,256]{1,0:T(8,128)(2,1)}, bf16[768,256]{1,0:T(8,128)(2,1)S(1)}, u32[]{:S(2)}, u32[]{:S(2)}) collective-permute-start(bf16[768,256]{1,0:T(8,128)(2,1)} %pack.1.mine.mine0.refs_0_), channel_id=1, source_target_pairs={{0,32},{8,40},{16,48},{24,56},{32,0},{40,8},{48,16},{56,24},{64,96... | collective-permute-start | bytes 1179656 | tf_op jit(solution)/shard_map/ppermute | solution.py:452
  17.5 2.2 %collective-permute-start.1 = (bf16[768,256]{1,0:T(8,128)(2,1)}, bf16[768,256]{1,0:T(8,128)(2,1)S(1)}, u32[]{:S(2)}, u32[]{:S(2)}) collective-permute-start(bf16[768,256]{1,0:T(8,128)(2,1)} %pack.1.mine.mine0.refs_0_), channel_id=1, source_target_pairs={{0,16},{8,24},{16,0},{24,8},{32,48},{40,56},{48,32},{56,40},{64,80... | collective-permute-start | bytes 1179656 | tf_op jit(solution)/shard_map/ppermute | solution.py:453
  19.7 0.0 collective-permute-done.3.r1
  19.8 3.1 %collective-permute-start.4 = (bf16[576,128]{1,0:T(8,128)(2,1)S(1)}, bf16[576,128]{1,0:T(8,128)(2,1)S(1)}, u32[]{:S(2)}, u32[]{:S(2)}) collective-permute-start(bf16[576,128]{1,0:T(8,128)(2,1)S(1)} %pad_maximum_fusion), channel_id=1, source_target_pairs={{0,128},{8,136},{16,144},{24,152},{32,160},{40,168},{48,176},{56,1... | collective-permute-start | bytes 442376 | tf_op jit(solution)/shard_map/ppermute | solution.py:455
  22.9 3.7 %collective-permute-start.6 = (bf16[192,128]{1,0:T(8,128)(2,1)S(1)}, bf16[192,128]{1,0:T(8,128)(2,1)S(1)}, u32[]{:S(2)}, u32[]{:S(2)}) collective-permute-start(bf16[192,128]{1,0:T(8,128)(2,1)S(1)} %pad_maximum_fusion.1), channel_id=1, source_target_pairs={{0,384},{8,392},{16,400},{24,408},{32,416},{40,424},{48,432},{56,4... | collective-permute-start | bytes 147464 | tf_op jit(solution)/shard_map/ppermute | solution.py:459
  26.6 0.0 collective-permute-done.other.other0.refs_1_
  26.7 2.6 %collective-permute-start.5 = (bf16[192,128]{1,0:T(8,128)(2,1)S(1)}, bf16[192,128]{1,0:T(8,128)(2,1)S(1)}, u32[]{:S(2)}, u32[]{:S(2)}) collective-permute-start(bf16[192,128]{1,0:T(8,128)(2,1)S(1)} %pad_maximum_fusion.1), channel_id=1, source_target_pairs={{0,256},{8,264},{16,272},{24,280},{32,288},{40,296},{48,304},{56,3... | collective-permute-start | bytes 147464 | tf_op jit(solution)/shard_map/ppermute | solution.py:458
  29.2 1.0 copy-done.1
  30.2 3.4 %own_chip.1.own_in = f32[1440,256]{1,0:T(8,128)S(1)} custom-call(s32[8]{0:T(128)S(1)} %pad_add_fusion.sm, bf16[768,256]{1,0:T(8,128)(2,1)S(1)} %copy-done.1, bf16[768,256]{1,0:T(8,128)(2,1)S(1)} %collective-permute-done.other.other0.refs_1_, bf16[768,128]{1,0:T(8,128)(2,1)S(1)} %copy-done.4, bf16[672,128]{1,0:T(8,128)(2,1)S(1)} %pick_queries.1.near.refs_9_), custom_call_target="tpu_custom_call" | custom-call | flops 1 | bytes 1 | tf_op jit(solution)/shard_map/own_chip/pallas_call | solution.py:383
  33.7 0.0 collective-permute-done.6.r6
  33.7 0.0 collective-permute-done.4.r2
  33.7 2.0 collective-permute-done.2.mine.refs_4_
  35.7 2.7 %collective-permute-start.8 = (bf16[768,256]{1,0:T(8,128)(2,1)S(1)}, bf16[768,256]{1,0:T(8,128)(2,1)S(1)}, u32[]{:S(2)}, u32[]{:S(2)}) collective-permute-start(bf16[768,256]{1,0:T(8,128)(2,1)S(1)} %collective-permute-done.2.mine.refs_4_), channel_id=1, source_target_pairs={{0,8},{8,0},{16,24},{24,16},{32,40},{40,32},{48,56},{56,48},{64,72... | collective-permute-start | bytes 1179656 | tf_op jit(solution)/shard_map/ppermute | solution.py:464
  38.4 0.0 collective-permute-done.1.mine.refs_2_
  38.5 1.9 collective-permute-start.7
  40.4 1.9 collective-permute-start.9
  42.3 0.0 collective-permute-done.7.other.refs_3_
  42.3 5.1 %chip_1.1 = (bf16[1632,128]{1,0:T(8,128)(2,1)S(1)}, f32[1632,256]{1,0:T(8,128)S(1)}, f32[1440,256]{1,0:T(8,128)S(1)}) custom-call(s32[8]{0:T(128)S(1)} %pad_add_fusion.sm, bf16[768,256]{1,0:T(8,128)(2,1)S(1)} %copy-done.1, bf16[768,256]{1,0:T(8,128)(2,1)S(1)} %collective-permute-done.other.other0.refs_1_, ...), custom_call_target="tpu_custom_call", output_to_operand_aliasing={{2}: (11, {})} | custom-call | flops 1 | bytes 1 | tf_op jit(solution)/shard_map/chip_1/pallas_call | solution.py:383
  47.5 3.9 %chip_2.1 = (f32[1632,256]{1,0:T(8,128)S(1)}, f32[1440,256]{1,0:T(8,128)S(1)}) custom-call(s32[8]{0:T(128)S(1)} %pad_add_fusion.sm, bf16[768,256]{1,0:T(8,128)(2,1)S(1)} %collective-permute-done.2.mine.refs_4_, bf16[768,256]{1,0:T(8,128)(2,1)S(1)} %collective-permute-done.8.other.refs_5_, ...), custom_call_target="tpu_custom_call", output_to_operand_aliasing={{0}: (6, {}), {1}: (7, {})} | custom-call | flops 1 | bytes 1 | tf_op jit(solution)/shard_map/chip_2/pallas_call | solution.py:383
  51.4 1.0 collective-permute-done.9.refs_6_
  52.5 3.4 %collective-permute-start.10 = (bf16[768,256]{1,0:T(8,128)(2,1)S(1)}, bf16[768,256]{1,0:T(8,128)(2,1)S(1)}, u32[]{:S(2)}, u32[]{:S(2)}) collective-permute-start(bf16[768,256]{1,0:T(8,128)(2,1)S(1)} %collective-permute-done.9.refs_6_), channel_id=1, source_target_pairs={{0,8},{8,0},{16,24},{24,16},{32,40},{40,32},{48,56},{56,48},{64,72... | collective-permute-start | bytes 1179656 | tf_op jit(solution)/shard_map/ppermute | solution.py:487
  55.9 1.1 collective-permute-done.10.refs_7_
  57.0 2.3 %cross_end.1 = (f32[1632,256]{1,0:T(8,128)S(1)}, bf16[704,128]{1,0:T(8,128)(2,1)S(1)}, bf16[304,128]{1,0:T(8,128)(2,1)S(1)}, bf16[304,128]{1,0:T(8,128)(2,1)S(1)...) custom-call(s32[8]{0:T(128)S(1)} %pad_add_fusion.sm, ...), custom_call_target="tpu_custom_call", output_to_operand_aliasing={{0}: (10, {})} | custom-call | flops 1 | bytes 1 | tf_op jit(solution)/shard_map/cross_end/pallas_call | solution.py:383
  59.4 3.6 %collective-permute-start.11 = (bf16[704,128]{1,0:T(8,128)(2,1)S(1)}, bf16[704,128]{1,0:T(8,128)(2,1)S(1)}, u32[]{:S(2)}, u32[]{:S(2)}) collective-permute-start(bf16[704,128]{1,0:T(8,128)(2,1)S(1)} %get-tuple-element.49), channel_id=1, source_target_pairs={{0,96},{8,104},{16,112},{24,120},{32,64},{40,72},{48,80},{56,88},{... | collective-permute-start | bytes 540680 | tf_op jit(solution)/shard_map/ppermute | solution.py:499
  63.0 2.8 %collective-permute-start.12 = (bf16[304,128]{1,0:T(8,128)(2,1)S(1)}, bf16[304,128]{1,0:T(8,128)(2,1)S(1)}, u32[]{:S(2)}, u32[]{:S(2)}) collective-permute-start(bf16[304,128]{1,0:T(8,128)(2,1)S(1)} %get-tuple-element.50), channel_id=1, source_target_pairs={{0,128},{8,136},{16,144},{24,152},{32,160},{40,168},{48,176},{56,1... | collective-permute-start | bytes 233480 | tf_op jit(solution)/shard_map/ppermute | solution.py:499
  65.8 1.3 collective-permute-start.13
  67.1 4.4 %collective-permute-start.14 = (bf16[112,128]{1,0:T(8,128)(2,1)S(1)}, bf16[112,128]{1,0:T(8,128)(2,1)S(1)}, u32[]{:S(2)}, u32[]{:S(2)}) collective-permute-start(bf16[112,128]{1,0:T(8,128)(2,1)S(1)} %get-tuple-element.52), channel_id=1, source_target_pairs={{0,256},{8,264},{16,272},{24,280},{32,288},{40,296},{48,304},{56,3... | collective-permute-start | bytes 86024 | tf_op jit(solution)/shard_map/ppermute | solution.py:499
  71.4 4.3 %collective-permute-start.15 = (bf16[112,128]{1,0:T(8,128)(2,1)S(1)}, bf16[112,128]{1,0:T(8,128)(2,1)S(1)}, u32[]{:S(2)}, u32[]{:S(2)}) collective-permute-start(bf16[112,128]{1,0:T(8,128)(2,1)S(1)} %get-tuple-element.53), channel_id=1, source_target_pairs={{0,352},{8,360},{16,368},{24,376},{32,320},{40,328},{48,336},{56,3... | collective-permute-start | bytes 86024 | tf_op jit(solution)/shard_map/ppermute | solution.py:499
  75.7 0.0 collective-permute-done.14.refs_3_
  75.7 1.3 collective-permute-start.16
  77.0 0.0 collective-permute-done.15.refs_4_
  77.1 3.1 %collective-permute-start.17 = (bf16[112,128]{1,0:T(8,128)(2,1)S(1)}, bf16[112,128]{1,0:T(8,128)(2,1)S(1)}, u32[]{:S(2)}, u32[]{:S(2)}) collective-permute-start(bf16[112,128]{1,0:T(8,128)(2,1)S(1)} %get-tuple-element.55), channel_id=1, source_target_pairs={{0,480},{8,488},{16,496},{24,504},{32,448},{40,456},{48,464},{56,4... | collective-permute-start | bytes 86024 | tf_op jit(solution)/shard_map/ppermute | solution.py:499
  80.1 73.2 %own_end.1 = (f32[1440,256]{1,0:T(8,128)S(1)}, f32[1440,128]{1,0:T(8,128)S(1)}, f32[1440,128]{1,0:T(8,128)S(1)}) custom-call(s32[8]{0:T(128)S(1)} %pad_add_fusion.sm, bf16[768,256]{1,0:T(8,128)(2,1)S(1)} %copy-done.2, bf16[768,256]{1,0:T(8,128)(2,1)S(1)} %collective-permute-done.other.other0.refs_1_, ...), custom_call_target="tpu_custom_call", output_to_operand_aliasing={{0}: (11, {})} | custom-call | flops 1 | bytes 1 | tf_op jit(solution)/shard_map/own_end/pallas_call | solution.py:383
  153.3 0.0 collective-permute-done.16.refs_5_
  153.3 0.0 collective-permute-done.17.refs_6_
  153.4 0.0 collective-permute-done.11.refs_0_
  153.4 2.1 %merge.1 = bf16[768,128]{1,0:T(8,128)(2,1)S(1)} custom-call(s32[8]{0:T(128)S(1)} %pad_add_fusion.sm, bf16[704,128]{1,0:T(8,128)(2,1)S(1)} %collective-permute-done.11.refs_0_, bf16[304,128]{1,0:T(8,128)(2,1)S(1)} %collective-permute-done.12.refs_1_, bf16[304,128]{1,0:T(8,128)(2,1)S(1)} %collective-permute-done.13.refs_2_, ...), custom_call_target="tpu_custom_call" | custom-call | flops 1 | bytes 1 | tf_op jit(solution)/shard_map/merge/pallas_call | solution.py:383
  155.5 48.0 %all_to_all.19 = bf16[8,96,128]{2,1,0:T(8,128)(2,1)S(1)} all-to-all(bf16[8,96,128]{2,1,0:T(8,128)(2,1)S(1)} %bitcast.9), channel_id=1, replica_groups=mesh['seq'=64,'head'=8] {'head'}, dimensions={0} | all-to-all | bytes 393216 | tf_op jit(solution)/shard_map/all_to_all | solution.py:520
  203.5 0.7 copy_bitcast_fusion
  (18 shorter events, 0.1 us)
Async XLA Ops:
  0.0 0.7 copy-start
  0.0 29.2 %copy-start.4 = (bf16[768,128]{1,0:T(8,128)(2,1)S(1)}, bf16[768,128]{1,0:T(8,128)(2,1)}, u32[]{:S(2)}) copy-start(bf16[768,128]{1,0:T(8,128)(2,1)} %refs_8_) | copy-start | bytes 589828
  2.8 0.9 copy-start.3
  4.5 15.2 %collective-permute-start.3 = (bf16[672,128]{1,0:T(8,128)(2,1)S(1)}, bf16[672,128]{1,0:T(8,128)(2,1)S(1)}, u32[]{:S(2)}, u32[]{:S(2)}) collective-permute-start(bf16[672,128]{1,0:T(8,128)(2,1)S(1)} %pick_queries.1.near.refs_9_), channel_id=1, source_target_pairs={{0,96},{8,104},{16,112},{24,120},{32,64},{40,72},{48,80},{56,88},{... | collective-permute-start | bytes 516104 | tf_op jit(solution)/shard_map/ppermute | solution.py:451
  10.6 16.0 %collective-permute-start = (bf16[768,256]{1,0:T(8,128)(2,1)}, bf16[768,256]{1,0:T(8,128)(2,1)S(1)}, u32[]{:S(2)}, u32[]{:S(2)}) collective-permute-start(bf16[768,256]{1,0:T(8,128)(2,1)} %pack.1.mine.mine0.refs_0_), channel_id=1, source_target_pairs={{0,8},{8,0},{16,24},{24,16},{32,40},{40,32},{48,56},{56,48},{64,72... | collective-permute-start | bytes 1179656 | tf_op jit(solution)/shard_map/ppermute | solution.py:454
  13.5 22.3 %collective-permute-start.2 = (bf16[768,256]{1,0:T(8,128)(2,1)}, bf16[768,256]{1,0:T(8,128)(2,1)S(1)}, u32[]{:S(2)}, u32[]{:S(2)}) collective-permute-start(bf16[768,256]{1,0:T(8,128)(2,1)} %pack.1.mine.mine0.refs_0_), channel_id=1, source_target_pairs={{0,32},{8,40},{16,48},{24,56},{32,0},{40,8},{48,16},{56,24},{64,96... | collective-permute-start | bytes 1179656 | tf_op jit(solution)/shard_map/ppermute | solution.py:452
  17.5 21.0 %collective-permute-start.1 = (bf16[768,256]{1,0:T(8,128)(2,1)}, bf16[768,256]{1,0:T(8,128)(2,1)S(1)}, u32[]{:S(2)}, u32[]{:S(2)}) collective-permute-start(bf16[768,256]{1,0:T(8,128)(2,1)} %pack.1.mine.mine0.refs_0_), channel_id=1, source_target_pairs={{0,16},{8,24},{16,0},{24,8},{32,48},{40,56},{48,32},{56,40},{64,80... | collective-permute-start | bytes 1179656 | tf_op jit(solution)/shard_map/ppermute | solution.py:453
  19.8 13.9 %collective-permute-start.4 = (bf16[576,128]{1,0:T(8,128)(2,1)S(1)}, bf16[576,128]{1,0:T(8,128)(2,1)S(1)}, u32[]{:S(2)}, u32[]{:S(2)}) collective-permute-start(bf16[576,128]{1,0:T(8,128)(2,1)S(1)} %pad_maximum_fusion), channel_id=1, source_target_pairs={{0,128},{8,136},{16,144},{24,152},{32,160},{40,168},{48,176},{56,1... | collective-permute-start | bytes 442376 | tf_op jit(solution)/shard_map/ppermute | solution.py:455
  22.9 10.8 %collective-permute-start.6 = (bf16[192,128]{1,0:T(8,128)(2,1)S(1)}, bf16[192,128]{1,0:T(8,128)(2,1)S(1)}, u32[]{:S(2)}, u32[]{:S(2)}) collective-permute-start(bf16[192,128]{1,0:T(8,128)(2,1)S(1)} %pad_maximum_fusion.1), channel_id=1, source_target_pairs={{0,384},{8,392},{16,400},{24,408},{32,416},{40,424},{48,432},{56,4... | collective-permute-start | bytes 147464 | tf_op jit(solution)/shard_map/ppermute | solution.py:459
  26.7 7.0 %collective-permute-start.5 = (bf16[192,128]{1,0:T(8,128)(2,1)S(1)}, bf16[192,128]{1,0:T(8,128)(2,1)S(1)}, u32[]{:S(2)}, u32[]{:S(2)}) collective-permute-start(bf16[192,128]{1,0:T(8,128)(2,1)S(1)} %pad_maximum_fusion.1), channel_id=1, source_target_pairs={{0,256},{8,264},{16,272},{24,280},{32,288},{40,296},{48,304},{56,3... | collective-permute-start | bytes 147464 | tf_op jit(solution)/shard_map/ppermute | solution.py:458
  29.2 1.0 copy-start.1
  35.7 6.6 %collective-permute-start.8 = (bf16[768,256]{1,0:T(8,128)(2,1)S(1)}, bf16[768,256]{1,0:T(8,128)(2,1)S(1)}, u32[]{:S(2)}, u32[]{:S(2)}) collective-permute-start(bf16[768,256]{1,0:T(8,128)(2,1)S(1)} %collective-permute-done.2.mine.refs_4_), channel_id=1, source_target_pairs={{0,8},{8,0},{16,24},{24,16},{32,40},{40,32},{48,56},{56,48},{64,72... | collective-permute-start | bytes 1179656 | tf_op jit(solution)/shard_map/ppermute | solution.py:464
  38.5 3.9 %collective-permute-start.7 = (bf16[768,256]{1,0:T(8,128)(2,1)S(1)}, bf16[768,256]{1,0:T(8,128)(2,1)S(1)}, u32[]{:S(2)}, u32[]{:S(2)}) collective-permute-start(bf16[768,256]{1,0:T(8,128)(2,1)S(1)} %collective-permute-done.1.mine.refs_2_), channel_id=1, source_target_pairs={{0,8},{8,0},{16,24},{24,16},{32,40},{40,32},{48,56},{56,48},{64,72... | collective-permute-start | bytes 1179656 | tf_op jit(solution)/shard_map/ppermute | solution.py:463
  40.4 12.1 %collective-permute-start.9 = (bf16[768,256]{1,0:T(8,128)(2,1)S(1)}, bf16[768,256]{1,0:T(8,128)(2,1)S(1)}, u32[]{:S(2)}, u32[]{:S(2)}) collective-permute-start(bf16[768,256]{1,0:T(8,128)(2,1)S(1)} %collective-permute-done.2.mine.refs_4_), channel_id=1, source_target_pairs={{0,16},{8,24},{16,0},{24,8},{32,48},{40,56},{48,32},{56,40},{64,80... | collective-permute-start | bytes 1179656 | tf_op jit(solution)/shard_map/ppermute | solution.py:461
  47.5 9.6 %copy-start.2 = (bf16[768,256]{1,0:T(8,128)(2,1)S(1)}, bf16[768,256]{1,0:T(8,128)(2,1)}, u32[]{:S(2)}) copy-start(bf16[768,256]{1,0:T(8,128)(2,1)} %pack.1.mine.mine0.refs_0_) | copy-start | bytes 1179652
  52.5 4.6 %collective-permute-start.10 = (bf16[768,256]{1,0:T(8,128)(2,1)S(1)}, bf16[768,256]{1,0:T(8,128)(2,1)S(1)}, u32[]{:S(2)}, u32[]{:S(2)}) collective-permute-start(bf16[768,256]{1,0:T(8,128)(2,1)S(1)} %collective-permute-done.9.refs_6_), channel_id=1, source_target_pairs={{0,8},{8,0},{16,24},{24,16},{32,40},{40,32},{48,56},{56,48},{64,72... | collective-permute-start | bytes 1179656 | tf_op jit(solution)/shard_map/ppermute | solution.py:487
  59.4 94.0 %collective-permute-start.11 = (bf16[704,128]{1,0:T(8,128)(2,1)S(1)}, bf16[704,128]{1,0:T(8,128)(2,1)S(1)}, u32[]{:S(2)}, u32[]{:S(2)}) collective-permute-start(bf16[704,128]{1,0:T(8,128)(2,1)S(1)} %get-tuple-element.49), channel_id=1, source_target_pairs={{0,96},{8,104},{16,112},{24,120},{32,64},{40,72},{48,80},{56,88},{... | collective-permute-start | bytes 540680 | tf_op jit(solution)/shard_map/ppermute | solution.py:499
  63.0 90.4 %collective-permute-start.12 = (bf16[304,128]{1,0:T(8,128)(2,1)S(1)}, bf16[304,128]{1,0:T(8,128)(2,1)S(1)}, u32[]{:S(2)}, u32[]{:S(2)}) collective-permute-start(bf16[304,128]{1,0:T(8,128)(2,1)S(1)} %get-tuple-element.50), channel_id=1, source_target_pairs={{0,128},{8,136},{16,144},{24,152},{32,160},{40,168},{48,176},{56,1... | collective-permute-start | bytes 233480 | tf_op jit(solution)/shard_map/ppermute | solution.py:499
  65.8 87.6 %collective-permute-start.13 = (bf16[304,128]{1,0:T(8,128)(2,1)S(1)}, bf16[304,128]{1,0:T(8,128)(2,1)S(1)}, u32[]{:S(2)}, u32[]{:S(2)}) collective-permute-start(bf16[304,128]{1,0:T(8,128)(2,1)S(1)} %get-tuple-element.51), channel_id=1, source_target_pairs={{0,224},{8,232},{16,240},{24,248},{32,192},{40,200},{48,208},{56,2... | collective-permute-start | bytes 233480 | tf_op jit(solution)/shard_map/ppermute | solution.py:499
  67.1 8.7 %collective-permute-start.14 = (bf16[112,128]{1,0:T(8,128)(2,1)S(1)}, bf16[112,128]{1,0:T(8,128)(2,1)S(1)}, u32[]{:S(2)}, u32[]{:S(2)}) collective-permute-start(bf16[112,128]{1,0:T(8,128)(2,1)S(1)} %get-tuple-element.52), channel_id=1, source_target_pairs={{0,256},{8,264},{16,272},{24,280},{32,288},{40,296},{48,304},{56,3... | collective-permute-start | bytes 86024 | tf_op jit(solution)/shard_map/ppermute | solution.py:499
  71.4 5.6 %collective-permute-start.15 = (bf16[112,128]{1,0:T(8,128)(2,1)S(1)}, bf16[112,128]{1,0:T(8,128)(2,1)S(1)}, u32[]{:S(2)}, u32[]{:S(2)}) collective-permute-start(bf16[112,128]{1,0:T(8,128)(2,1)S(1)} %get-tuple-element.53), channel_id=1, source_target_pairs={{0,352},{8,360},{16,368},{24,376},{32,320},{40,328},{48,336},{56,3... | collective-permute-start | bytes 86024 | tf_op jit(solution)/shard_map/ppermute | solution.py:499
  75.7 77.6 %collective-permute-start.16 = (bf16[112,128]{1,0:T(8,128)(2,1)S(1)}, bf16[112,128]{1,0:T(8,128)(2,1)S(1)}, u32[]{:S(2)}, u32[]{:S(2)}) collective-permute-start(bf16[112,128]{1,0:T(8,128)(2,1)S(1)} %get-tuple-element.54), channel_id=1, source_target_pairs={{0,384},{8,392},{16,400},{24,408},{32,416},{40,424},{48,432},{56,4... | collective-permute-start | bytes 86024 | tf_op jit(solution)/shard_map/ppermute | solution.py:499
  77.1 76.3 %collective-permute-start.17 = (bf16[112,128]{1,0:T(8,128)(2,1)S(1)}, bf16[112,128]{1,0:T(8,128)(2,1)S(1)}, u32[]{:S(2)}, u32[]{:S(2)}) collective-permute-start(bf16[112,128]{1,0:T(8,128)(2,1)S(1)} %get-tuple-element.55), channel_id=1, source_target_pairs={{0,480},{8,488},{16,496},{24,504},{32,448},{40,456},{48,464},{56,4... | collective-permute-start | bytes 86024 | tf_op jit(solution)/shard_map/ppermute | solution.py:499

commit v3 on v2

--- a/solution.py
+++ b/solution.py
@@ -20,6 +20,7 @@
 CROSS = (0, 384, 576, 672)
 CROSS_START = (0, 0, 384, 960)
 VISITING = 1632
+CROSS_STEP = (0, 192, 192, 224)
 CUT = (0, 0, 384, 384, 576, 576, 576, 576)
 SCALE = math.log2(math.e) / math.sqrt(HD)
 NEG = -1e30
@@ -61,34 +62,38 @@
     return high, mid, (rest - mid.astype(F32)).astype(BF16)
 
 
-def pack_kernel(k, v, kv, sems):
+def pack_kernel(sm, q, k, v, near, kv, q_here, sems):
     copies = [
-        pltpu.make_async_copy(k, kv.at[:, pl.ds(0, HD)], sems.at[0]),
-        pltpu.make_async_copy(v, kv.at[:, pl.ds(HD, HD)], sems.at[1]),
+        pltpu.make_async_copy(q, q_here, sems.at[0]),
+        pltpu.make_async_copy(k, kv.at[:, pl.ds(0, HD)], sems.at[1]),
+        pltpu.make_async_copy(v, kv.at[:, pl.ds(HD, HD)], sems.at[2]),
     ]
     for copy in copies:
         copy.start()
-    for copy in copies:
-        copy.wait()
-
-
-def pick_kernel(sm, q, near):
     pick = pick_matrix(sm)
+    copies[0].wait()
     for c in range(ROWS // CHUNK):
-        got = jnp.dot(pick, q[c * CHUNK : (c + 1) * CHUNK, :], preferred_element_type=F32).astype(BF16)
+        got = jnp.dot(pick, q_here[c * CHUNK : (c + 1) * CHUNK, :], preferred_element_type=F32).astype(BF16)
         for b in range(1, BRANCHES):
             count = CHUNK >> b
             at = CHUNK - (CHUNK >> (b - 1))
-            piece = got[at : at + count, :]
             row = START[b] + c * count
-            near[row : row + count, :] = piece
+            near[row : row + count, :] = got[at : at + count, :]
+    copies[1].wait()
+    copies[2].wait()
 
 
 def fast_tile(q, kv, allowed=None):
-    p = jnp.exp2(dot_t(q, kv[:, :HD]) * SCALE)
-    if allowed is not None:
-        p = jnp.where(allowed, p, 0.0)
-    return jnp.dot(p.astype(BF16), with_ones(kv[:, HD:]), preferred_element_type=F32)
+    total = None
+    step = CHUNK if allowed is None and kv.shape[0] % CHUNK == 0 else kv.shape[0]
+    for at in range(0, kv.shape[0], step):
+        part = kv[at : at + step, :]
+        p = jnp.exp2(dot_t(q, part[:, :HD]) * SCALE)
+        if allowed is not None:
+            p = jnp.where(allowed, p, 0.0)
+        added = jnp.dot(p.astype(BF16), with_ones(part[:, HD:]), preferred_element_type=F32)
+        total = added if total is None else total + added
+    return total
 
 
 def slow_tile(q, kv, allowed, acc, top, rows):
@@ -110,74 +115,46 @@
     return (jnp.min(total) >= LOW) & (jnp.max(total) <= HIGH)
 
 
-def select_keys(sm, kv, keys, part):
+def select_keys(sm, pair, keys, part):
     pick = pick_matrix(sm)
-    for c in range(ROWS // CHUNK):
-        got = jnp.dot(pick, kv[c * CHUNK : (c + 1) * CHUNK, :], preferred_element_type=F32).astype(BF16)
+    for c in range(2 * ROWS // CHUNK):
+        got = jnp.dot(pick, pair[c * CHUNK : (c + 1) * CHUNK, :], preferred_element_type=F32).astype(BF16)
         for b in range(1, BRANCHES):
             count = CHUNK >> b
             at = CHUNK - (CHUNK >> (b - 1))
-            row = part * PICKED[b] + c * count
+            row = part * 2 * PICKED[b] + c * count
             keys[b][row : row + count, :] = got[at : at + count, :]
 
 
-def add_cross(q, keys, acc, first):
+def add_cross(q, keys, acc, parts, first):
     for b in range(1, BRANCHES):
-        size = CROSS[b]
-        step = 192
-        for at in range(0, size, step):
-            rows = pl.ds(CROSS_START[b] + at, min(step, size - at))
-            total = fast_tile(q[rows, :], keys[b][...])
-            acc[rows, :] = total if first else acc[rows, :] + total
-
-
-def add_own(q, own_q, blocks, keys, acc):
+        size = 2 * PICKED[b]
+        step = CROSS_STEP[b]
+        for at in range(0, CROSS[b], step):
+            rows = pl.ds(CROSS_START[b] + at, step)
+            total = None if first else acc[rows, :]
+            for part in parts:
+                added = fast_tile(q[rows, :], keys[b][part * size : (part + 1) * size, :])
+                total = added if total is None else total + added
+            acc[rows, :] = total
+
+
+def add_own(q, own_q, pair, keys, part, acc):
     for c in range(ROWS // CHUNK):
         rows = pl.ds(c * CHUNK, CHUNK)
-        total = acc[rows, :]
-        for kv in blocks:
-            total = total + fast_tile(q[rows, :], kv[...])
-        acc[rows, :] = total
+        acc[rows, :] += fast_tile(q[rows, :], pair[:ROWS, :]) + fast_tile(q[rows, :], pair[ROWS:, :])
     for b in range(1, BRANCHES):
+        size = 2 * PICKED[b]
         step = min(192, PICKED[b])
         for at in range(0, PICKED[b], step):
             start = START[b] + at
             rows = pl.ds(ROWS + start, step)
-            acc[rows, :] += fast_tile(own_q[start : start + step, :], keys[b][...])
-
-
-def first_kernel(sm, mine, other, q, near, own, *keys):
+            acc[rows, :] += fast_tile(own_q[start : start + step, :], keys[b][part * size : (part + 1) * size, :])
+
+
+def early_kernel(sm, pair0, pair1, pair2, q, near, r1, r2, r4, r6, visiting, cross, own, *keys):
     keys = (None,) + keys
-    select_keys(sm, mine, keys, 0)
-    select_keys(sm, other, keys, 1)
-    lower = iota((CHUNK, CHUNK), 1) <= iota((CHUNK, CHUNK), 0)
-    for c in range(ROWS // CHUNK):
-        rows = pl.ds(c * CHUNK, CHUNK)
-        total = fast_tile(q[rows, :], mine[c * CHUNK : (c + 1) * CHUNK, :], lower)
-        if c:
-            total = total + fast_tile(q[rows, :], mine[: c * CHUNK, :])
-        own[rows, :] = total
-    for b in range(1, BRANCHES):
-        size = PICKED[b]
-        lower = iota((size, size), 1) <= iota((size, size), 0)
-        own[ROWS + START[b] : ROWS + START[b] + size, :] = fast_tile(
-            near[START[b] : START[b] + size, :], keys[b][0:size, :], lower
-        )
-
-    @pl.when(lax.rem(sm[1], 2) == 1)
-    def _():
-        for c in range(ROWS // CHUNK):
-            rows = pl.ds(c * CHUNK, CHUNK)
-            own[rows, :] += fast_tile(q[rows, :], other[...])
-        for b in range(1, BRANCHES):
-            size = PICKED[b]
-            rows = pl.ds(ROWS + START[b], size)
-            own[rows, :] += fast_tile(near[START[b] : START[b] + size, :], keys[b][size : 2 * size, :])
-
-
-def second_kernel(sm, mine0, other0, mine, other, q, near, r1, r2, r4, r6, own_in, visiting, cross, own, *keys):
-    del own_in
-    keys = (None,) + keys
+    core = lax.rem(sm[1], 2)
     visiting[0:384, :] = r1[0:384, :]
     visiting[384:576, :] = r1[384:576, :]
     visiting[576:768, :] = r2[0:192, :]
@@ -187,16 +164,37 @@
     visiting[1152:1248, :] = r2[480:576, :]
     visiting[1248:1440, :] = r4[...]
     visiting[1440:1632, :] = r6[...]
-    select_keys(sm, mine0, keys, 0)
-    select_keys(sm, other0, keys, 1)
-    add_cross(visiting, keys, cross, True)
-    select_keys(sm, mine, keys, 0)
-    select_keys(sm, other, keys, 1)
-    add_cross(visiting, keys, cross, False)
+    for part, pair in enumerate((pair0, pair1, pair2)):
+        select_keys(sm, pair, keys, part)
+    add_cross(visiting, keys, cross, (0, 1, 2), True)
+    lower = iota((CHUNK, CHUNK), 1) <= iota((CHUNK, CHUNK), 0)
+    for c in range(ROWS // CHUNK):
+        rows = pl.ds(c * CHUNK, CHUNK)
+        start = pl.multiple_of(core * ROWS, ROWS)
+        total = fast_tile(q[rows, :], pair0[pl.ds(start + c * CHUNK, CHUNK), :], lower)
+        if c:
+            total = total + fast_tile(q[rows, :], pair0[pl.ds(start, c * CHUNK), :])
+        own[rows, :] = total
+    for b in range(1, BRANCHES):
+        size = PICKED[b]
+        lower = iota((size, size), 1) <= iota((size, size), 0)
+        own[ROWS + START[b] : ROWS + START[b] + size, :] = fast_tile(
+            near[START[b] : START[b] + size, :], keys[b][pl.ds(pl.multiple_of(core * size, size), size), :], lower
+        )
+
+    @pl.when(core == 1)
+    def _():
+        for c in range(ROWS // CHUNK):
+            rows = pl.ds(c * CHUNK, CHUNK)
+            own[rows, :] += fast_tile(q[rows, :], pair0[:ROWS, :])
+        for b in range(1, BRANCHES):
+            size = PICKED[b]
+            rows = pl.ds(ROWS + START[b], size)
+            own[rows, :] += fast_tile(near[START[b] : START[b] + size, :], keys[b][:size, :])
 
     @pl.when(before(sm, 1))
     def _():
-        add_own(q, near, (mine, other), keys, own)
+        add_own(q, near, pair1, keys, 1, own)
 
 
 def before(sm, stage):
@@ -204,35 +202,21 @@
     return jnp.bitwise_xor(z, stage) < z
 
 
-def stage_kernel(stage, sm, mine, other, q, near, visiting, cross_in, own_in, cross, own, *keys):
-    del cross_in, own_in
-    keys = (None,) + keys
-    select_keys(sm, mine, keys, 0)
-    select_keys(sm, other, keys, 1)
-    add_cross(visiting, keys, cross, False)
-
-    @pl.when(before(sm, stage))
-    def _():
-        add_own(q, near, (mine, other), keys, own)
-
-
 def last_cross_kernel(sm, *refs):
-    kvs, refs = refs[:8], refs[8:]
+    pairs, refs = refs[:4], refs[4:]
     visiting, cross, refs = refs[0], refs[2], refs[3:]
     outs, refs = (None,) + refs[:7], refs[7:]
     keys, top, sums = (None,) + refs[:3], refs[3], (None,) + refs[4:11]
-    select_keys(sm, kvs[6], keys, 0)
-    select_keys(sm, kvs[7], keys, 1)
-    add_cross(visiting, keys, cross, False)
+    select_keys(sm, pairs[3], keys, 0)
+    add_cross(visiting, keys, cross, (0,), False)
     top[...] = jnp.zeros_like(top)
 
     @pl.when(jnp.logical_not(in_range(cross[:, HD:])))
     def _():
         cross[...] = jnp.zeros_like(cross)
         top[...] = jnp.full_like(top, NEG)
-        for n in range(0, 8, 2):
-            select_keys(sm, kvs[n], keys, 0)
-            select_keys(sm, kvs[n + 1], keys, 1)
+        for pair in pairs:
+            select_keys(sm, pair, keys, 0)
             for b in range(1, BRANCHES):
 
                 def step(i, carry, b=b):
@@ -265,16 +249,17 @@
 
 
 def last_own_kernel(sm, *refs):
-    kvs, refs = refs[:8], refs[8:]
+    pairs, refs = refs[:4], refs[4:]
     q, near, own, out, log_sum, refs = refs[0], refs[1], refs[3], refs[4], refs[5], refs[6:]
     keys, top = (None,) + refs[:3], refs[3]
     lane = sm[1]
 
-    @pl.when(before(sm, 3))
-    def _():
-        select_keys(sm, kvs[6], keys, 0)
-        select_keys(sm, kvs[7], keys, 1)
-        add_own(q, near, kvs[6:8], keys, own)
+    for part in (2, 3):
+
+        @pl.when(before(sm, part))
+        def _(part=part):
+            select_keys(sm, pairs[part], keys, 0)
+            add_own(q, near, pairs[part], keys, 0, own)
 
     top[...] = jnp.zeros_like(top)
 
@@ -282,26 +267,27 @@
     def _():
         own[...] = jnp.zeros_like(own)
         top[...] = jnp.full_like(top, NEG)
-        for n in range(8):
-            z = jnp.bitwise_xor(lane // 2, n // 2)
-            block = 2 * z + (lax.rem(lane, 2) if n % 2 == 0 else 1 - lax.rem(lane, 2))
-
-            @pl.when(block <= lane)
-            def _(n=n, block=block):
-                select_keys(sm, kvs[n], keys, 0)
-                for b in range(BRANCHES):
-                    size = ROWS >> b
-                    source, key = (q, kvs[n]) if b == 0 else (near, keys[b])
-
-                    def step(i, carry, b=b, size=size, source=source, key=key):
-                        at = pl.multiple_of(START[b] + i * 96, 96)
-                        rows = pl.ds(pl.multiple_of((ROWS if b else 0) + at, 96), 96)
-                        row = iota((96, size), 0) + i * 96 + lane * size
-                        col = iota((96, size), 1) + block * size
-                        slow_tile(source[pl.ds(at, 96), :], key[0:size, :], col <= row, own, top, rows)
-                        return carry
-
-                    lax.fori_loop(0, size // 96, step, 0)
+        for n, pair in enumerate(pairs):
+            select_keys(sm, pair, keys, 0)
+            for core in range(2):
+                block = 2 * jnp.bitwise_xor(lane // 2, n) + core
+
+                @pl.when(block <= lane)
+                def _(pair=pair, core=core, block=block):
+                    for b in range(BRANCHES):
+                        size = ROWS >> b
+                        source, key = (q, pair) if b == 0 else (near, keys[b])
+
+                        def step(i, carry, b=b, size=size, source=source, key=key):
+                            at = pl.multiple_of(START[b] + i * 96, 96)
+                            rows = pl.ds(pl.multiple_of((ROWS if b else 0) + at, 96), 96)
+                            row = iota((96, size), 0) + i * 96 + lane * size
+                            col = iota((96, size), 1) + block * size
+                            part = key[core * size : (core + 1) * size, :]
+                            slow_tile(source[pl.ds(at, 96), :], part, col <= row, own, top, rows)
+                            return carry
+
+                        lax.fori_loop(0, size // 96, step, 0)
 
     total = own[:, HD:]
     out[...] = own[:, :HD] / total
@@ -394,15 +380,16 @@
     )(sm, *operands)
 
 
-def pack(k, v):
+def pack(sm, q, k, v):
     return pl.pallas_call(
         pack_kernel,
         name="pack",
-        out_shape=jax.ShapeDtypeStruct((ROWS, 2 * HD), BF16),
-        in_specs=[pl.BlockSpec(memory_space=pl.ANY)] * 2,
-        out_specs=pl.BlockSpec(memory_space=pltpu.VMEM),
-        scratch_shapes=[pltpu.SemaphoreType.DMA((2,))],
-    )(k, v)
+        out_shape=[jax.ShapeDtypeStruct((TOTAL, HD), BF16), jax.ShapeDtypeStruct((ROWS, 2 * HD), BF16)],
+        in_specs=[pl.BlockSpec(memory_space=pltpu.SMEM)] + [pl.BlockSpec(memory_space=pl.ANY)] * 3,
+        out_specs=[pl.BlockSpec(memory_space=pltpu.VMEM)] * 2,
+        scratch_shapes=[pltpu.VMEM((ROWS, HD), BF16), pltpu.SemaphoreType.DMA((3,))],
+        cost_estimate=pl.CostEstimate(flops=1, bytes_accessed=1, transcendentals=0),
+    )(sm, q, k, v)
 
 
 def place_of(index):
@@ -435,78 +422,64 @@
     return pairs
 
 
+def both_cores(block):
+    groups = [[i, i + 1] for i in range(0, 64, 2)]
+    return lax.all_gather(block, "seq", axis_index_groups=groups, tiled=True)
+
+
 def on_device(queries, key_rows, values, offsets):
     seq, head = lax.axis_index("seq"), lax.axis_index("head")
     mine = lax.dynamic_slice_in_dim(offsets, head, 1, axis=1)[:, 0]
     sm = jnp.concatenate([jnp.stack([seq // 8, seq % 8]).astype(jnp.int32), mine[1:], jnp.zeros((3,), jnp.int32)])
-    kv = pack(key_rows, values)
-    queries, kv = lax.optimization_barrier((queries, kv))
-    (near,) = call(
-        pick_kernel, "pick_queries", sm, [queries], [((TOTAL, HD), BF16)], [], 2 * 672 * 256 * 128
-    )
-    pair = [(i, i ^ 1) for i in range(64)]
+    near, kv = pack(sm, queries, key_rows, values)
     keys = [((ROWS, 2 * HD), BF16), ((384, 2 * HD), BF16), ((192, 2 * HD), BF16)]
     state = [((VISITING, 2 * HD), F32), ((ROWS + TOTAL, 2 * HD), F32)]
     work = 4 * HD * 2 * ROWS * 2 * ROWS
     r1 = lax.ppermute(near, "seq", meet(1))
     block2 = lax.ppermute(kv, "seq", exchange(2))
     block1 = lax.ppermute(kv, "seq", exchange(1))
-    kvs = [kv, lax.ppermute(kv, "seq", pair)]
     r2 = lax.ppermute(jnp.concatenate([near[384:], r1[384:]]), "seq", meet(2))
-    (own,) = call(first_kernel, "own_chip", sm, kvs + [queries, near], state[1:], keys, work // 2)
     pair3 = jnp.concatenate([near[576:], r1[576:]])
     r4 = lax.ppermute(pair3, "seq", meet(4))
     r6 = lax.ppermute(pair3, "seq", meet(6))
-    block2, r2, r4, r6, own = lax.optimization_barrier((block2, r2, r4, r6, own))
+    pairs = [both_cores(kv), both_cores(block1)]
+    block2, r2, r4, r6, pairs[1] = lax.optimization_barrier((block2, r2, r4, r6, pairs[1]))
     block3 = lax.ppermute(block2, "seq", exchange(1))
-    block1, own = lax.optimization_barrier((block1, own))
-    kvs += [block1, lax.ppermute(block1, "seq", pair)]
-    kvs += [block2, lax.ppermute(block2, "seq", pair)]
-    kvs[5], own = lax.optimization_barrier((kvs[5], own))
+    pairs.append(both_cores(block2))
     visiting, cross, own = call(
-        second_kernel,
-        "chip_1",
+        early_kernel,
+        "three_chips",
         sm,
-        kvs[:4] + [queries, near, r1, r2, r4, r6, own],
+        pairs + [queries, near, r1, r2, r4, r6],
         [((VISITING, HD), BF16)] + state,
-        keys,
+        [((3 * rows, width), dtype) for (rows, width), dtype in keys],
         work,
-        {11: 2},
-    )
-    cross, own = call(
-        functools.partial(stage_kernel, 2),
-        "chip_2",
-        sm,
-        kvs[4:] + [queries, near, visiting, cross, own],
-        state,
-        keys,
-        work,
-        {6: 0, 7: 1},
     )
     block3, own = lax.optimization_barrier((block3, own))
-    kvs += [block3, lax.ppermute(block3, "seq", pair)]
+    pairs.append(both_cores(block3))
     crossed = call(
         last_cross_kernel,
         "cross_end",
         sm,
-        kvs + [visiting, cross],
+        pairs + [visiting, cross],
         state[:1] + [((message_rows(d)[2], HD), BF16) for d in range(1, GROUPS)],
         keys + [((VISITING, HD), F32)] + [((message_rows(d)[1] * 128, 128), F32) for d in range(1, GROUPS)],
         work // 2,
-        {10: 0},
+        {6: 0},
     )
-    back = [
-        lax.ppermute(crossed[d], "seq", to_later(d)) for d in range(1, GROUPS)
-    ]
+    back = [lax.ppermute(crossed[j], "seq", to_later(j)) for j in range(1, 6)]
+    for j in (6, 7):
+        message, back[j - 6] = lax.optimization_barrier((crossed[j], back[j - 6]))
+        back.append(lax.ppermute(message, "seq", to_later(j)))
     _, out, log_sum = call(
         last_own_kernel,
         "own_end",
         sm,
-        kvs + [queries, near, own],
+        pairs + [queries, near, own],
         state[1:] + [((ROWS + TOTAL, HD), F32)] * 2,
         keys + [((ROWS + TOTAL, HD), F32)],
         work // 2,
-        {11: 0},
+        {7: 0},
     )
     (merged,) = call(
         merge_kernel,

time: 205 us -> 200 us (0.976)
  the two profiles are of different devices: /device:TPU:193 before, /device:TPU:449 now
where the time goes in v3:
time: 200 us; the launch traced here: 199 us
  Pallas kernels  90.5 us (45%)
  blocking collectives  63.1 us (32%)
  starting transfers between devices  35.1 us (18%)
  waiting for transfers between devices  6.56 us (3%)
  local copies, waits for them, and re-layouts  3.23 us (2%)
    pallas_call x4, Pallas kernels, call(): pl.pallas_call(kernel, name=name, out_shape=shapes, in_specs=[pl.BlockSpe...  87.8 us
    all_to_all x1, blocking collectives, on_device(): lax.all_to_all(merged, 'head', split_axis=0, concat_axis=1, tiled=True)  50.6 us
    ppermute x5, starting transfers between devices, on_device(): back = [lax.ppermute(crossed[j], 'seq', to_later(j)) for j in range(1, 6)]  14.6 us
    all_gather x4, blocking collectives, both_cores(): return lax.all_gather(block, 'seq', axis_index_groups=groups, tiled=True)  12.5 us
    ppermute x1, waiting for transfers between devices, on_device(): block1 = lax.ppermute(kv, 'seq', exchange(1))  4.4 us
    ppermute x1, starting transfers between devices, on_device(): r6 = lax.ppermute(pair3, 'seq', meet(6))  4.37 us
  transfers between devices with their start and end apart: 14, of which 2 were waited for; matrix products, arithmetic and copies ran while one was open for 1% of the time, Pallas kernels for 42%

profile of v3, /device:TPU:449, one launch (start us, length us, event | category | flops | bytes accessed | tf_op | source)
XLA Modules:
  0.0 199.4 jit_solution(15816755863841264677)
XLA Ops:
  0.0 0.7 copy-done
  0.7 0.1 constant_dynamic-slice_fusion
  0.8 0.1 slice_reduce_fusion
  0.9 0.6 pad_add_fusion.sm
  1.5 2.7 %pack.1 = (bf16[672,128]{1,0:T(8,128)(2,1)}, bf16[768,256]{1,0:T(8,128)(2,1)}) custom-call(s32[8]{0:T(128)} %pad_add_fusion.sm, bf16[768,128]{1,0:T(8,128)(2,1)} %refs_4_.1, bf16[768,128]{1,0:T(8,128)(2,1)} %k.1, bf16[768,128]{1,0:T(8,128)(2,1)} %v.1), custom_call_target="tpu_custom_call" | custom-call | flops 1 | bytes 1 | tf_op jit(solution)/shard_map/pack/pallas_call | solution.py:384
  4.2 2.1 %collective-permute-start.1 = (bf16[672,128]{1,0:T(8,128)(2,1)}, bf16[672,128]{1,0:T(8,128)(2,1)S(1)}, u32[]{:S(2)}, u32[]{:S(2)}) collective-permute-start(bf16[672,128]{1,0:T(8,128)(2,1)} %get-tuple-element.31.near.refs_5_), channel_id=1, source_target_pairs={{0,96},{8,104},{16,112},{24,120},{32,64},{40,72},{48,80},{56,88},{... | collective-permute-start | bytes 516104 | tf_op jit(solution)/shard_map/ppermute | solution.py:438
  6.2 2.2 %collective-permute-start.5 = (bf16[768,256]{1,0:T(8,128)(2,1)}, bf16[768,256]{1,0:T(8,128)(2,1)S(1)}, u32[]{:S(2)}, u32[]{:S(2)}) collective-permute-start(bf16[768,256]{1,0:T(8,128)(2,1)} %get-tuple-element.30), channel_id=1, source_target_pairs={{0,16},{8,24},{16,0},{24,8},{32,48},{40,56},{48,32},{56,40},{64,80... | collective-permute-start | bytes 1179656 | tf_op jit(solution)/shard_map/ppermute | solution.py:440
  8.4 2.2 %collective-permute-start = (bf16[768,256]{1,0:T(8,128)(2,1)}, bf16[768,256]{1,0:T(8,128)(2,1)S(1)}, u32[]{:S(2)}, u32[]{:S(2)}) collective-permute-start(bf16[768,256]{1,0:T(8,128)(2,1)} %get-tuple-element.30), channel_id=1, source_target_pairs={{0,32},{8,40},{16,48},{24,56},{32,0},{40,8},{48,16},{56,24},{64,96... | collective-permute-start | bytes 1179656 | tf_op jit(solution)/shard_map/ppermute | solution.py:439
  10.6 0.7 slice.22
  11.3 0.9 slice.20
  12.2 2.1 %collective-permute-done.1.r1 = bf16[672,128]{1,0:T(8,128)(2,1)S(1)} collective-permute-done((bf16[672,128]{1,0:T(8,128)(2,1)}, bf16[672,128]{1,0:T(8,128)(2,1)S(1)}, u32[]{:S(2)}, u32[]{:S(2)}) %collective-permute-start.1) | collective-permute-done | bytes 172064 | tf_op jit(solution)/shard_map/ppermute | solution.py:438
  14.4 4.4 %collective-permute-start.4 = (bf16[192,128]{1,0:T(8,128)(2,1)S(1)}, bf16[192,128]{1,0:T(8,128)(2,1)S(1)}, u32[]{:S(2)}, u32[]{:S(2)}) collective-permute-start(bf16[192,128]{1,0:T(8,128)(2,1)S(1)} %pad_maximum_fusion.1), channel_id=1, source_target_pairs={{0,384},{8,392},{16,400},{24,408},{32,416},{40,424},{48,432},{56,4... | collective-permute-start | bytes 147464 | tf_op jit(solution)/shard_map/ppermute | solution.py:444
  18.7 2.4 %collective-permute-start.3 = (bf16[192,128]{1,0:T(8,128)(2,1)S(1)}, bf16[192,128]{1,0:T(8,128)(2,1)S(1)}, u32[]{:S(2)}, u32[]{:S(2)}) collective-permute-start(bf16[192,128]{1,0:T(8,128)(2,1)S(1)} %pad_maximum_fusion.1), channel_id=1, source_target_pairs={{0,256},{8,264},{16,272},{24,280},{32,288},{40,296},{48,304},{56,3... | collective-permute-start | bytes 147464 | tf_op jit(solution)/shard_map/ppermute | solution.py:443
  21.2 0.0 copy-start.1
  21.2 0.0 copy-start.2
  21.3 2.3 %collective-permute-start.2 = (bf16[576,128]{1,0:T(8,128)(2,1)S(1)}, bf16[576,128]{1,0:T(8,128)(2,1)S(1)}, u32[]{:S(2)}, u32[]{:S(2)}) collective-permute-start(bf16[576,128]{1,0:T(8,128)(2,1)S(1)} %pad_maximum_fusion), channel_id=1, source_target_pairs={{0,128},{8,136},{16,144},{24,152},{32,160},{40,168},{48,176},{56,1... | collective-permute-start | bytes 442376 | tf_op jit(solution)/shard_map/ppermute | solution.py:441
  23.6 4.4 %collective-permute-done.5 = bf16[768,256]{1,0:T(8,128)(2,1)S(1)} collective-permute-done((bf16[768,256]{1,0:T(8,128)(2,1)}, bf16[768,256]{1,0:T(8,128)(2,1)S(1)}, u32[]{:S(2)}, u32[]{:S(2)}) %collective-permute-start.5) | collective-permute-done | bytes 393248 | tf_op jit(solution)/shard_map/ppermute | solution.py:440
  28.0 2.9 %all_gather.13.pair1.refs_1_ = bf16[1536,256]{1,0:T(8,128)(2,1)S(1)} all-gather(bf16[768,256]{1,0:T(8,128)(2,1)S(1)} %collective-permute-done.5), channel_id=1, replica_groups={{0,8},{16,24},{32,40},{48,56},{64,72},{80,88},{96,104},{112,120},{128,1..., dimensions={0}, use_global_device_ids=true | all-gather | bytes 1179648 | tf_op jit(solution)/shard_map/all_gather | solution.py:427
  30.9 0.0 collective-permute-done.4.r6
  30.9 0.0 collective-permute-done.3.r4
  30.9 0.0 collective-permute-done.2.r2
  30.9 0.0 collective-permute-done
  30.9 2.4 %collective-permute-start.6 = (bf16[768,256]{1,0:T(8,128)(2,1)S(1)}, bf16[768,256]{1,0:T(8,128)(2,1)S(1)}, u32[]{:S(2)}, u32[]{:S(2)}) collective-permute-start(bf16[768,256]{1,0:T(8,128)(2,1)S(1)} %collective-permute-done), channel_id=1, source_target_pairs={{0,16},{8,24},{16,0},{24,8},{32,48},{40,56},{48,32},{56,40},{64,80... | collective-permute-start | bytes 1179656 | tf_op jit(solution)/shard_map/ppermute | solution.py:447
  33.4 4.8 %all_gather.12.pair0.refs_0_ = bf16[1536,256]{1,0:T(8,128)(2,1)S(1)} all-gather(bf16[768,256]{1,0:T(8,128)(2,1)S(1)} %copy-done.4), channel_id=1, replica_groups={{0,8},{16,24},{32,40},{48,56},{64,72},{80,88},{96,104},{112,120},{128,1..., dimensions={0}, use_global_device_ids=true | all-gather | bytes 1179648 | tf_op jit(solution)/shard_map/all_gather | solution.py:427
  38.2 2.4 %all_gather.14.pair2.refs_2_ = bf16[1536,256]{1,0:T(8,128)(2,1)S(1)} all-gather(bf16[768,256]{1,0:T(8,128)(2,1)S(1)} %collective-permute-done), channel_id=1, replica_groups={{0,8},{16,24},{32,40},{48,56},{64,72},{80,88},{96,104},{112,120},{128,1..., dimensions={0}, use_global_device_ids=true | all-gather | bytes 1179648 | tf_op jit(solution)/shard_map/all_gather | solution.py:427
  40.6 0.0 copy-done.1
  40.6 8.5 %three_chips.1 = (bf16[1632,128]{1,0:T(8,128)(2,1)S(1)}, f32[1632,256]{1,0:T(8,128)S(1)}, f32[1440,256]{1,0:T(8,128)S(1)}) custom-call(s32[8]{0:T(128)S(1)} %copy-done.3, bf16[1536,256]{1,0:T(8,128)(2,1)S(1)} %all_gather.12.pair0.refs_0_, bf16[1536,256]{1,0:T(8,128)(2,1)S(1)} %all_gather.13.pair1.refs_1_, bf16[1536,256]{1,0:T(8,128)(2,1)S(1)} %all_gather.14.pair2.refs_2_, ...), custom_call_target="tpu_custom_call" | custom-call | flops 1 | bytes 1 | tf_op jit(solution)/shard_map/three_chips/pallas_call | solution.py:369
  49.1 0.0 collective-permute-done.6
  49.1 2.4 %all_gather.15.refs_3_ = bf16[1536,256]{1,0:T(8,128)(2,1)S(1)} all-gather(bf16[768,256]{1,0:T(8,128)(2,1)S(1)} %collective-permute-done.6), channel_id=1, replica_groups={{0,8},{16,24},{32,40},{48,56},{64,72},{80,88},{96,104},{112,120},{128,1..., dimensions={0}, use_global_device_ids=true | all-gather | bytes 1179648 | tf_op jit(solution)/shard_map/all_gather | solution.py:427
  51.5 2.5 %cross_end.1 = (f32[1632,256]{1,0:T(8,128)S(1)}, bf16[704,128]{1,0:T(8,128)(2,1)S(1)}, bf16[304,128]{1,0:T(8,128)(2,1)S(1)}, bf16[304,128]{1,0:T(8,128)(2,1)S(1)...) custom-call(s32[8]{0:T(128)S(1)} %copy-done.3, ...), custom_call_target="tpu_custom_call", output_to_operand_aliasing={{0}: (6, {})} | custom-call | flops 1 | bytes 1 | tf_op jit(solution)/shard_map/cross_end/pallas_call | solution.py:369
  54.0 1.3 collective-permute-start.7
  55.3 2.2 %collective-permute-start.8 = (bf16[304,128]{1,0:T(8,128)(2,1)S(1)}, bf16[304,128]{1,0:T(8,128)(2,1)S(1)}, u32[]{:S(2)}, u32[]{:S(2)}) collective-permute-start(bf16[304,128]{1,0:T(8,128)(2,1)S(1)} %get-tuple-element.45), channel_id=1, source_target_pairs={{0,128},{8,136},{16,144},{24,152},{32,160},{40,168},{48,176},{56,1... | collective-permute-start | bytes 233480 | tf_op jit(solution)/shard_map/ppermute | solution.py:470
  57.5 5.2 %collective-permute-start.9 = (bf16[304,128]{1,0:T(8,128)(2,1)S(1)}, bf16[304,128]{1,0:T(8,128)(2,1)S(1)}, u32[]{:S(2)}, u32[]{:S(2)}) collective-permute-start(bf16[304,128]{1,0:T(8,128)(2,1)S(1)} %get-tuple-element.47), channel_id=1, source_target_pairs={{0,224},{8,232},{16,240},{24,248},{32,192},{40,200},{48,208},{56,2... | collective-permute-start | bytes 233480 | tf_op jit(solution)/shard_map/ppermute | solution.py:470
  62.7 4.6 %collective-permute-start.10 = (bf16[112,128]{1,0:T(8,128)(2,1)S(1)}, bf16[112,128]{1,0:T(8,128)(2,1)S(1)}, u32[]{:S(2)}, u32[]{:S(2)}) collective-permute-start(bf16[112,128]{1,0:T(8,128)(2,1)S(1)} %get-tuple-element.48), channel_id=1, source_target_pairs={{0,256},{8,264},{16,272},{24,280},{32,288},{40,296},{48,304},{56,3... | collective-permute-start | bytes 86024 | tf_op jit(solution)/shard_map/ppermute | solution.py:470
  67.4 1.3 collective-permute-start.11
  68.7 0.0 collective-permute-done.8.refs_1_
  68.7 1.3 collective-permute-start.13
  70.0 0.0 collective-permute-done.7.refs_0_
  70.0 1.3 collective-permute-start.12
  71.3 74.6 %own_end.1 = (f32[1440,256]{1,0:T(8,128)S(1)}, f32[1440,128]{1,0:T(8,128)S(1)}, f32[1440,128]{1,0:T(8,128)S(1)}) custom-call(s32[8]{0:T(128)S(1)} %copy-done.3, bf16[1536,256]{1,0:T(8,128)(2,1)S(1)} %all_gather.12.pair0.refs_0_, bf16[1536,256]{1,0:T(8,128)(2,1)S(1)} %all_gather.13.pair1.refs_1_, ...), custom_call_target="tpu_custom_call", output_to_operand_aliasing={{0}: (7, {})} | custom-call | flops 1 | bytes 1 | tf_op jit(solution)/shard_map/own_end/pallas_call | solution.py:369
  145.9 0.0 collective-permute-done.10.refs_3_
  145.9 0.0 collective-permute-done.11.refs_4_
  145.9 0.0 collective-permute-done.9.refs_2_
  145.9 0.0 collective-permute-done.13.refs_6_
  145.9 0.0 collective-permute-done.12.refs_5_
  145.9 2.1 %merge.1 = bf16[768,128]{1,0:T(8,128)(2,1)S(1)} custom-call(s32[8]{0:T(128)S(1)} %copy-done.3, bf16[704,128]{1,0:T(8,128)(2,1)S(1)} %collective-permute-done.7.refs_0_, bf16[304,128]{1,0:T(8,128)(2,1)S(1)} %collective-permute-done.8.refs_1_, bf16[304,128]{1,0:T(8,128)(2,1)S(1)} %collective-permute-done.9.refs_2_, ...), custom_call_target="tpu_custom_call" | custom-call | flops 1 | bytes 1 | tf_op jit(solution)/shard_map/merge/pallas_call | solution.py:369
  148.1 50.6 %all_to_all.19 = bf16[8,96,128]{2,1,0:T(8,128)(2,1)S(1)} all-to-all(bf16[8,96,128]{2,1,0:T(8,128)(2,1)S(1)} %bitcast.9), channel_id=1, replica_groups=mesh['seq'=64,'head'=8] {'head'}, dimensions={0} | all-to-all | bytes 393216 | tf_op jit(solution)/shard_map/all_to_all | solution.py:493
  198.7 0.7 copy_bitcast_fusion
  (11 shorter events, 0.0 us)
Async XLA Ops:
  0.0 0.7 copy-start
  4.2 29.2 %copy-start.4 = (bf16[768,256]{1,0:T(8,128)(2,1)S(1)}, bf16[768,256]{1,0:T(8,128)(2,1)}, u32[]{:S(2)}) copy-start(bf16[768,256]{1,0:T(8,128)(2,1)} %get-tuple-element.30) | copy-start | bytes 1179652
  4.2 10.2 %collective-permute-start.1 = (bf16[672,128]{1,0:T(8,128)(2,1)}, bf16[672,128]{1,0:T(8,128)(2,1)S(1)}, u32[]{:S(2)}, u32[]{:S(2)}) collective-permute-start(bf16[672,128]{1,0:T(8,128)(2,1)} %get-tuple-element.31.near.refs_5_), channel_id=1, source_target_pairs={{0,96},{8,104},{16,112},{24,120},{32,64},{40,72},{48,80},{56,88},{... | collective-permute-start | bytes 516104 | tf_op jit(solution)/shard_map/ppermute | solution.py:438
  6.2 21.7 %collective-permute-start.5 = (bf16[768,256]{1,0:T(8,128)(2,1)}, bf16[768,256]{1,0:T(8,128)(2,1)S(1)}, u32[]{:S(2)}, u32[]{:S(2)}) collective-permute-start(bf16[768,256]{1,0:T(8,128)(2,1)} %get-tuple-element.30), channel_id=1, source_target_pairs={{0,16},{8,24},{16,0},{24,8},{32,48},{40,56},{48,32},{56,40},{64,80... | collective-permute-start | bytes 1179656 | tf_op jit(solution)/shard_map/ppermute | solution.py:440
  8.4 22.5 %collective-permute-start = (bf16[768,256]{1,0:T(8,128)(2,1)}, bf16[768,256]{1,0:T(8,128)(2,1)S(1)}, u32[]{:S(2)}, u32[]{:S(2)}) collective-permute-start(bf16[768,256]{1,0:T(8,128)(2,1)} %get-tuple-element.30), channel_id=1, source_target_pairs={{0,32},{8,40},{16,48},{24,56},{32,0},{40,8},{48,16},{56,24},{64,96... | collective-permute-start | bytes 1179656 | tf_op jit(solution)/shard_map/ppermute | solution.py:439
  14.4 16.5 %collective-permute-start.4 = (bf16[192,128]{1,0:T(8,128)(2,1)S(1)}, bf16[192,128]{1,0:T(8,128)(2,1)S(1)}, u32[]{:S(2)}, u32[]{:S(2)}) collective-permute-start(bf16[192,128]{1,0:T(8,128)(2,1)S(1)} %pad_maximum_fusion.1), channel_id=1, source_target_pairs={{0,384},{8,392},{16,400},{24,408},{32,416},{40,424},{48,432},{56,4... | collective-permute-start | bytes 147464 | tf_op jit(solution)/shard_map/ppermute | solution.py:444
  18.7 12.2 %collective-permute-start.3 = (bf16[192,128]{1,0:T(8,128)(2,1)S(1)}, bf16[192,128]{1,0:T(8,128)(2,1)S(1)}, u32[]{:S(2)}, u32[]{:S(2)}) collective-permute-start(bf16[192,128]{1,0:T(8,128)(2,1)S(1)} %pad_maximum_fusion.1), channel_id=1, source_target_pairs={{0,256},{8,264},{16,272},{24,280},{32,288},{40,296},{48,304},{56,3... | collective-permute-start | bytes 147464 | tf_op jit(solution)/shard_map/ppermute | solution.py:443
  21.2 19.4 %copy-start.1 = (bf16[768,128]{1,0:T(8,128)(2,1)S(1)}, bf16[768,128]{1,0:T(8,128)(2,1)}, u32[]{:S(2)}) copy-start(bf16[768,128]{1,0:T(8,128)(2,1)} %refs_4_.1) | copy-start | bytes 589828
  21.2 19.3 %copy-start.2 = (bf16[672,128]{1,0:T(8,128)(2,1)S(1)}, bf16[672,128]{1,0:T(8,128)(2,1)}, u32[]{:S(2)}) copy-start(bf16[672,128]{1,0:T(8,128)(2,1)} %get-tuple-element.31.near.refs_5_) | copy-start | bytes 516100
  21.2 19.3 %copy-start.3 = (s32[8]{0:T(128)S(1)}, s32[8]{0:T(128)}, u32[]{:S(2)}) copy-start(s32[8]{0:T(128)} %pad_add_fusion.sm) | copy-start | bytes 100
  21.3 9.7 %collective-permute-start.2 = (bf16[576,128]{1,0:T(8,128)(2,1)S(1)}, bf16[576,128]{1,0:T(8,128)(2,1)S(1)}, u32[]{:S(2)}, u32[]{:S(2)}) collective-permute-start(bf16[576,128]{1,0:T(8,128)(2,1)S(1)} %pad_maximum_fusion), channel_id=1, source_target_pairs={{0,128},{8,136},{16,144},{24,152},{32,160},{40,168},{48,176},{56,1... | collective-permute-start | bytes 442376 | tf_op jit(solution)/shard_map/ppermute | solution.py:441
  30.9 18.2 %collective-permute-start.6 = (bf16[768,256]{1,0:T(8,128)(2,1)S(1)}, bf16[768,256]{1,0:T(8,128)(2,1)S(1)}, u32[]{:S(2)}, u32[]{:S(2)}) collective-permute-start(bf16[768,256]{1,0:T(8,128)(2,1)S(1)} %collective-permute-done), channel_id=1, source_target_pairs={{0,16},{8,24},{16,0},{24,8},{32,48},{40,56},{48,32},{56,40},{64,80... | collective-permute-start | bytes 1179656 | tf_op jit(solution)/shard_map/ppermute | solution.py:447
  54.0 16.0 %collective-permute-start.7 = (bf16[704,128]{1,0:T(8,128)(2,1)S(1)}, bf16[704,128]{1,0:T(8,128)(2,1)S(1)}, u32[]{:S(2)}, u32[]{:S(2)}) collective-permute-start(bf16[704,128]{1,0:T(8,128)(2,1)S(1)} %get-tuple-element.42), channel_id=1, source_target_pairs={{0,96},{8,104},{16,112},{24,120},{32,64},{40,72},{48,80},{56,88},{... | collective-permute-start | bytes 540680 | tf_op jit(solution)/shard_map/ppermute | solution.py:470
  55.3 13.3 %collective-permute-start.8 = (bf16[304,128]{1,0:T(8,128)(2,1)S(1)}, bf16[304,128]{1,0:T(8,128)(2,1)S(1)}, u32[]{:S(2)}, u32[]{:S(2)}) collective-permute-start(bf16[304,128]{1,0:T(8,128)(2,1)S(1)} %get-tuple-element.45), channel_id=1, source_target_pairs={{0,128},{8,136},{16,144},{24,152},{32,160},{40,168},{48,176},{56,1... | collective-permute-start | bytes 233480 | tf_op jit(solution)/shard_map/ppermute | solution.py:470
  57.5 88.4 %collective-permute-start.9 = (bf16[304,128]{1,0:T(8,128)(2,1)S(1)}, bf16[304,128]{1,0:T(8,128)(2,1)S(1)}, u32[]{:S(2)}, u32[]{:S(2)}) collective-permute-start(bf16[304,128]{1,0:T(8,128)(2,1)S(1)} %get-tuple-element.47), channel_id=1, source_target_pairs={{0,224},{8,232},{16,240},{24,248},{32,192},{40,200},{48,208},{56,2... | collective-permute-start | bytes 233480 | tf_op jit(solution)/shard_map/ppermute | solution.py:470
  62.7 83.2 %collective-permute-start.10 = (bf16[112,128]{1,0:T(8,128)(2,1)S(1)}, bf16[112,128]{1,0:T(8,128)(2,1)S(1)}, u32[]{:S(2)}, u32[]{:S(2)}) collective-permute-start(bf16[112,128]{1,0:T(8,128)(2,1)S(1)} %get-tuple-element.48), channel_id=1, source_target_pairs={{0,256},{8,264},{16,272},{24,280},{32,288},{40,296},{48,304},{56,3... | collective-permute-start | bytes 86024 | tf_op jit(solution)/shard_map/ppermute | solution.py:470
  67.4 78.5 %collective-permute-start.11 = (bf16[112,128]{1,0:T(8,128)(2,1)S(1)}, bf16[112,128]{1,0:T(8,128)(2,1)S(1)}, u32[]{:S(2)}, u32[]{:S(2)}) collective-permute-start(bf16[112,128]{1,0:T(8,128)(2,1)S(1)} %get-tuple-element.49), channel_id=1, source_target_pairs={{0,352},{8,360},{16,368},{24,376},{32,320},{40,328},{48,336},{56,3... | collective-permute-start | bytes 86024 | tf_op jit(solution)/shard_map/ppermute | solution.py:470
  68.7 77.2 %collective-permute-start.13 = (bf16[112,128]{1,0:T(8,128)(2,1)S(1)}, bf16[112,128]{1,0:T(8,128)(2,1)S(1)}, u32[]{:S(2)}, u32[]{:S(2)}) collective-permute-start(bf16[112,128]{1,0:T(8,128)(2,1)S(1)} %get-tuple-element.51), channel_id=1, source_target_pairs={{0,480},{8,488},{16,496},{24,504},{32,448},{40,456},{48,464},{56,4... | collective-permute-start | bytes 86024 | tf_op jit(solution)/shard_map/ppermute | solution.py:473
  70.0 75.9 %collective-permute-start.12 = (bf16[112,128]{1,0:T(8,128)(2,1)S(1)}, bf16[112,128]{1,0:T(8,128)(2,1)S(1)}, u32[]{:S(2)}, u32[]{:S(2)}) collective-permute-start(bf16[112,128]{1,0:T(8,128)(2,1)S(1)} %get-tuple-element.50), channel_id=1, source_target_pairs={{0,384},{8,392},{16,400},{24,408},{32,416},{40,424},{48,432},{56,4... | collective-permute-start | bytes 86024 | tf_op jit(solution)/shard_map/ppermute | solution.py:473

commit v4 on v3

--- a/solution.py
+++ b/solution.py
@@ -152,7 +152,7 @@
             acc[rows, :] += fast_tile(own_q[start : start + step, :], keys[b][part * size : (part + 1) * size, :])
 
 
-def early_kernel(sm, pair0, pair1, pair2, q, near, r1, r2, r4, r6, visiting, cross, own, *keys):
+def early_kernel(sm, pair0, pair1, pair2, q, near, r1, r2, r4, visiting, cross, own, *keys):
     keys = (None,) + keys
     core = lax.rem(sm[1], 2)
     visiting[0:384, :] = r1[0:384, :]
@@ -162,8 +162,7 @@
     visiting[960:1056, :] = r1[576:672, :]
     visiting[1056:1152, :] = r2[192:288, :]
     visiting[1152:1248, :] = r2[480:576, :]
-    visiting[1248:1440, :] = r4[...]
-    visiting[1440:1632, :] = r6[...]
+    visiting[1248:1632, :] = r4[...]
     for part, pair in enumerate((pair0, pair1, pair2)):
         select_keys(sm, pair, keys, part)
     add_cross(visiting, keys, cross, (0, 1, 2), True)
@@ -439,18 +438,16 @@
     block2 = lax.ppermute(kv, "seq", exchange(2))
     block1 = lax.ppermute(kv, "seq", exchange(1))
     r2 = lax.ppermute(jnp.concatenate([near[384:], r1[384:]]), "seq", meet(2))
-    pair3 = jnp.concatenate([near[576:], r1[576:]])
-    r4 = lax.ppermute(pair3, "seq", meet(4))
-    r6 = lax.ppermute(pair3, "seq", meet(6))
+    r4 = lax.ppermute(jnp.concatenate([near[576:], r1[576:], r2[192:288], r2[480:]]), "seq", meet(4))
     pairs = [both_cores(kv), both_cores(block1)]
-    block2, r2, r4, r6, pairs[1] = lax.optimization_barrier((block2, r2, r4, r6, pairs[1]))
+    block2, r2 = lax.optimization_barrier((block2, r2))
     block3 = lax.ppermute(block2, "seq", exchange(1))
     pairs.append(both_cores(block2))
     visiting, cross, own = call(
         early_kernel,
         "three_chips",
         sm,
-        pairs + [queries, near, r1, r2, r4, r6],
+        pairs + [queries, near, r1, r2, r4],
         [((VISITING, HD), BF16)] + state,
         [((3 * rows, width), dtype) for (rows, width), dtype in keys],
         work,

time: 200 us -> 195 us (0.975)
  the two profiles are of different devices: /device:TPU:449 before, /device:TPU:193 now
where the time goes in v4:
time: 195 us; the launch traced here: 194 us
  Pallas kernels  90.5 us (46%)
  blocking collectives  55.4 us (28%)
  starting transfers between devices  40.5 us (21%)
  waiting for transfers between devices  4.61 us (2%)
  local copies, waits for them, and re-layouts  2.49 us (1%)
    pallas_call x4, Pallas kernels, call(): pl.pallas_call(kernel, name=name, out_shape=shapes, in_specs=[pl.BlockSpe...  87.8 us
    all_to_all x1, blocking collectives, on_device(): lax.all_to_all(merged, 'head', split_axis=0, concat_axis=1, tiled=True)  45.1 us
    ppermute x5, starting transfers between devices, on_device(): back = [lax.ppermute(crossed[j], 'seq', to_later(j)) for j in range(1, 6)]  15.7 us
    all_gather x4, blocking collectives, both_cores(): return lax.all_gather(block, 'seq', axis_index_groups=groups, tiled=True)  10.3 us
    ppermute x1, starting transfers between devices, on_device(): r1 = lax.ppermute(near, 'seq', meet(1))  6.25 us
    ppermute x1, starting transfers between devices, on_device(): lax.ppermute(jnp.concatenate([near[576:], r1[576:], r2[192:288], r2[480:]...  4.65 us
    ppermute x1, starting transfers between devices, on_device(): block2 = lax.ppermute(kv, 'seq', exchange(2))  4.01 us
  transfers between devices with their start and end apart: 13, of which 3 were waited for; matrix products, arithmetic and copies ran while one was open for 0% of the time, Pallas kernels for 43%

profile of v4, /device:TPU:193, one launch (start us, length us, event | category | flops | bytes accessed | tf_op | source)
XLA Modules:
  0.0 194.3 jit_solution(5350931140461860214)
XLA Ops:
  0.0 0.0 copy-start
  0.0 0.7 copy-done
  0.7 0.1 constant_dynamic-slice_fusion
  0.8 0.1 slice_reduce_fusion
  0.9 0.6 pad_add_fusion.sm
  1.5 2.7 %pack.1 = (bf16[672,128]{1,0:T(8,128)(2,1)}, bf16[768,256]{1,0:T(8,128)(2,1)}) custom-call(s32[8]{0:T(128)} %pad_add_fusion.sm, bf16[768,128]{1,0:T(8,128)(2,1)} %refs_4_.1, bf16[768,128]{1,0:T(8,128)(2,1)} %k.1, bf16[768,128]{1,0:T(8,128)(2,1)} %v.1), custom_call_target="tpu_custom_call" | custom-call | flops 1 | bytes 1 | tf_op jit(solution)/shard_map/pack/pallas_call | solution.py:383
  4.2 0.0 copy-start.2
  4.2 6.3 %collective-permute-start.2 = (bf16[672,128]{1,0:T(8,128)(2,1)}, bf16[672,128]{1,0:T(8,128)(2,1)S(1)}, u32[]{:S(2)}, u32[]{:S(2)}) collective-permute-start(bf16[672,128]{1,0:T(8,128)(2,1)} %get-tuple-element.28.near.refs_5_), channel_id=1, source_target_pairs={{0,96},{8,104},{16,112},{24,120},{32,64},{40,72},{48,80},{56,88},{... | collective-permute-start | bytes 516104 | tf_op jit(solution)/shard_map/ppermute | solution.py:437
  10.5 4.0 %collective-permute-start.1 = (bf16[768,256]{1,0:T(8,128)(2,1)}, bf16[768,256]{1,0:T(8,128)(2,1)S(1)}, u32[]{:S(2)}, u32[]{:S(2)}) collective-permute-start(bf16[768,256]{1,0:T(8,128)(2,1)} %get-tuple-element.27), channel_id=1, source_target_pairs={{0,32},{8,40},{16,48},{24,56},{32,0},{40,8},{48,16},{56,24},{64,96... | collective-permute-start | bytes 1179656 | tf_op jit(solution)/shard_map/ppermute | solution.py:438
  14.5 2.2 %collective-permute-start = (bf16[768,256]{1,0:T(8,128)(2,1)}, bf16[768,256]{1,0:T(8,128)(2,1)S(1)}, u32[]{:S(2)}, u32[]{:S(2)}) collective-permute-start(bf16[768,256]{1,0:T(8,128)(2,1)} %get-tuple-element.27), channel_id=1, source_target_pairs={{0,16},{8,24},{16,0},{24,8},{32,48},{40,56},{48,32},{56,40},{64,80... | collective-permute-start | bytes 1179656 | tf_op jit(solution)/shard_map/ppermute | solution.py:439
  16.7 0.9 slice.26
  17.6 1.0 collective-permute-done.2.r1
  18.6 3.1 %collective-permute-start.3 = (bf16[576,128]{1,0:T(8,128)(2,1)S(1)}, bf16[576,128]{1,0:T(8,128)(2,1)S(1)}, u32[]{:S(2)}, u32[]{:S(2)}) collective-permute-start(bf16[576,128]{1,0:T(8,128)(2,1)S(1)} %pad_maximum_fusion), channel_id=1, source_target_pairs={{0,128},{8,136},{16,144},{24,152},{32,160},{40,168},{48,176},{56,1... | collective-permute-start | bytes 442376 | tf_op jit(solution)/shard_map/ppermute | solution.py:440
  21.7 3.0 %all_gather.12.pair0.refs_0_ = bf16[1536,256]{1,0:T(8,128)(2,1)S(1)} all-gather(bf16[768,256]{1,0:T(8,128)(2,1)} %get-tuple-element.27), channel_id=1, replica_groups={{0,8},{16,24},{32,40},{48,56},{64,72},{80,88},{96,104},{112,120},{128,1..., dimensions={0}, use_global_device_ids=true | all-gather | bytes 1179648 | tf_op jit(solution)/shard_map/all_gather | solution.py:426
  24.7 0.0 copy-done.2
  24.7 0.0 copy-start.1
  24.7 0.6 collective-permute-done.3.r2
  25.4 4.7 %collective-permute-start.5 = (bf16[384,128]{1,0:T(8,128)(2,1)S(1)}, bf16[384,128]{1,0:T(8,128)(2,1)S(1)}, u32[]{:S(2)}, u32[]{:S(2)}) collective-permute-start(bf16[384,128]{1,0:T(8,128)(2,1)S(1)} %pad_maximum_fusion.1), channel_id=1, source_target_pairs={{0,256},{8,264},{16,272},{24,280},{32,288},{40,296},{48,304},{56,3... | collective-permute-start | bytes 294920 | tf_op jit(solution)/shard_map/ppermute | solution.py:441
  30.0 2.9 %collective-permute-done.1 = bf16[768,256]{1,0:T(8,128)(2,1)S(1)} collective-permute-done((bf16[768,256]{1,0:T(8,128)(2,1)}, bf16[768,256]{1,0:T(8,128)(2,1)S(1)}, u32[]{:S(2)}, u32[]{:S(2)}) %collective-permute-start.1) | collective-permute-done | bytes 393248 | tf_op jit(solution)/shard_map/ppermute | solution.py:438
  33.0 1.9 collective-permute-start.4
  34.9 2.6 %all_gather.14.pair2.refs_2_ = bf16[1536,256]{1,0:T(8,128)(2,1)S(1)} all-gather(bf16[768,256]{1,0:T(8,128)(2,1)S(1)} %collective-permute-done.1), channel_id=1, replica_groups={{0,8},{16,24},{32,40},{48,56},{64,72},{80,88},{96,104},{112,120},{128,1..., dimensions={0}, use_global_device_ids=true | all-gather | bytes 1179648 | tf_op jit(solution)/shard_map/all_gather | solution.py:426
  37.5 0.0 collective-permute-done
  37.5 2.4 %all_gather.13.pair1.refs_1_ = bf16[1536,256]{1,0:T(8,128)(2,1)S(1)} all-gather(bf16[768,256]{1,0:T(8,128)(2,1)S(1)} %collective-permute-done), channel_id=1, replica_groups={{0,8},{16,24},{32,40},{48,56},{64,72},{80,88},{96,104},{112,120},{128,1..., dimensions={0}, use_global_device_ids=true | all-gather | bytes 1179648 | tf_op jit(solution)/shard_map/all_gather | solution.py:426
  39.8 0.0 collective-permute-done.5.r4
  39.8 0.0 copy-done.1
  39.8 0.0 copy-done.3
  39.8 8.5 %three_chips.1 = (bf16[1632,128]{1,0:T(8,128)(2,1)S(1)}, f32[1632,256]{1,0:T(8,128)S(1)}, f32[1440,256]{1,0:T(8,128)S(1)}) custom-call(s32[8]{0:T(128)S(1)} %copy-done.3, bf16[1536,256]{1,0:T(8,128)(2,1)S(1)} %all_gather.12.pair0.refs_0_, bf16[1536,256]{1,0:T(8,128)(2,1)S(1)} %all_gather.13.pair1.refs_1_, bf16[1536,256]{1,0:T(8,128)(2,1)S(1)} %all_gather.14.pair2.refs_2_, ...), custom_call_target="tpu_custom_call" | custom-call | flops 1 | bytes 1 | tf_op jit(solution)/shard_map/three_chips/pallas_call | solution.py:368
  48.4 0.0 collective-permute-done.4
  48.4 2.4 %all_gather.15.refs_3_ = bf16[1536,256]{1,0:T(8,128)(2,1)S(1)} all-gather(bf16[768,256]{1,0:T(8,128)(2,1)S(1)} %collective-permute-done.4), channel_id=1, replica_groups={{0,8},{16,24},{32,40},{48,56},{64,72},{80,88},{96,104},{112,120},{128,1..., dimensions={0}, use_global_device_ids=true | all-gather | bytes 1179648 | tf_op jit(solution)/shard_map/all_gather | solution.py:426
  50.8 2.5 %cross_end.1 = (f32[1632,256]{1,0:T(8,128)S(1)}, bf16[704,128]{1,0:T(8,128)(2,1)S(1)}, bf16[304,128]{1,0:T(8,128)(2,1)S(1)}, bf16[304,128]{1,0:T(8,128)(2,1)S(1)...) custom-call(s32[8]{0:T(128)S(1)} %copy-done.3, ...), custom_call_target="tpu_custom_call", output_to_operand_aliasing={{0}: (6, {})} | custom-call | flops 1 | bytes 1 | tf_op jit(solution)/shard_map/cross_end/pallas_call | solution.py:368
  53.3 4.3 %collective-permute-start.6 = (bf16[704,128]{1,0:T(8,128)(2,1)S(1)}, bf16[704,128]{1,0:T(8,128)(2,1)S(1)}, u32[]{:S(2)}, u32[]{:S(2)}) collective-permute-start(bf16[704,128]{1,0:T(8,128)(2,1)S(1)} %get-tuple-element.36), channel_id=1, source_target_pairs={{0,96},{8,104},{16,112},{24,120},{32,64},{40,72},{48,80},{56,88},{... | collective-permute-start | bytes 540680 | tf_op jit(solution)/shard_map/ppermute | solution.py:467
  57.6 2.2 %collective-permute-start.7 = (bf16[304,128]{1,0:T(8,128)(2,1)S(1)}, bf16[304,128]{1,0:T(8,128)(2,1)S(1)}, u32[]{:S(2)}, u32[]{:S(2)}) collective-permute-start(bf16[304,128]{1,0:T(8,128)(2,1)S(1)} %get-tuple-element.39), channel_id=1, source_target_pairs={{0,128},{8,136},{16,144},{24,152},{32,160},{40,168},{48,176},{56,1... | collective-permute-start | bytes 233480 | tf_op jit(solution)/shard_map/ppermute | solution.py:467
  59.8 1.3 collective-permute-start.8
  61.1 3.6 %collective-permute-start.9 = (bf16[112,128]{1,0:T(8,128)(2,1)S(1)}, bf16[112,128]{1,0:T(8,128)(2,1)S(1)}, u32[]{:S(2)}, u32[]{:S(2)}) collective-permute-start(bf16[112,128]{1,0:T(8,128)(2,1)S(1)} %get-tuple-element.42), channel_id=1, source_target_pairs={{0,256},{8,264},{16,272},{24,280},{32,288},{40,296},{48,304},{56,3... | collective-permute-start | bytes 86024 | tf_op jit(solution)/shard_map/ppermute | solution.py:467
  64.7 4.3 %collective-permute-start.10 = (bf16[112,128]{1,0:T(8,128)(2,1)S(1)}, bf16[112,128]{1,0:T(8,128)(2,1)S(1)}, u32[]{:S(2)}, u32[]{:S(2)}) collective-permute-start(bf16[112,128]{1,0:T(8,128)(2,1)S(1)} %get-tuple-element.43), channel_id=1, source_target_pairs={{0,352},{8,360},{16,368},{24,376},{32,320},{40,328},{48,336},{56,3... | collective-permute-start | bytes 86024 | tf_op jit(solution)/shard_map/ppermute | solution.py:467
  69.1 0.0 collective-permute-done.7.refs_1_
  69.1 1.3 collective-permute-start.12
  70.4 0.0 collective-permute-done.6.refs_0_
  70.4 1.3 collective-permute-start.11
  71.7 74.6 %own_end.1 = (f32[1440,256]{1,0:T(8,128)S(1)}, f32[1440,128]{1,0:T(8,128)S(1)}, f32[1440,128]{1,0:T(8,128)S(1)}) custom-call(s32[8]{0:T(128)S(1)} %copy-done.3, bf16[1536,256]{1,0:T(8,128)(2,1)S(1)} %all_gather.12.pair0.refs_0_, bf16[1536,256]{1,0:T(8,128)(2,1)S(1)} %all_gather.13.pair1.refs_1_, ...), custom_call_target="tpu_custom_call", output_to_operand_aliasing={{0}: (7, {})} | custom-call | flops 1 | bytes 1 | tf_op jit(solution)/shard_map/own_end/pallas_call | solution.py:368
  146.3 0.0 collective-permute-done.9.refs_3_
  146.3 0.0 collective-permute-done.10.refs_4_
  146.3 0.0 collective-permute-done.8.refs_2_
  146.3 0.0 collective-permute-done.12.refs_6_
  146.3 0.0 collective-permute-done.11.refs_5_
  146.3 2.1 %merge.1 = bf16[768,128]{1,0:T(8,128)(2,1)S(1)} custom-call(s32[8]{0:T(128)S(1)} %copy-done.3, bf16[704,128]{1,0:T(8,128)(2,1)S(1)} %collective-permute-done.6.refs_0_, bf16[304,128]{1,0:T(8,128)(2,1)S(1)} %collective-permute-done.7.refs_1_, bf16[304,128]{1,0:T(8,128)(2,1)S(1)} %collective-permute-done.8.refs_2_, ...), custom_call_target="tpu_custom_call" | custom-call | flops 1 | bytes 1 | tf_op jit(solution)/shard_map/merge/pallas_call | solution.py:368
  148.5 45.1 %all_to_all.19 = bf16[8,96,128]{2,1,0:T(8,128)(2,1)S(1)} all-to-all(bf16[8,96,128]{2,1,0:T(8,128)(2,1)S(1)} %bitcast.9), channel_id=1, replica_groups=mesh['seq'=64,'head'=8] {'head'}, dimensions={0} | all-to-all | bytes 393216 | tf_op jit(solution)/shard_map/all_to_all | solution.py:490
  193.6 0.7 copy_bitcast_fusion
  (8 shorter events, 0.0 us)
Async XLA Ops:
  0.0 0.7 copy-start
  4.2 20.5 %copy-start.2 = (bf16[672,128]{1,0:T(8,128)(2,1)S(1)}, bf16[672,128]{1,0:T(8,128)(2,1)}, u32[]{:S(2)}) copy-start(bf16[672,128]{1,0:T(8,128)(2,1)} %get-tuple-element.28.near.refs_5_) | copy-start | bytes 516100
  4.2 14.4 %collective-permute-start.2 = (bf16[672,128]{1,0:T(8,128)(2,1)}, bf16[672,128]{1,0:T(8,128)(2,1)S(1)}, u32[]{:S(2)}, u32[]{:S(2)}) collective-permute-start(bf16[672,128]{1,0:T(8,128)(2,1)} %get-tuple-element.28.near.refs_5_), channel_id=1, source_target_pairs={{0,96},{8,104},{16,112},{24,120},{32,64},{40,72},{48,80},{56,88},{... | collective-permute-start | bytes 516104 | tf_op jit(solution)/shard_map/ppermute | solution.py:437
  10.5 22.5 %collective-permute-start.1 = (bf16[768,256]{1,0:T(8,128)(2,1)}, bf16[768,256]{1,0:T(8,128)(2,1)S(1)}, u32[]{:S(2)}, u32[]{:S(2)}) collective-permute-start(bf16[768,256]{1,0:T(8,128)(2,1)} %get-tuple-element.27), channel_id=1, source_target_pairs={{0,32},{8,40},{16,48},{24,56},{32,0},{40,8},{48,16},{56,24},{64,96... | collective-permute-start | bytes 1179656 | tf_op jit(solution)/shard_map/ppermute | solution.py:438
  14.5 23.0 %collective-permute-start = (bf16[768,256]{1,0:T(8,128)(2,1)}, bf16[768,256]{1,0:T(8,128)(2,1)S(1)}, u32[]{:S(2)}, u32[]{:S(2)}) collective-permute-start(bf16[768,256]{1,0:T(8,128)(2,1)} %get-tuple-element.27), channel_id=1, source_target_pairs={{0,16},{8,24},{16,0},{24,8},{32,48},{40,56},{48,32},{56,40},{64,80... | collective-permute-start | bytes 1179656 | tf_op jit(solution)/shard_map/ppermute | solution.py:439
  18.6 6.8 %collective-permute-start.3 = (bf16[576,128]{1,0:T(8,128)(2,1)S(1)}, bf16[576,128]{1,0:T(8,128)(2,1)S(1)}, u32[]{:S(2)}, u32[]{:S(2)}) collective-permute-start(bf16[576,128]{1,0:T(8,128)(2,1)S(1)} %pad_maximum_fusion), channel_id=1, source_target_pairs={{0,128},{8,136},{16,144},{24,152},{32,160},{40,168},{48,176},{56,1... | collective-permute-start | bytes 442376 | tf_op jit(solution)/shard_map/ppermute | solution.py:440
  24.7 15.1 %copy-start.1 = (bf16[768,128]{1,0:T(8,128)(2,1)S(1)}, bf16[768,128]{1,0:T(8,128)(2,1)}, u32[]{:S(2)}) copy-start(bf16[768,128]{1,0:T(8,128)(2,1)} %refs_4_.1) | copy-start | bytes 589828
  24.7 15.1 %copy-start.3 = (s32[8]{0:T(128)S(1)}, s32[8]{0:T(128)}, u32[]{:S(2)}) copy-start(s32[8]{0:T(128)} %pad_add_fusion.sm) | copy-start | bytes 100
  25.4 14.4 %collective-permute-start.5 = (bf16[384,128]{1,0:T(8,128)(2,1)S(1)}, bf16[384,128]{1,0:T(8,128)(2,1)S(1)}, u32[]{:S(2)}, u32[]{:S(2)}) collective-permute-start(bf16[384,128]{1,0:T(8,128)(2,1)S(1)} %pad_maximum_fusion.1), channel_id=1, source_target_pairs={{0,256},{8,264},{16,272},{24,280},{32,288},{40,296},{48,304},{56,3... | collective-permute-start | bytes 294920 | tf_op jit(solution)/shard_map/ppermute | solution.py:441
  33.0 15.4 %collective-permute-start.4 = (bf16[768,256]{1,0:T(8,128)(2,1)S(1)}, bf16[768,256]{1,0:T(8,128)(2,1)S(1)}, u32[]{:S(2)}, u32[]{:S(2)}) collective-permute-start(bf16[768,256]{1,0:T(8,128)(2,1)S(1)} %collective-permute-done.1), channel_id=1, source_target_pairs={{0,16},{8,24},{16,0},{24,8},{32,48},{40,56},{48,32},{56,40},{64,80... | collective-permute-start | bytes 1179656 | tf_op jit(solution)/shard_map/ppermute | solution.py:444
  53.3 17.1 %collective-permute-start.6 = (bf16[704,128]{1,0:T(8,128)(2,1)S(1)}, bf16[704,128]{1,0:T(8,128)(2,1)S(1)}, u32[]{:S(2)}, u32[]{:S(2)}) collective-permute-start(bf16[704,128]{1,0:T(8,128)(2,1)S(1)} %get-tuple-element.36), channel_id=1, source_target_pairs={{0,96},{8,104},{16,112},{24,120},{32,64},{40,72},{48,80},{56,88},{... | collective-permute-start | bytes 540680 | tf_op jit(solution)/shard_map/ppermute | solution.py:467
  57.6 11.5 %collective-permute-start.7 = (bf16[304,128]{1,0:T(8,128)(2,1)S(1)}, bf16[304,128]{1,0:T(8,128)(2,1)S(1)}, u32[]{:S(2)}, u32[]{:S(2)}) collective-permute-start(bf16[304,128]{1,0:T(8,128)(2,1)S(1)} %get-tuple-element.39), channel_id=1, source_target_pairs={{0,128},{8,136},{16,144},{24,152},{32,160},{40,168},{48,176},{56,1... | collective-permute-start | bytes 233480 | tf_op jit(solution)/shard_map/ppermute | solution.py:467
  59.8 86.5 %collective-permute-start.8 = (bf16[304,128]{1,0:T(8,128)(2,1)S(1)}, bf16[304,128]{1,0:T(8,128)(2,1)S(1)}, u32[]{:S(2)}, u32[]{:S(2)}) collective-permute-start(bf16[304,128]{1,0:T(8,128)(2,1)S(1)} %get-tuple-element.41), channel_id=1, source_target_pairs={{0,224},{8,232},{16,240},{24,248},{32,192},{40,200},{48,208},{56,2... | collective-permute-start | bytes 233480 | tf_op jit(solution)/shard_map/ppermute | solution.py:467
  61.1 85.2 %collective-permute-start.9 = (bf16[112,128]{1,0:T(8,128)(2,1)S(1)}, bf16[112,128]{1,0:T(8,128)(2,1)S(1)}, u32[]{:S(2)}, u32[]{:S(2)}) collective-permute-start(bf16[112,128]{1,0:T(8,128)(2,1)S(1)} %get-tuple-element.42), channel_id=1, source_target_pairs={{0,256},{8,264},{16,272},{24,280},{32,288},{40,296},{48,304},{56,3... | collective-permute-start | bytes 86024 | tf_op jit(solution)/shard_map/ppermute | solution.py:467
  64.7 81.5 %collective-permute-start.10 = (bf16[112,128]{1,0:T(8,128)(2,1)S(1)}, bf16[112,128]{1,0:T(8,128)(2,1)S(1)}, u32[]{:S(2)}, u32[]{:S(2)}) collective-permute-start(bf16[112,128]{1,0:T(8,128)(2,1)S(1)} %get-tuple-element.43), channel_id=1, source_target_pairs={{0,352},{8,360},{16,368},{24,376},{32,320},{40,328},{48,336},{56,3... | collective-permute-start | bytes 86024 | tf_op jit(solution)/shard_map/ppermute | solution.py:467
  69.1 77.3 %collective-permute-start.12 = (bf16[112,128]{1,0:T(8,128)(2,1)S(1)}, bf16[112,128]{1,0:T(8,128)(2,1)S(1)}, u32[]{:S(2)}, u32[]{:S(2)}) collective-permute-start(bf16[112,128]{1,0:T(8,128)(2,1)S(1)} %get-tuple-element.45), channel_id=1, source_target_pairs={{0,480},{8,488},{16,496},{24,504},{32,448},{40,456},{48,464},{56,4... | collective-permute-start | bytes 86024 | tf_op jit(solution)/shard_map/ppermute | solution.py:470
  70.4 76.0 %collective-permute-start.11 = (bf16[112,128]{1,0:T(8,128)(2,1)S(1)}, bf16[112,128]{1,0:T(8,128)(2,1)S(1)}, u32[]{:S(2)}, u32[]{:S(2)}) collective-permute-start(bf16[112,128]{1,0:T(8,128)(2,1)S(1)} %get-tuple-element.44), channel_id=1, source_target_pairs={{0,384},{8,392},{16,400},{24,408},{32,416},{40,424},{48,432},{56,4... | collective-permute-start | bytes 86024 | tf_op jit(solution)/shard_map/ppermute | solution.py:470

commit v5 on v4

--- a/solution.py
+++ b/solution.py
@@ -249,16 +249,17 @@
 
 def last_own_kernel(sm, *refs):
     pairs, refs = refs[:4], refs[4:]
-    q, near, own, out, log_sum, refs = refs[0], refs[1], refs[3], refs[4], refs[5], refs[6:]
+    q, near, refs = refs[0], refs[1], refs[3:]
+    early, late, refs = (None,) + refs[:3], (None,) + refs[3:6], refs[6:]
+    own, out, log_sum, refs = refs[0], refs[1], refs[2], refs[3:]
     keys, top = (None,) + refs[:3], refs[3]
     lane = sm[1]
 
-    for part in (2, 3):
+    for part, chosen, at in ((2, early, 2), (3, late, 0)):
 
         @pl.when(before(sm, part))
-        def _(part=part):
-            select_keys(sm, pairs[part], keys, 0)
-            add_own(q, near, pairs[part], keys, 0, own)
+        def _(part=part, chosen=chosen, at=at):
+            add_own(q, near, pairs[part], chosen, at, own)
 
     top[...] = jnp.zeros_like(top)
 
@@ -443,13 +444,14 @@
     block2, r2 = lax.optimization_barrier((block2, r2))
     block3 = lax.ppermute(block2, "seq", exchange(1))
     pairs.append(both_cores(block2))
-    visiting, cross, own = call(
+    early_keys = [((3 * rows, width), dtype) for (rows, width), dtype in keys]
+    visiting, cross, own, *early = call(
         early_kernel,
         "three_chips",
         sm,
         pairs + [queries, near, r1, r2, r4],
-        [((VISITING, HD), BF16)] + state,
-        [((3 * rows, width), dtype) for (rows, width), dtype in keys],
+        [((VISITING, HD), BF16)] + state + early_keys,
+        [],
         work,
     )
     block3, own = lax.optimization_barrier((block3, own))
@@ -459,8 +461,8 @@
         "cross_end",
         sm,
         pairs + [visiting, cross],
-        state[:1] + [((message_rows(d)[2], HD), BF16) for d in range(1, GROUPS)],
-        keys + [((VISITING, HD), F32)] + [((message_rows(d)[1] * 128, 128), F32) for d in range(1, GROUPS)],
+        state[:1] + [((message_rows(d)[2], HD), BF16) for d in range(1, GROUPS)] + keys,
+        [((VISITING, HD), F32)] + [((message_rows(d)[1] * 128, 128), F32) for d in range(1, GROUPS)],
         work // 2,
         {6: 0},
     )
@@ -472,7 +474,7 @@
         last_own_kernel,
         "own_end",
         sm,
-        pairs + [queries, near, own],
+        pairs + [queries, near, own] + early + list(crossed[8:]),
         state[1:] + [((ROWS + TOTAL, HD), F32)] * 2,
         keys + [((ROWS + TOTAL, HD), F32)],
         work // 2,

time: 195 us -> 192 us (0.985)
  the two profiles are of different devices: /device:TPU:193 before, /device:TPU:449 now
where the time goes in v5:
time: 192 us; the launch traced here: 193 us
  Pallas kernels  90.1 us (47%)
  blocking collectives  64.2 us (33%)
  starting transfers between devices  32.6 us (17%)
  waiting for transfers between devices  3.04 us (2%)
  local copies, waits for them, and re-layouts  2.49 us (1%)
    pallas_call x4, Pallas kernels, call(): pl.pallas_call(kernel, name=name, out_shape=shapes, in_specs=[pl.BlockSpe...  87.4 us
    all_to_all x1, blocking collectives, on_device(): lax.all_to_all(merged, 'head', split_axis=0, concat_axis=1, tiled=True)  48.8 us
    all_gather x4, blocking collectives, both_cores(): return lax.all_gather(block, 'seq', axis_index_groups=groups, tiled=True)  15.4 us
    ppermute x5, starting transfers between devices, on_device(): back = [lax.ppermute(crossed[j], 'seq', to_later(j)) for j in range(1, 6)]  13.7 us
    ppermute x1, starting transfers between devices, on_device(): lax.ppermute(jnp.concatenate([near[576:], r1[576:], r2[192:288], r2[480:]...  4.47 us
  transfers between devices with their start and end apart: 13, of which 2 were waited for; matrix products, arithmetic and copies ran while one was open for 0% of the time, Pallas kernels for 43%

profile of v5, /device:TPU:449, one launch (start us, length us, event | category | flops | bytes accessed | tf_op | source)
XLA Modules:
  0.0 193.3 jit_solution(14895323983714234282)
XLA Ops:
  0.0 0.0 copy-start
  0.0 0.7 copy-done
  0.7 0.1 constant_dynamic-slice_fusion
  0.8 0.1 slice_reduce_fusion
  0.9 0.6 pad_add_fusion.sm
  1.5 2.7 %pack.1 = (bf16[672,128]{1,0:T(8,128)(2,1)}, bf16[768,256]{1,0:T(8,128)(2,1)}) custom-call(s32[8]{0:T(128)} %pad_add_fusion.sm, bf16[768,128]{1,0:T(8,128)(2,1)} %refs_4_.1, bf16[768,128]{1,0:T(8,128)(2,1)} %k.1, bf16[768,128]{1,0:T(8,128)(2,1)} %v.1), custom_call_target="tpu_custom_call" | custom-call | flops 1 | bytes 1 | tf_op jit(solution)/shard_map/pack/pallas_call | solution.py:384
  4.2 0.0 copy-start.2
  4.2 2.1 %collective-permute-start.2 = (bf16[672,128]{1,0:T(8,128)(2,1)}, bf16[672,128]{1,0:T(8,128)(2,1)S(1)}, u32[]{:S(2)}, u32[]{:S(2)}) collective-permute-start(bf16[672,128]{1,0:T(8,128)(2,1)} %get-tuple-element.34.near.refs_5_), channel_id=1, source_target_pairs={{0,96},{8,104},{16,112},{24,120},{32,64},{40,72},{48,80},{56,88},{... | collective-permute-start | bytes 516104 | tf_op jit(solution)/shard_map/ppermute | solution.py:438
  6.2 2.2 %collective-permute-start.1 = (bf16[768,256]{1,0:T(8,128)(2,1)}, bf16[768,256]{1,0:T(8,128)(2,1)S(1)}, u32[]{:S(2)}, u32[]{:S(2)}) collective-permute-start(bf16[768,256]{1,0:T(8,128)(2,1)} %get-tuple-element.33), channel_id=1, source_target_pairs={{0,32},{8,40},{16,48},{24,56},{32,0},{40,8},{48,16},{56,24},{64,96... | collective-permute-start | bytes 1179656 | tf_op jit(solution)/shard_map/ppermute | solution.py:439
  8.4 2.2 %collective-permute-start = (bf16[768,256]{1,0:T(8,128)(2,1)}, bf16[768,256]{1,0:T(8,128)(2,1)S(1)}, u32[]{:S(2)}, u32[]{:S(2)}) collective-permute-start(bf16[768,256]{1,0:T(8,128)(2,1)} %get-tuple-element.33), channel_id=1, source_target_pairs={{0,16},{8,24},{16,0},{24,8},{32,48},{40,56},{48,32},{56,40},{64,80... | collective-permute-start | bytes 1179656 | tf_op jit(solution)/shard_map/ppermute | solution.py:440
  10.6 0.9 slice.26
  11.5 2.9 %collective-permute-done.2.r1 = bf16[672,128]{1,0:T(8,128)(2,1)S(1)} collective-permute-done((bf16[672,128]{1,0:T(8,128)(2,1)}, bf16[672,128]{1,0:T(8,128)(2,1)S(1)}, u32[]{:S(2)}, u32[]{:S(2)}) %collective-permute-start.2) | collective-permute-done | bytes 172064 | tf_op jit(solution)/shard_map/ppermute | solution.py:438
  14.4 3.1 %collective-permute-start.3 = (bf16[576,128]{1,0:T(8,128)(2,1)S(1)}, bf16[576,128]{1,0:T(8,128)(2,1)S(1)}, u32[]{:S(2)}, u32[]{:S(2)}) collective-permute-start(bf16[576,128]{1,0:T(8,128)(2,1)S(1)} %pad_maximum_fusion), channel_id=1, source_target_pairs={{0,128},{8,136},{16,144},{24,152},{32,160},{40,168},{48,176},{56,1... | collective-permute-start | bytes 442376 | tf_op jit(solution)/shard_map/ppermute | solution.py:441
  17.5 6.6 %all_gather.12.pair0.refs_0_ = bf16[1536,256]{1,0:T(8,128)(2,1)S(1)} all-gather(bf16[768,256]{1,0:T(8,128)(2,1)} %get-tuple-element.33), channel_id=1, replica_groups={{0,8},{16,24},{32,40},{48,56},{64,72},{80,88},{96,104},{112,120},{128,1..., dimensions={0}, use_global_device_ids=true | all-gather | bytes 1179648 | tf_op jit(solution)/shard_map/all_gather | solution.py:427
  24.1 0.0 copy-done.2
  24.1 0.0 copy-start.1
  24.1 0.0 collective-permute-done.3.r2
  24.2 4.5 %collective-permute-start.5 = (bf16[384,128]{1,0:T(8,128)(2,1)S(1)}, bf16[384,128]{1,0:T(8,128)(2,1)S(1)}, u32[]{:S(2)}, u32[]{:S(2)}) collective-permute-start(bf16[384,128]{1,0:T(8,128)(2,1)S(1)} %pad_maximum_fusion.1), channel_id=1, source_target_pairs={{0,256},{8,264},{16,272},{24,280},{32,288},{40,296},{48,304},{56,3... | collective-permute-start | bytes 294920 | tf_op jit(solution)/shard_map/ppermute | solution.py:442
  28.7 0.1 collective-permute-done.1
  28.8 2.3 %collective-permute-start.4 = (bf16[768,256]{1,0:T(8,128)(2,1)S(1)}, bf16[768,256]{1,0:T(8,128)(2,1)S(1)}, u32[]{:S(2)}, u32[]{:S(2)}) collective-permute-start(bf16[768,256]{1,0:T(8,128)(2,1)S(1)} %collective-permute-done.1), channel_id=1, source_target_pairs={{0,16},{8,24},{16,0},{24,8},{32,48},{40,56},{48,32},{56,40},{64,80... | collective-permute-start | bytes 1179656 | tf_op jit(solution)/shard_map/ppermute | solution.py:445
  31.1 4.1 %all_gather.14.pair2.refs_2_ = bf16[1536,256]{1,0:T(8,128)(2,1)S(1)} all-gather(bf16[768,256]{1,0:T(8,128)(2,1)S(1)} %collective-permute-done.1), channel_id=1, replica_groups={{0,8},{16,24},{32,40},{48,56},{64,72},{80,88},{96,104},{112,120},{128,1..., dimensions={0}, use_global_device_ids=true | all-gather | bytes 1179648 | tf_op jit(solution)/shard_map/all_gather | solution.py:427
  35.2 0.0 collective-permute-done
  35.2 2.4 %all_gather.13.pair1.refs_1_ = bf16[1536,256]{1,0:T(8,128)(2,1)S(1)} all-gather(bf16[768,256]{1,0:T(8,128)(2,1)S(1)} %collective-permute-done), channel_id=1, replica_groups={{0,8},{16,24},{32,40},{48,56},{64,72},{80,88},{96,104},{112,120},{128,1..., dimensions={0}, use_global_device_ids=true | all-gather | bytes 1179648 | tf_op jit(solution)/shard_map/all_gather | solution.py:427
  37.6 0.0 collective-permute-done.5.r4
  37.6 0.0 copy-done.1
  37.6 0.0 copy-done.3
  37.6 8.5 %three_chips.1 = (bf16[1632,128]{1,0:T(8,128)(2,1)S(1)}, f32[1632,256]{1,0:T(8,128)S(1)}, f32[1440,256]{1,0:T(8,128)S(1)}, bf16[2304,256]{1,0:T(8,128)(2,1)S(1)}...) custom-call(s32[8]{0:T(128)S(1)} %copy-done.3, bf16[1536,256]{1,0:T(8,128)(2,1)S(1)} %all_gather.12.pair0.refs_0_, ...), custom_call_target="tpu_custom_call" | custom-call | flops 1 | bytes 1 | tf_op jit(solution)/shard_map/three_chips/pallas_call | solution.py:369
  46.1 0.0 collective-permute-done.4
  46.1 2.4 %all_gather.15.refs_3_ = bf16[1536,256]{1,0:T(8,128)(2,1)S(1)} all-gather(bf16[768,256]{1,0:T(8,128)(2,1)S(1)} %collective-permute-done.4), channel_id=1, replica_groups={{0,8},{16,24},{32,40},{48,56},{64,72},{80,88},{96,104},{112,120},{128,1..., dimensions={0}, use_global_device_ids=true | all-gather | bytes 1179648 | tf_op jit(solution)/shard_map/all_gather | solution.py:427
  48.5 2.5 %cross_end.1 = (f32[1632,256]{1,0:T(8,128)S(1)}, bf16[704,128]{1,0:T(8,128)(2,1)S(1)}, bf16[304,128]{1,0:T(8,128)(2,1)S(1)}, bf16[304,128]{1,0:T(8,128)(2,1)S(1)...) custom-call(s32[8]{0:T(128)S(1)} %copy-done.3, ...), custom_call_target="tpu_custom_call", output_to_operand_aliasing={{0}: (6, {})} | custom-call | flops 1 | bytes 1 | tf_op jit(solution)/shard_map/cross_end/pallas_call | solution.py:369
  51.0 1.3 collective-permute-start.6
  52.3 2.2 %collective-permute-start.7 = (bf16[304,128]{1,0:T(8,128)(2,1)S(1)}, bf16[304,128]{1,0:T(8,128)(2,1)S(1)}, u32[]{:S(2)}, u32[]{:S(2)}) collective-permute-start(bf16[304,128]{1,0:T(8,128)(2,1)S(1)} %get-tuple-element.45), channel_id=1, source_target_pairs={{0,128},{8,136},{16,144},{24,152},{32,160},{40,168},{48,176},{56,1... | collective-permute-start | bytes 233480 | tf_op jit(solution)/shard_map/ppermute | solution.py:469
  54.6 5.2 %collective-permute-start.8 = (bf16[304,128]{1,0:T(8,128)(2,1)S(1)}, bf16[304,128]{1,0:T(8,128)(2,1)S(1)}, u32[]{:S(2)}, u32[]{:S(2)}) collective-permute-start(bf16[304,128]{1,0:T(8,128)(2,1)S(1)} %get-tuple-element.47), channel_id=1, source_target_pairs={{0,224},{8,232},{16,240},{24,248},{32,192},{40,200},{48,208},{56,2... | collective-permute-start | bytes 233480 | tf_op jit(solution)/shard_map/ppermute | solution.py:469
  59.8 3.6 %collective-permute-start.9 = (bf16[112,128]{1,0:T(8,128)(2,1)S(1)}, bf16[112,128]{1,0:T(8,128)(2,1)S(1)}, u32[]{:S(2)}, u32[]{:S(2)}) collective-permute-start(bf16[112,128]{1,0:T(8,128)(2,1)S(1)} %get-tuple-element.48), channel_id=1, source_target_pairs={{0,256},{8,264},{16,272},{24,280},{32,288},{40,296},{48,304},{56,3... | collective-permute-start | bytes 86024 | tf_op jit(solution)/shard_map/ppermute | solution.py:469
  63.4 1.3 collective-permute-start.10
  64.7 0.0 collective-permute-done.7.refs_1_
  64.7 1.3 collective-permute-start.12
  66.0 0.0 collective-permute-done.6.refs_0_
  66.0 1.3 collective-permute-start.11
  67.3 74.3 %own_end.1 = (f32[1440,256]{1,0:T(8,128)S(1)}, f32[1440,128]{1,0:T(8,128)S(1)}, f32[1440,128]{1,0:T(8,128)S(1)}) custom-call(s32[8]{0:T(128)S(1)} %copy-done.3, bf16[1536,256]{1,0:T(8,128)(2,1)S(1)} %all_gather.12.pair0.refs_0_, bf16[1536,256]{1,0:T(8,128)(2,1)S(1)} %all_gather.13.pair1.refs_1_, ...), custom_call_target="tpu_custom_call", output_to_operand_aliasing={{0}: (7, {})} | custom-call | flops 1 | bytes 1 | tf_op jit(solution)/shard_map/own_end/pallas_call | solution.py:369
  141.6 0.0 collective-permute-done.9.refs_3_
  141.6 0.0 collective-permute-done.10.refs_4_
  141.6 0.0 collective-permute-done.8.refs_2_
  141.6 0.0 collective-permute-done.12.refs_6_
  141.6 0.0 collective-permute-done.11.refs_5_
  141.6 2.1 %merge.1 = bf16[768,128]{1,0:T(8,128)(2,1)S(1)} custom-call(s32[8]{0:T(128)S(1)} %copy-done.3, bf16[704,128]{1,0:T(8,128)(2,1)S(1)} %collective-permute-done.6.refs_0_, bf16[304,128]{1,0:T(8,128)(2,1)S(1)} %collective-permute-done.7.refs_1_, bf16[304,128]{1,0:T(8,128)(2,1)S(1)} %collective-permute-done.8.refs_2_, ...), custom_call_target="tpu_custom_call" | custom-call | flops 1 | bytes 1 | tf_op jit(solution)/shard_map/merge/pallas_call | solution.py:369
  143.8 48.8 %all_to_all.19 = bf16[8,96,128]{2,1,0:T(8,128)(2,1)S(1)} all-to-all(bf16[8,96,128]{2,1,0:T(8,128)(2,1)S(1)} %bitcast.9), channel_id=1, replica_groups=mesh['seq'=64,'head'=8] {'head'}, dimensions={0} | all-to-all | bytes 393216 | tf_op jit(solution)/shard_map/all_to_all | solution.py:492
  192.6 0.7 copy_bitcast_fusion
  (8 shorter events, 0.0 us)
Async XLA Ops:
  0.0 0.7 copy-start
  4.2 19.9 %copy-start.2 = (bf16[672,128]{1,0:T(8,128)(2,1)S(1)}, bf16[672,128]{1,0:T(8,128)(2,1)}, u32[]{:S(2)}) copy-start(bf16[672,128]{1,0:T(8,128)(2,1)} %get-tuple-element.34.near.refs_5_) | copy-start | bytes 516100
  4.2 10.2 %collective-permute-start.2 = (bf16[672,128]{1,0:T(8,128)(2,1)}, bf16[672,128]{1,0:T(8,128)(2,1)S(1)}, u32[]{:S(2)}, u32[]{:S(2)}) collective-permute-start(bf16[672,128]{1,0:T(8,128)(2,1)} %get-tuple-element.34.near.refs_5_), channel_id=1, source_target_pairs={{0,96},{8,104},{16,112},{24,120},{32,64},{40,72},{48,80},{56,88},{... | collective-permute-start | bytes 516104 | tf_op jit(solution)/shard_map/ppermute | solution.py:438
  6.2 22.6 %collective-permute-start.1 = (bf16[768,256]{1,0:T(8,128)(2,1)}, bf16[768,256]{1,0:T(8,128)(2,1)S(1)}, u32[]{:S(2)}, u32[]{:S(2)}) collective-permute-start(bf16[768,256]{1,0:T(8,128)(2,1)} %get-tuple-element.33), channel_id=1, source_target_pairs={{0,32},{8,40},{16,48},{24,56},{32,0},{40,8},{48,16},{56,24},{64,96... | collective-permute-start | bytes 1179656 | tf_op jit(solution)/shard_map/ppermute | solution.py:439
  8.4 26.8 %collective-permute-start = (bf16[768,256]{1,0:T(8,128)(2,1)}, bf16[768,256]{1,0:T(8,128)(2,1)S(1)}, u32[]{:S(2)}, u32[]{:S(2)}) collective-permute-start(bf16[768,256]{1,0:T(8,128)(2,1)} %get-tuple-element.33), channel_id=1, source_target_pairs={{0,16},{8,24},{16,0},{24,8},{32,48},{40,56},{48,32},{56,40},{64,80... | collective-permute-start | bytes 1179656 | tf_op jit(solution)/shard_map/ppermute | solution.py:440
  14.4 9.7 %collective-permute-start.3 = (bf16[576,128]{1,0:T(8,128)(2,1)S(1)}, bf16[576,128]{1,0:T(8,128)(2,1)S(1)}, u32[]{:S(2)}, u32[]{:S(2)}) collective-permute-start(bf16[576,128]{1,0:T(8,128)(2,1)S(1)} %pad_maximum_fusion), channel_id=1, source_target_pairs={{0,128},{8,136},{16,144},{24,152},{32,160},{40,168},{48,176},{56,1... | collective-permute-start | bytes 442376 | tf_op jit(solution)/shard_map/ppermute | solution.py:441
  24.1 13.5 %copy-start.1 = (bf16[768,128]{1,0:T(8,128)(2,1)S(1)}, bf16[768,128]{1,0:T(8,128)(2,1)}, u32[]{:S(2)}) copy-start(bf16[768,128]{1,0:T(8,128)(2,1)} %refs_4_.1) | copy-start | bytes 589828
  24.1 13.5 %copy-start.3 = (s32[8]{0:T(128)S(1)}, s32[8]{0:T(128)}, u32[]{:S(2)}) copy-start(s32[8]{0:T(128)} %pad_add_fusion.sm) | copy-start | bytes 100
  24.2 13.4 %collective-permute-start.5 = (bf16[384,128]{1,0:T(8,128)(2,1)S(1)}, bf16[384,128]{1,0:T(8,128)(2,1)S(1)}, u32[]{:S(2)}, u32[]{:S(2)}) collective-permute-start(bf16[384,128]{1,0:T(8,128)(2,1)S(1)} %pad_maximum_fusion.1), channel_id=1, source_target_pairs={{0,256},{8,264},{16,272},{24,280},{32,288},{40,296},{48,304},{56,3... | collective-permute-start | bytes 294920 | tf_op jit(solution)/shard_map/ppermute | solution.py:442
  28.8 17.3 %collective-permute-start.4 = (bf16[768,256]{1,0:T(8,128)(2,1)S(1)}, bf16[768,256]{1,0:T(8,128)(2,1)S(1)}, u32[]{:S(2)}, u32[]{:S(2)}) collective-permute-start(bf16[768,256]{1,0:T(8,128)(2,1)S(1)} %collective-permute-done.1), channel_id=1, source_target_pairs={{0,16},{8,24},{16,0},{24,8},{32,48},{40,56},{48,32},{56,40},{64,80... | collective-permute-start | bytes 1179656 | tf_op jit(solution)/shard_map/ppermute | solution.py:445
  51.0 15.0 %collective-permute-start.6 = (bf16[704,128]{1,0:T(8,128)(2,1)S(1)}, bf16[704,128]{1,0:T(8,128)(2,1)S(1)}, u32[]{:S(2)}, u32[]{:S(2)}) collective-permute-start(bf16[704,128]{1,0:T(8,128)(2,1)S(1)} %get-tuple-element.42), channel_id=1, source_target_pairs={{0,96},{8,104},{16,112},{24,120},{32,64},{40,72},{48,80},{56,88},{... | collective-permute-start | bytes 540680 | tf_op jit(solution)/shard_map/ppermute | solution.py:469
  52.3 12.4 %collective-permute-start.7 = (bf16[304,128]{1,0:T(8,128)(2,1)S(1)}, bf16[304,128]{1,0:T(8,128)(2,1)S(1)}, u32[]{:S(2)}, u32[]{:S(2)}) collective-permute-start(bf16[304,128]{1,0:T(8,128)(2,1)S(1)} %get-tuple-element.45), channel_id=1, source_target_pairs={{0,128},{8,136},{16,144},{24,152},{32,160},{40,168},{48,176},{56,1... | collective-permute-start | bytes 233480 | tf_op jit(solution)/shard_map/ppermute | solution.py:469
  54.6 87.1 %collective-permute-start.8 = (bf16[304,128]{1,0:T(8,128)(2,1)S(1)}, bf16[304,128]{1,0:T(8,128)(2,1)S(1)}, u32[]{:S(2)}, u32[]{:S(2)}) collective-permute-start(bf16[304,128]{1,0:T(8,128)(2,1)S(1)} %get-tuple-element.47), channel_id=1, source_target_pairs={{0,224},{8,232},{16,240},{24,248},{32,192},{40,200},{48,208},{56,2... | collective-permute-start | bytes 233480 | tf_op jit(solution)/shard_map/ppermute | solution.py:469
  59.8 81.8 %collective-permute-start.9 = (bf16[112,128]{1,0:T(8,128)(2,1)S(1)}, bf16[112,128]{1,0:T(8,128)(2,1)S(1)}, u32[]{:S(2)}, u32[]{:S(2)}) collective-permute-start(bf16[112,128]{1,0:T(8,128)(2,1)S(1)} %get-tuple-element.48), channel_id=1, source_target_pairs={{0,256},{8,264},{16,272},{24,280},{32,288},{40,296},{48,304},{56,3... | collective-permute-start | bytes 86024 | tf_op jit(solution)/shard_map/ppermute | solution.py:469
  63.4 78.2 %collective-permute-start.10 = (bf16[112,128]{1,0:T(8,128)(2,1)S(1)}, bf16[112,128]{1,0:T(8,128)(2,1)S(1)}, u32[]{:S(2)}, u32[]{:S(2)}) collective-permute-start(bf16[112,128]{1,0:T(8,128)(2,1)S(1)} %get-tuple-element.49), channel_id=1, source_target_pairs={{0,352},{8,360},{16,368},{24,376},{32,320},{40,328},{48,336},{56,3... | collective-permute-start | bytes 86024 | tf_op jit(solution)/shard_map/ppermute | solution.py:469
  64.7 76.9 %collective-permute-start.12 = (bf16[112,128]{1,0:T(8,128)(2,1)S(1)}, bf16[112,128]{1,0:T(8,128)(2,1)S(1)}, u32[]{:S(2)}, u32[]{:S(2)}) collective-permute-start(bf16[112,128]{1,0:T(8,128)(2,1)S(1)} %get-tuple-element.51), channel_id=1, source_target_pairs={{0,480},{8,488},{16,496},{24,504},{32,448},{40,456},{48,464},{56,4... | collective-permute-start | bytes 86024 | tf_op jit(solution)/shard_map/ppermute | solution.py:472
  66.0 75.6 %collective-permute-start.11 = (bf16[112,128]{1,0:T(8,128)(2,1)S(1)}, bf16[112,128]{1,0:T(8,128)(2,1)S(1)}, u32[]{:S(2)}, u32[]{:S(2)}) collective-permute-start(bf16[112,128]{1,0:T(8,128)(2,1)S(1)} %get-tuple-element.50), channel_id=1, source_target_pairs={{0,384},{8,392},{16,400},{24,408},{32,416},{40,424},{48,432},{56,4... | collective-permute-start | bytes 86024 | tf_op jit(solution)/shard_map/ppermute | solution.py:472
